TPU v7x, 32 devices: a whole 2x2x4 slice. The times are simulated.
32 devices in a mesh: dp: 8 (over z, y), mp: 4 (over x, core).
Axes of the slice: x: 2, y: 2, z: 4, core: 2. Of those that a mesh axis runs over, the one named last changes fastest.
Arguments:
- tokens: bfloat16 [16384, 2048], P(('dp', 'mp')), may hold values from -6 to 6
- patches: bfloat16 [32768, 2048], P('dp'), may hold values from -6 to 6
- text_lengths: int32 [128], P('dp'), may hold values from 8 to 128, as said below
- prefix_lengths: int32 [128], P('dp'), may hold values from 1 to 128, as said below
- group_map: int32 [128], P('dp'), may hold values from 0 to 1, as said below
- ratio: int32 [2], replicated, may hold values from 1 to 4
- cotangent: bfloat16 [16384, 2048], P(('dp', 'mp')), may hold values from -6 to 6
- q_self: bfloat16 [2048, 2048], P(None, 'mp'), may hold values from -0.125 to 0.125
- k_self: bfloat16 [2048, 2048], P(None, 'mp'), may hold values from -0.125 to 0.125
- v_self: bfloat16 [2048, 2048], P(None, 'mp'), may hold values from -0.125 to 0.125
- o_self: bfloat16 [2048, 2048], P('mp'), may hold values from -0.375 to 0.375
- q_cross: bfloat16 [2048, 2048], P(None, 'mp'), may hold values from -0.125 to 0.125
- k_cross: bfloat16 [2048, 2048], P(None, 'mp'), may hold values from -0.125 to 0.125
- v_cross: bfloat16 [2048, 2048], P(None, 'mp'), may hold values from -0.125 to 0.125
- o_cross: bfloat16 [2048, 2048], P('mp'), may hold values from -0.5 to 0.5
- w_gate: bfloat16 [2048, 5120], P(None, 'mp'), may hold values from -0.125 to 0.125
- w_up: bfloat16 [2048, 5120], P(None, 'mp'), may hold values from -0.125 to 0.125
- w_down: bfloat16 [5120, 2048], P('mp'), may hold values from -0.15625 to 0.15625
- gain_attn: float32 [2048], replicated, may hold values from 0.1 to 1.9
- gain_cross: float32 [2048], replicated, may hold values from 0.1 to 1.9
- gain_mlp: float32 [2048], replicated, may hold values from 0.1 to 1.9
Outputs:
- output: bfloat16 [16384, 2048], P(('dp', 'mp'))
- grad_tokens: float32 [16384, 2048], P(('dp', 'mp'))
- grad_q_self: float32 [2048, 2048], P(None, 'mp')
- grad_k_self: float32 [2048, 2048], P(None, 'mp')
- grad_v_self: float32 [2048, 2048], P(None, 'mp')
- grad_o_self: float32 [2048, 2048], P('mp')
- grad_q_cross: float32 [2048, 2048], P(None, 'mp')
- grad_k_cross: float32 [2048, 2048], P(None, 'mp')
- grad_v_cross: float32 [2048, 2048], P(None, 'mp')
- grad_o_cross: float32 [2048, 2048], P('mp')
- grad_w_gate: float32 [2048, 5120], P(None, 'mp')
- grad_w_up: float32 [2048, 5120], P(None, 'mp')
- grad_w_down: float32 [5120, 2048], P('mp')
- grad_gain_attn: float32 [2048], replicated
- grad_gain_cross: float32 [2048], replicated
- grad_gain_mlp: float32 [2048], replicated
Inputs may be any that keep to these rules, and one draw needn't show every extreme that they name: `text_lengths`: each of the two groups holds an example of length 128. `prefix_lengths`: at most the example's text length. `group_map`: both groups occur.
All inputs are finite; a program needn't handle non-finite values.
Results may differ from a plain program's by a relative error of at most 0.028.
Values may be sent and summed in bfloat16 or wider, within the bound.
A program may use at most 384 MiB of HBM per device.

v0:
```python
from functools import partial

import jax
import jax.numpy as jnp
from jax import lax
from jax.sharding import PartitionSpec as P

HEAD = 64
SEQ = 128


epsilon = 1e-06


def fdot(left, right):
    return jnp.dot(left, right, preferred_element_type=jnp.float32)


def tdot(left, right):
    return lax.dot_general(
        left, right, (((0,), (0,)), ((), ())), preferred_element_type=jnp.float32
    )


def rdot(left, right):
    return lax.dot_general(
        left, right, (((1,), (1,)), ((), ())), preferred_element_type=jnp.float32
    )


def normalize(values_in, gain):
    row_scale = lax.rsqrt(jnp.mean(values_in * values_in, axis=-1, keepdims=True) + epsilon)
    return ((values_in * row_scale * gain).astype(jnp.bfloat16), row_scale)


def norm_back(values_in, row_scale, gain, incoming):
    weighted = incoming * gain
    inner = jnp.mean(weighted * values_in, axis=-1, keepdims=True)
    return (
        row_scale * weighted - values_in * row_scale**3 * inner,
        jnp.sum(incoming * values_in * row_scale, axis=0),
    )


def spread(rows_local):
    return lax.all_gather(rows_local, "mp", axis=0, tiled=True)


def spread_grad(rows_local):
    return lax.all_gather(rows_local, "mp", axis=0, tiled=True)


def collect(term, row_count):
    return lax.psum_scatter(
        term(jnp.int32(0), row_count * lax.axis_size("mp")), "mp", scatter_dimension=0, tiled=True
    )


def send_back(term, row_count):
    return lax.psum_scatter(
        term(jnp.int32(0), row_count * lax.axis_size("mp")).astype(jnp.bfloat16),
        "mp",
        scatter_dimension=0,
        tiled=True,
    ).astype(jnp.float32)


def rows_slice(tensor, start, count):
    return lax.dynamic_slice_in_dim(tensor, start, count, 0)


def split_heads(tensor, batches):
    return tensor.reshape(batches, tensor.shape[0] // batches, tensor.shape[1] // HEAD, HEAD)


def score_of(query, keys, key_mask, batches):
    scores = jnp.einsum(
        "eqhd,ekhd->ehqk",
        split_heads(query, batches),
        split_heads(keys, batches),
        preferred_element_type=jnp.float32,
    ) * HEAD ** (-0.5)
    if key_mask is not None:
        scores = jnp.where(key_mask, scores, -1e30)
    return scores


def attend(query, keys, values, key_mask, batches):
    scores = score_of(query, keys, key_mask, batches)
    highest_score = jnp.max(scores, axis=-1, keepdims=True)
    log_total = highest_score + jnp.log(
        jnp.sum(jnp.exp(scores - highest_score), axis=-1, keepdims=True)
    )
    attn_probs = jnp.exp(scores - log_total).astype(jnp.bfloat16)
    mixed = jnp.einsum(
        "ehqk,ekhd->eqhd",
        attn_probs,
        split_heads(values, batches),
        preferred_element_type=jnp.float32,
    )
    return (mixed.reshape(query.shape).astype(jnp.bfloat16), log_total)


def attend_back(grad_rows, query, keys, values, log_total, key_mask, batches):
    attn_probs = jnp.exp(score_of(query, keys, key_mask, batches) - log_total)
    grad_heads = split_heads(grad_rows, batches)
    d_values = jnp.einsum(
        "ehqk,eqhd->ekhd",
        attn_probs.astype(jnp.bfloat16),
        grad_heads,
        preferred_element_type=jnp.float32,
    )
    d_probs = jnp.einsum(
        "eqhd,ekhd->ehqk",
        grad_heads,
        split_heads(values, batches),
        preferred_element_type=jnp.float32,
    )
    d_scores = (
        attn_probs * (d_probs - jnp.sum(attn_probs * d_probs, axis=-1, keepdims=True))
    ).astype(jnp.bfloat16)
    d_query = jnp.einsum(
        "ehqk,ekhd->eqhd", d_scores, split_heads(keys, batches), preferred_element_type=jnp.float32
    ) * HEAD ** (-0.5)
    d_keys = jnp.einsum(
        "ehqk,eqhd->ekhd", d_scores, split_heads(query, batches), preferred_element_type=jnp.float32
    ) * HEAD ** (-0.5)
    return (
        d_query.reshape(query.shape).astype(jnp.bfloat16),
        d_keys.reshape(keys.shape).astype(jnp.bfloat16),
        d_values.reshape(values.shape).astype(jnp.bfloat16),
    )


def on_device(
    tokens,
    patches,
    text_lengths,
    prefix_lengths,
    group_map,
    ratio,
    cotangent,
    q_self,
    k_self,
    v_self,
    o_self,
    q_cross,
    k_cross,
    v_cross,
    o_cross,
    w_gate,
    w_up,
    w_down,
    gain_attn,
    gain_cross,
    gain_mlp,
):
    local_rows = tokens.shape[0]
    examples = text_lengths.shape[0]
    lens_f = text_lengths.astype(jnp.float32)
    robot = (group_map == 0).astype(jnp.float32)
    web = 1.0 - robot
    counts = lax.psum(jnp.stack([jnp.sum(lens_f * robot), jnp.sum(lens_f * web)]), "dp")
    ratio_f = ratio.astype(jnp.float32)
    share = ratio_f / jnp.sum(ratio_f)
    group_scale = share * jnp.sum(counts) / jnp.maximum(counts, 1.0)
    example_scale = robot * group_scale[0] + web * group_scale[1]
    row_ids = lax.axis_index("mp") * local_rows + jnp.arange(local_rows, dtype=jnp.int32)
    owner = row_ids // SEQ
    place = row_ids % SEQ
    picker = (owner[:, None] == jnp.arange(examples, dtype=jnp.int32)[None, :]).astype(jnp.float32)
    row_length = jnp.sum(picker * lens_f[None, :], axis=1)
    live = (place.astype(jnp.float32) < row_length).astype(jnp.float32)
    row_weight = jnp.sum(picker * example_scale[None, :], axis=1) * live
    outer_grad = cotangent.astype(jnp.float32) * row_weight[:, None]
    position = jnp.arange(SEQ, dtype=jnp.int32)
    key_ok = position[None, None, :] < text_lengths[:, None, None]
    causal = (position[None, None, :] <= position[None, :, None]) | (
        position[None, None, :] < prefix_lengths[:, None, None]
    )
    key_mask = (key_ok & causal)[:, None]
    x_zero = tokens.astype(jnp.float32)
    norm_one, scale_one = normalize(x_zero, gain_attn)
    full_one = spread(norm_one)
    query_self = fdot(full_one, q_self).astype(jnp.bfloat16)
    keys_self = fdot(full_one, k_self).astype(jnp.bfloat16)
    values_self = fdot(full_one, v_self).astype(jnp.bfloat16)
    mixed_self, total_self = attend(query_self, keys_self, values_self, key_mask, examples)

    def project_self(start, count):
        return fdot(rows_slice(mixed_self, start, count), o_self)

    x_one = x_zero + collect(project_self, local_rows)
    norm_two, scale_two = normalize(x_one, gain_cross)
    full_two = spread(norm_two)
    query_cross = fdot(full_two, q_cross).astype(jnp.bfloat16)
    keys_cross = fdot(patches, k_cross).astype(jnp.bfloat16)
    values_cross = fdot(patches, v_cross).astype(jnp.bfloat16)
    mixed_cross, total_cross = attend(query_cross, keys_cross, values_cross, None, examples)

    def project_cross(start, count):
        return fdot(rows_slice(mixed_cross, start, count), o_cross)

    x_two = x_one + collect(project_cross, local_rows)
    norm_three, scale_three = normalize(x_two, gain_mlp)
    full_three = spread(norm_three)
    gate_pre = fdot(full_three, w_gate)
    up_pre = fdot(full_three, w_up)
    gelu_value, gelu_pull = jax.vjp(partial(jax.nn.gelu, approximate=True), gate_pre)
    hidden = (gelu_value * up_pre).astype(jnp.bfloat16)

    def project_mlp(start, count):
        return fdot(rows_slice(hidden, start, count), w_down)

    x_three = x_two + collect(project_mlp, local_rows)
    output = x_three.astype(jnp.bfloat16)
    grad_three = spread_grad(outer_grad.astype(jnp.bfloat16))
    d_wdown = tdot(hidden, grad_three)
    d_hidden = rdot(grad_three, w_down)
    d_gate = gelu_pull(d_hidden * up_pre)[0].astype(jnp.bfloat16)
    d_up = (d_hidden * gelu_value).astype(jnp.bfloat16)
    d_wgate = tdot(full_three, d_gate)
    d_wup = tdot(full_three, d_up)

    def mlp_back(start, count):
        return rdot(rows_slice(d_gate, start, count), w_gate) + rdot(
            rows_slice(d_up, start, count), w_up
        )

    back_three, d_gain_mlp = norm_back(
        x_two, scale_three, gain_mlp, send_back(mlp_back, local_rows)
    )
    grad_two_rows = outer_grad + back_three
    grad_two = spread_grad(grad_two_rows.astype(jnp.bfloat16))
    d_ocross = tdot(mixed_cross, grad_two)
    d_mixed_cross = rdot(grad_two, o_cross).astype(jnp.bfloat16)
    dq_cross, dk_cross, dv_cross = attend_back(
        d_mixed_cross, query_cross, keys_cross, values_cross, total_cross, None, examples
    )
    d_qcross = tdot(full_two, dq_cross)
    d_kcross = tdot(patches, dk_cross)
    d_vcross = tdot(patches, dv_cross)

    def cross_back(start, count):
        return rdot(rows_slice(dq_cross, start, count), q_cross)

    back_two, d_gain_cross = norm_back(
        x_one, scale_two, gain_cross, send_back(cross_back, local_rows)
    )
    grad_one_rows = grad_two_rows + back_two
    grad_one = spread_grad(grad_one_rows.astype(jnp.bfloat16))
    d_oself = tdot(mixed_self, grad_one)
    d_mixed_self = rdot(grad_one, o_self).astype(jnp.bfloat16)
    dq_self, dk_self, dv_self = attend_back(
        d_mixed_self, query_self, keys_self, values_self, total_self, key_mask, examples
    )
    d_qself = tdot(full_one, dq_self)
    d_kself = tdot(full_one, dk_self)
    d_vself = tdot(full_one, dv_self)

    def self_back(start, count):
        first = rdot(rows_slice(dq_self, start, count), q_self)
        return (
            first
            + rdot(rows_slice(dk_self, start, count), k_self)
            + rdot(rows_slice(dv_self, start, count), v_self)
        )

    back_one, d_gain_attn = norm_back(
        x_zero, scale_one, gain_attn, send_back(self_back, local_rows)
    )
    grad_input = grad_one_rows + back_one
    (
        d_qself,
        d_kself,
        d_vself,
        d_oself,
        d_qcross,
        d_kcross,
        d_vcross,
        d_ocross,
        d_wgate,
        d_wup,
        d_wdown,
    ) = (
        lax.psum(d_qself.astype(jnp.bfloat16), "dp").astype(jnp.float32),
        lax.psum(d_kself.astype(jnp.bfloat16), "dp").astype(jnp.float32),
        lax.psum(d_vself.astype(jnp.bfloat16), "dp").astype(jnp.float32),
        lax.psum(d_oself.astype(jnp.bfloat16), "dp").astype(jnp.float32),
        lax.psum(d_qcross.astype(jnp.bfloat16), "dp").astype(jnp.float32),
        lax.psum(d_kcross.astype(jnp.bfloat16), "dp").astype(jnp.float32),
        lax.psum(d_vcross.astype(jnp.bfloat16), "dp").astype(jnp.float32),
        lax.psum(d_ocross.astype(jnp.bfloat16), "dp").astype(jnp.float32),
        lax.psum(d_wgate.astype(jnp.bfloat16), "dp").astype(jnp.float32),
        lax.psum(d_wup.astype(jnp.bfloat16), "dp").astype(jnp.float32),
        lax.psum(d_wdown.astype(jnp.bfloat16), "dp").astype(jnp.float32),
    )
    d_gain_attn, d_gain_cross, d_gain_mlp = lax.psum(
        (d_gain_attn, d_gain_cross, d_gain_mlp), ("dp", "mp")
    )
    return (
        output,
        grad_input,
        d_qself,
        d_kself,
        d_vself,
        d_oself,
        d_qcross,
        d_kcross,
        d_vcross,
        d_ocross,
        d_wgate,
        d_wup,
        d_wdown,
        d_gain_attn,
        d_gain_cross,
        d_gain_mlp,
    )


def solution(mesh):
    in_specs = (
        P(("dp", "mp"), None),
        P("dp", None),
        P("dp"),
        P("dp"),
        P("dp"),
        P(),
        P(("dp", "mp"), None),
        P(None, "mp"),
        P(None, "mp"),
        P(None, "mp"),
        P("mp", None),
        P(None, "mp"),
        P(None, "mp"),
        P(None, "mp"),
        P("mp", None),
        P(None, "mp"),
        P(None, "mp"),
        P("mp", None),
        P(),
        P(),
        P(),
    )
    out_specs = (
        P(("dp", "mp"), None),
        P(("dp", "mp"), None),
        P(None, "mp"),
        P(None, "mp"),
        P(None, "mp"),
        P("mp", None),
        P(None, "mp"),
        P(None, "mp"),
        P(None, "mp"),
        P("mp", None),
        P(None, "mp"),
        P(None, "mp"),
        P("mp", None),
        P(),
        P(),
        P(),
    )
    return jax.shard_map(
        on_device, mesh=mesh, in_specs=in_specs, out_specs=out_specs, check_vma=False
    )
```

profile of v0, /device:TPU:0, one launch (start us, length us, event | category | flops | bytes accessed | tf_op | source)
XLA Modules:
  0.0 2392.2 jit_solution(3949105578454352830)
XLA Ops:
  15.0 60.2 %all-gather.7.cloned.1.call-done = bf16[2048,2048]{1,0:T(8,128)(2,1)} async-done(((bf16[512,2048]{1,0:T(8,128)(2,1)}), bf16[2048,2048]{1,0:T(8,128)(2,1)}) %all-gather.7.cloned.1.call-update) | async-done | bytes 8388624 | tf_op jit(solution)/shard_map/all_gather | solution.py:46
  160.0 126.2 %reduce-scatter.7.cloned.1.call-done = f32[512,2048]{1,0:T(8,128)} async-done(((f32[2048,2048]{1,0:T(8,128)}), f32[512,2048]{1,0:T(8,128)}) %reduce-scatter.7.cloned.1.call-update) | async-done | bytes 4194320 | tf_op jit(solution)/shard_map/reduce_scatter | solution.py:54
  293.6 14.5 convolution_convert_fusion.4
  328.3 14.4 convolution_convert_fusion.5
  423.3 126.2 %reduce-scatter.9.cloned.1.call-done = f32[512,2048]{1,0:T(8,128)} async-done(((f32[2048,2048]{1,0:T(8,128)}), f32[512,2048]{1,0:T(8,128)}) %reduce-scatter.9.cloned.1.call-update) | async-done | bytes 4194320 | tf_op jit(solution)/shard_map/reduce_scatter | solution.py:54
  559.4 21.3 psum.105
  589.2 26.6 %all-gather.11.cloned.1.call-done = bf16[2048,2048]{1,0:T(8,128)(2,1)} async-done(((bf16[512,2048]{1,0:T(8,128)(2,1)}), bf16[2048,2048]{1,0:T(8,128)(2,1)}) %all-gather.11.cloned.1.call-update) | async-done | bytes 8388624 | tf_op jit(solution)/shard_map/all_gather | solution.py:46
  615.8 16.7 fusion.87
  632.4 16.0 fusion.86
  648.4 27.6 %all-gather.13.cloned.1.call-done = bf16[2048,2048]{1,0:T(8,128)(2,1)} async-done(((bf16[512,2048]{1,0:T(8,128)(2,1)}), bf16[2048,2048]{1,0:T(8,128)(2,1)}) %all-gather.13.cloned.1.call-update) | async-done | bytes 8388624 | tf_op jit(solution)/shard_map/all_gather | solution.py:50
  676.1 26.5 %multiply_convert_fusion.1 = (bf16[2048,1280]{1,0:T(8,128)(2,1)}, bf16[2048,1280]{1,0:T(8,128)(2,1)}, bf16[2048,1280]{1,0:T(8,128)(2,1)}) fusion(f32[2048,1280]{1,0:T(8,128)} %fusion.86, f32[2048,1280]{1,0:T(8,128)} %fusion.87, bf16[2048,2048]{1,0:T(8,128)(2,1)} %all-gather.13.cloned.1.call-done, bf16[1280,2048]{1,0:T(8,128)(2,1)} %param.38), kind=kOutput, calls=%fused_computation.17 | convolution fusion | flops 10805575680 | bytes 50331648 | tf_op jit(solution)/shard_map/dot_general | solution.py:26
  702.6 18.0 fusion.89
  720.6 19.2 add_convert_fusion.1
  739.9 17.9 fusion.88
  757.9 53.8 %reduce-scatter.13.cloned.1.call-done = bf16[512,2048]{1,0:T(8,128)(2,1)} async-done(((bf16[2048,2048]{1,0:T(8,128)(2,1)}), bf16[512,2048]{1,0:T(8,128)(2,1)}) %reduce-scatter.13.cloned.1.call-update) | async-done | bytes 2097168 | tf_op jit(solution)/shard_map/reduce_scatter | solution.py:60
  816.5 124.1 %reduce-scatter.11.cloned.1.call-done = f32[512,2048]{1,0:T(8,128)} async-done(((f32[2048,2048]{1,0:T(8,128)}), f32[512,2048]{1,0:T(8,128)}) %reduce-scatter.11.cloned.1.call-update) | async-done | bytes 4194320 | tf_op jit(solution)/shard_map/reduce_scatter | solution.py:54
  948.8 58.4 %all-gather.15.cloned.1.call-done = bf16[2048,2048]{1,0:T(8,128)(2,1)} async-done(((bf16[512,2048]{1,0:T(8,128)(2,1)}), bf16[2048,2048]{1,0:T(8,128)(2,1)}) %all-gather.15.cloned.1.call-update) | async-done | bytes 8388624 | tf_op jit(solution)/shard_map/all_gather | solution.py:50
  1070.0 71.8 %reduce-scatter.15.cloned.1.call-done = bf16[512,2048]{1,0:T(8,128)(2,1)} async-done(((bf16[2048,2048]{1,0:T(8,128)(2,1)}), bf16[512,2048]{1,0:T(8,128)(2,1)}) %reduce-scatter.15.cloned.1.call-update) | async-done | bytes 2097168 | tf_op jit(solution)/shard_map/reduce_scatter | solution.py:60
  1151.8 16.7 convolution_convert_fusion.1
  1168.6 16.9 convolution_convert_fusion.2
  1185.5 16.5 convolution_convert_fusion.3
  1270.2 17.7 add_convert_fusion
  1377.8 45.7 %all-reduce = (f32[2048]{0:T(1024)}, f32[2048]{0:T(1024)}, f32[2048]{0:T(1024)}) all-reduce(f32[2048]{0:T(1024)S(1)} %get-tuple-element.68, f32[2048]{0:T(1024)S(1)} %copy-done.53, f32[2048]{0:T(1024)S(1)} %copy-done.52), channel_id=1, replica_groups=mesh['dp'=8,'mp'=4] {'dp','mp'}, use_global_device_ids=true, to_apply=%region_37.38 | all-reduce | flops 6144 | bytes 49152 | tf_op jit(solution)/shard_map/psum | solution.py:298
  1429.6 914.1 %all-reduce.4.cloned.1.call-done = (bf16[2048,512]{0,1:T(8,128)(2,1)}, bf16[2048,512]{0,1:T(8,128)(2,1)}, bf16[2048,512]{1,0:T(8,128)(2,1)}, bf16[2048,512]{1,0:...) async-done(((bf16[2048,512]{0,1:T(8,128)(2,1)}, ...) | async-done | bytes 32505872 | tf_op jit(solution)/shard_map/psum | solution.py:291
  (327 shorter events, 509.7 us)
Async XLA Ops:
  7.2 407.7 %copy-start = (bf16[512,2048]{1,0:T(8,128)(2,1)S(1)}, bf16[512,2048]{1,0:T(8,128)(2,1)}, u32[]{:S(2)}) copy-start(bf16[512,2048]{1,0:T(8,128)(2,1)} %param.35) | copy-start | bytes 6291460
  7.2 68.1 %all-gather.7.cloned.1.call-start = ((), (), s32[]{:S(2)}) async-start(), calls=%async_computation.6 | async-start | bytes 10485760 | tf_op jit(solution)/shard_map/all_gather | solution.py:46
  14.1 272.1 %reduce-scatter.7.cloned.1.call-start = ((), (), s32[]{:S(2)}) async-start(), calls=%async_computation.7 | async-start | bytes 20971520 | tf_op jit(solution)/shard_map/reduce_scatter | solution.py:54
  15.0 130.6 %copy-start.20 = (pred[16,128,128]{1,2,0:T(8,128)(4,1)}, pred[16,128,128]{1,2,0:T(8,128)(4,1)S(1)}, u32[]{:S(2)}) copy-start(pred[16,128,128]{1,2,0:T(8,128)(4,1)S(1)} %or_and_fusion) | copy-start | bytes 786436
  160.0 131.8 %copy-start.45 = (f32[2048]{0:T(1024)S(1)}, f32[2048]{0:T(1024)}, u32[]{:S(2)}) copy-start(f32[2048]{0:T(1024)} %param.40) | copy-start | bytes 24580
  160.0 203.2 %all-gather.9.cloned.1.call-start = ((), (), s32[]{:S(2)}) async-start(), calls=%async_computation.8 | async-start | bytes 10485760 | tf_op jit(solution)/shard_map/all_gather | solution.py:46
  293.5 256.0 %reduce-scatter.9.cloned.1.call-start = ((), (), s32[]{:S(2)}) async-start(), calls=%async_computation.9 | async-start | bytes 20971520 | tf_op jit(solution)/shard_map/reduce_scatter | solution.py:54
  423.2 132.3 %copy-start.43 = (f32[2048]{0:T(1024)S(1)}, f32[2048]{0:T(1024)}, u32[]{:S(2)}) copy-start(f32[2048]{0:T(1024)} %param.41) | copy-start | bytes 24580
  423.2 192.5 %all-gather.11.cloned.1.call-start = ((), (), s32[]{:S(2)}) async-start(), calls=%async_computation.10 | async-start | bytes 10485760 | tf_op jit(solution)/shard_map/all_gather | solution.py:46
  557.3 118.8 %all-gather.13.cloned.1.call-start = ((), (), s32[]{:S(2)}) async-start(), calls=%async_computation.12 | async-start | bytes 10485760 | tf_op jit(solution)/shard_map/all_gather | solution.py:50
  589.1 222.5 %reduce-scatter.13.cloned.1.call-start = ((), (), s32[]{:S(2)}) async-start(), calls=%async_computation.13 | async-start | bytes 10485760 | tf_op jit(solution)/shard_map/reduce_scatter | solution.py:60
  739.8 200.8 %reduce-scatter.11.cloned.1.call-start = ((), (), s32[]{:S(2)}) async-start(), calls=%async_computation.11 | async-start | bytes 20971520 | tf_op jit(solution)/shard_map/reduce_scatter | solution.py:54
  757.8 53.9 %copy-start.44 = (f32[2048]{0:T(1024)S(1)}, f32[2048]{0:T(1024)}, u32[]{:S(2)}) copy-start(f32[2048]{0:T(1024)} %param.41) | copy-start | bytes 24580
  757.8 53.9 %copy-start.51 = (f32[512]{0:T(512)S(1)}, f32[512]{0:T(512)}, u32[]{:S(2)}) copy-start(f32[512]{0:T(512)} %copy-done.50) | copy-start | bytes 6148
  757.8 182.8 %copy-start.57 = (f32[512]{0:T(512)S(1)}, f32[512]{0:T(512)}, u32[]{:S(2)}) copy-start(f32[512]{0:T(512)} %copy-done.56) | copy-start | bytes 6148
  757.8 182.8 %copy-start.59 = (f32[512]{0:T(512)S(1)}, f32[512]{0:T(512)}, u32[]{:S(2)}) copy-start(f32[512]{0:T(512)} %get-tuple-element.104) | copy-start | bytes 6148
  757.8 249.4 %all-gather.15.cloned.1.call-start = ((), (), s32[]{:S(2)}) async-start(), calls=%async_computation.14 | async-start | bytes 10485760 | tf_op jit(solution)/shard_map/all_gather | solution.py:50
  948.8 193.0 %reduce-scatter.15.cloned.1.call-start = ((), (), s32[]{:S(2)}) async-start(), calls=%async_computation.15 | async-start | bytes 10485760 | tf_op jit(solution)/shard_map/reduce_scatter | solution.py:60
  1069.9 71.9 %copy-start.46 = (f32[2048]{0:T(1024)S(1)}, f32[2048]{0:T(1024)}, u32[]{:S(2)}) copy-start(f32[2048]{0:T(1024)} %param.40) | copy-start | bytes 24580
  1069.9 71.9 %copy-start.49 = (f32[512]{0:T(512)S(1)}, f32[512]{0:T(512)}, u32[]{:S(2)}) copy-start(f32[512]{0:T(512)} %copy-done.48) | copy-start | bytes 6148
  1069.9 76.8 %copy-start.58 = (f32[512]{0:T(512)S(1)}, f32[512]{0:T(512)}, u32[]{:S(2)}) copy-start(f32[512]{0:T(512)} %get-tuple-element.102) | copy-start | bytes 6148
  1070.0 140.2 %all-gather.17.cloned.1.call-start = ((), (), s32[]{:S(2)}) async-start(), calls=%async_computation.16 | async-start | bytes 10485760 | tf_op jit(solution)/shard_map/all_gather | solution.py:50
  1151.7 221.3 %reduce-scatter.17.cloned.1.call-start = ((), (), s32[]{:S(2)}) async-start(), calls=%async_computation.17 | async-start | bytes 10485760 | tf_op jit(solution)/shard_map/reduce_scatter | solution.py:60
  1287.8 1055.9 %all-reduce.4.cloned.1.call-start = ((), (), s32[]{:S(2)}) async-start(), calls=%async_computation.18 | async-start | bytes 65011712 | tf_op jit(solution)/shard_map/psum | solution.py:291
  (80 other events, 692.0 us)
Sparse Core Ops, SparseCore 0:
  14.3 60.9 all-gather.6
  160.1 126.1 reduce-scatter.6
  293.6 58.2 all-gather.8
  423.3 126.1 reduce-scatter.8
  557.4 58.2 all-gather.10
  617.8 58.2 all-gather.12
  739.9 71.7 reduce-scatter.12
  814.4 126.0 reduce-scatter.10
  948.9 58.2 all-gather.14
  1070.1 71.7 reduce-scatter.14
  1151.9 58.2 all-gather.16
  1288.0 71.6 reduce-scatter.16
  1373.2 970.5 all-reduce.3
where the time goes:
time: 2400 us; the launch traced here: 2390 us
  waiting for transfers between devices  1590 us (66%)
  matrix products  449 us (19%)
  local copies, waits for them, and re-layouts  146 us (6%)
  other arithmetic  122 us (5%)
  blocking collectives  67 us (3%)
    psum x1, waiting for transfers between devices, on_device(): lax.psum(d_kcross.astype(jnp.bfloat16), 'dp').astype(jnp.float32)  914 us
    reduce_scatter x3, waiting for transfers between devices, collect(): lax.psum_scatter(term(jnp.int32(0), row_count * lax.axis_size('mp')), 'mp...  377 us
    dot_general x11, matrix products, fdot(): return jnp.dot(left, right, preferred_element_type=jnp.float32)  136 us
    reduce_scatter x3, waiting for transfers between devices, send_back(): lax.psum_scatter(term(jnp.int32(0), row_count * lax.axis_size('mp')).asty...  126 us
    dot_general x9, matrix products, rdot(): lax.dot_general(left, right, (((1,), (1,)), ((), ())), preferred_element_...  123 us
    dot_general x11, matrix products, tdot(): lax.dot_general(left, right, (((0,), (0,)), ((), ())), preferred_element_...  119 us
    reshape x16, local copies, waits for them, and re-layouts, split_heads(): tensor.reshape(batches, tensor.shape[0] // batches, tensor.shape[1] // HE...  105 us
    all_gather x3, waiting for transfers between devices, spread_grad(): return lax.all_gather(rows_local, 'mp', axis=0, tiled=True)  89.2 us
  transfers between devices with their start and end apart: 13, of which 11 were waited for; matrix products, arithmetic and copies ran while one was open for 12% of the time, Pallas kernels for 0%

commit v1 on v0

v1 whole, which is shorter than its diff:
```python
from functools import partial

import jax
import jax.numpy as jnp
from jax import lax
from jax.experimental import pallas as pl
from jax.experimental.pallas import tpu as pltpu
from jax.sharding import PartitionSpec as P

HEAD = 64
SEQ = 128
PAIR = 2 * HEAD
epsilon = 1e-06
f32 = jnp.float32
bf16 = jnp.bfloat16
VMEM_LIMIT = 56 * 1024 * 1024


def dot_nn(left, right):
    return jnp.dot(left, right, preferred_element_type=f32)


def dot_tn(left, right):
    return lax.dot_general(left, right, (((0,), (0,)), ((), ())), preferred_element_type=f32)


def dot_nt(left, right):
    return lax.dot_general(left, right, (((1,), (1,)), ((), ())), preferred_element_type=f32)


def normalize(values_in, gain):
    row_scale = lax.rsqrt(jnp.mean(values_in * values_in, axis=-1, keepdims=True) + epsilon)
    return ((values_in * row_scale * gain).astype(bf16), row_scale)


def norm_back(values_in, row_scale, gain, incoming):
    weighted = incoming * gain
    inner = jnp.mean(weighted * values_in, axis=-1, keepdims=True)
    return (
        row_scale * weighted - values_in * row_scale**3 * inner,
        jnp.sum(incoming * values_in * row_scale, axis=0),
    )


def first_head():
    return lax.broadcasted_iota(jnp.int32, (SEQ, PAIR), 1) < HEAD


def stack_pair(rows, first):
    zero = jnp.zeros_like(rows)
    return jnp.concatenate([jnp.where(first, rows, zero), jnp.where(first, zero, rows)], axis=0)


def unstack_pair(stacked, first):
    return jnp.where(first, stacked[:SEQ], stacked[SEQ:])


def self_mask(length, prefix):
    query_at = lax.broadcasted_iota(jnp.int32, (2 * SEQ, SEQ), 0) % SEQ
    key_at = lax.broadcasted_iota(jnp.int32, (2 * SEQ, SEQ), 1)
    return (key_at < length) & ((key_at <= query_at) | (key_at < prefix))


def pair_probs(stacked_query, keys, mask):
    scores = dot_nt(stacked_query, keys)
    if mask is not None:
        scores = jnp.where(mask, scores, -1e30)
    expd = jnp.exp(scores - jnp.max(scores, axis=-1, keepdims=True))
    return expd * (1.0 / jnp.sum(expd, axis=-1, keepdims=True))


def pair_forward(query, keys, values, mask, first):
    scaled = stack_pair(query * jnp.asarray(HEAD**-0.5, bf16), first)
    probs = pair_probs(scaled, keys, mask)
    return unstack_pair(dot_nn(probs.astype(bf16), values), first).astype(bf16)


def pair_backward(grad, query, keys, values, mask, first):
    scaled = stack_pair(query * jnp.asarray(HEAD**-0.5, bf16), first)
    probs = pair_probs(scaled, keys, mask)
    grads = stack_pair(grad, first)
    d_probs = dot_nt(grads, values)
    d_scores = (
        probs * (d_probs - jnp.sum(probs * d_probs, axis=-1, keepdims=True))
    ).astype(bf16)
    d_query = unstack_pair(dot_nn(d_scores, keys), first) * HEAD**-0.5
    d_keys = dot_tn(d_scores, scaled)
    d_values = dot_tn(probs.astype(bf16), grads)
    return d_query.astype(bf16), d_keys.astype(bf16), d_values.astype(bf16)


def lanes(part, width, pair):
    return slice(part * width + pair * PAIR, part * width + (pair + 1) * PAIR)


def self_forward_kernel(length_ref, prefix_ref, qkv_ref, out_ref):
    at = pl.program_id(0)
    width = out_ref.shape[1]
    first = first_head()
    mask = self_mask(length_ref[at], prefix_ref[at])
    for pair in range(width // PAIR):
        out_ref[:, lanes(0, width, pair)] = pair_forward(
            qkv_ref[:, lanes(0, width, pair)],
            qkv_ref[:, lanes(1, width, pair)],
            qkv_ref[:, lanes(2, width, pair)],
            mask,
            first,
        )


def self_backward_kernel(length_ref, prefix_ref, qkv_ref, grad_ref, out_ref):
    at = pl.program_id(0)
    width = grad_ref.shape[1]
    first = first_head()
    mask = self_mask(length_ref[at], prefix_ref[at])
    for pair in range(width // PAIR):
        for part, value in enumerate(
            pair_backward(
                grad_ref[:, lanes(0, width, pair)],
                qkv_ref[:, lanes(0, width, pair)],
                qkv_ref[:, lanes(1, width, pair)],
                qkv_ref[:, lanes(2, width, pair)],
                mask,
                first,
            )
        ):
            out_ref[:, lanes(part, width, pair)] = value


def cross_forward_kernel(which_ref, query_ref, kv_ref, out_ref):
    width = out_ref.shape[1]
    first = first_head()
    for pair in range(width // PAIR):
        out_ref[:, lanes(0, width, pair)] = pair_forward(
            query_ref[:, lanes(0, width, pair)],
            kv_ref[:, lanes(0, width, pair)],
            kv_ref[:, lanes(1, width, pair)],
            None,
            first,
        )


def cross_backward_kernel(which_ref, query_ref, kv_ref, grad_ref, *rest):
    d_query_ref, d_kv_ref = rest[-2:]
    width = query_ref.shape[1]
    first = first_head()
    for pair in range(width // PAIR):
        d_query, d_keys, d_values = pair_backward(
            grad_ref[:, lanes(0, width, pair)],
            query_ref[:, lanes(0, width, pair)],
            kv_ref[:, lanes(0, width, pair)],
            kv_ref[:, lanes(1, width, pair)],
            None,
            first,
        )
        d_query_ref[:, lanes(0, width, pair)] = d_query
        d_kv_ref[:, lanes(0, width, pair)] = d_keys
        d_kv_ref[:, lanes(1, width, pair)] = d_values


def params():
    return pltpu.CompilerParams(vmem_limit_bytes=VMEM_LIMIT)


def by_row(width):
    return pl.BlockSpec((SEQ, width), lambda i, *_: (i, 0))


def attention_cost(examples, width, keys, dots, moved):
    return pl.CostEstimate(
        flops=dots * 2 * examples * SEQ * keys * width * 2,
        bytes_accessed=moved,
        transcendentals=examples * SEQ * keys * width // HEAD,
    )


def self_forward(qkv, length, prefix):
    rows, triple = qkv.shape
    width = triple // 3
    return pl.pallas_call(
        self_forward_kernel,
        grid_spec=pltpu.PrefetchScalarGridSpec(
            num_scalar_prefetch=2,
            grid=(rows // SEQ,),
            in_specs=[by_row(triple)],
            out_specs=by_row(width),
        ),
        out_shape=jax.ShapeDtypeStruct((rows, width), bf16),
        compiler_params=params(),
        cost_estimate=attention_cost(rows // SEQ, width, SEQ, 2, rows * width * 8),
    )(length, prefix, qkv)


def self_backward(qkv, grad, length, prefix):
    rows, triple = qkv.shape
    width = triple // 3
    return pl.pallas_call(
        self_backward_kernel,
        grid_spec=pltpu.PrefetchScalarGridSpec(
            num_scalar_prefetch=2,
            grid=(rows // SEQ,),
            in_specs=[by_row(triple), by_row(width)],
            out_specs=by_row(triple),
        ),
        out_shape=jax.ShapeDtypeStruct((rows, triple), bf16),
        compiler_params=params(),
        cost_estimate=attention_cost(rows // SEQ, width, SEQ, 5, rows * width * 14),
    )(length, prefix, qkv, grad)


def cross_forward(query, kv, which, patch):
    rows, width = query.shape
    return pl.pallas_call(
        cross_forward_kernel,
        grid_spec=pltpu.PrefetchScalarGridSpec(
            num_scalar_prefetch=1,
            grid=(rows // SEQ,),
            in_specs=[
                by_row(width),
                pl.BlockSpec((patch, 2 * width), lambda i, which: (which[i], 0)),
            ],
            out_specs=by_row(width),
        ),
        out_shape=jax.ShapeDtypeStruct((rows, width), bf16),
        compiler_params=params(),
        cost_estimate=attention_cost(rows // SEQ, width, patch, 2, rows * width * 12),
    )(which, query, kv)


def cross_backward(query, kv, grad, which, patch, earlier):
    rows, width = query.shape
    kv_spec = pl.BlockSpec((patch, 2 * width), lambda i, which: (which[i], 0))
    in_specs = [by_row(width), kv_spec, by_row(width)]
    operands = [which, query, kv, grad]
    aliases = {}
    if earlier is not None:
        in_specs.append(pl.BlockSpec(memory_space=pl.ANY))
        aliases = {len(operands): 1}
        operands.append(earlier)
    return pl.pallas_call(
        cross_backward_kernel,
        grid_spec=pltpu.PrefetchScalarGridSpec(
            num_scalar_prefetch=1,
            grid=(rows // SEQ,),
            in_specs=in_specs,
            out_specs=[by_row(width), kv_spec],
        ),
        out_shape=[
            jax.ShapeDtypeStruct((rows, width), bf16),
            jax.ShapeDtypeStruct(kv.shape, bf16),
        ],
        input_output_aliases=aliases,
        compiler_params=params(),
        cost_estimate=attention_cost(rows // SEQ, width, patch, 5, rows * width * 24),
    )(*operands)


def mlp_kernel(norm_ref, grad_ref, gate_ref, up_ref, down_ref, hidden_ref, d_gate_ref, d_up_ref):
    rows = norm_ref.shape[0]
    step = min(rows, 256)
    curve = 0.7978845608028654
    for start in range(0, rows, step):
        at = slice(start, start + step)
        gate = dot_nn(norm_ref[at, :], gate_ref[...])
        up = dot_nn(norm_ref[at, :], up_ref[...])
        d_hidden = dot_nt(grad_ref[at, :], down_ref[...])
        square = gate * gate
        bend = jnp.tanh(curve * gate * (1.0 + 0.044715 * square))
        half = 0.5 * (1.0 + bend)
        value = gate * half
        slope = half + 0.5 * curve * gate * (1.0 - bend * bend) * (1.0 + 0.134145 * square)
        hidden_ref[at, :] = (value * up).astype(bf16)
        d_gate_ref[at, :] = (d_hidden * up * slope).astype(bf16)
        d_up_ref[at, :] = (d_hidden * value).astype(bf16)


def mlp(norm, grad, w_gate, w_up, w_down):
    rows, model = norm.shape
    units = w_gate.shape[1]
    tile = 256 if units % 256 == 0 else units
    whole = pl.BlockSpec((rows, model), lambda i: (0, 0))
    columns = pl.BlockSpec((model, tile), lambda i: (0, i))
    out = pl.BlockSpec((rows, tile), lambda i: (0, i))
    shape = jax.ShapeDtypeStruct((rows, units), bf16)
    return pl.pallas_call(
        mlp_kernel,
        grid=(units // tile,),
        in_specs=[whole, whole, columns, columns, pl.BlockSpec((tile, model), lambda i: (i, 0))],
        out_specs=[out, out, out],
        out_shape=[shape, shape, shape],
        compiler_params=params(),
        cost_estimate=pl.CostEstimate(
            flops=6 * rows * model * units,
            bytes_accessed=4 * rows * model + 6 * model * units + 6 * rows * units,
            transcendentals=rows * units,
        ),
    )(norm, grad, w_gate, w_up, w_down)


def flip(tensor, axis, bit):
    count = lax.axis_size(axis)
    return lax.ppermute(tensor, axis, [(i, i ^ bit) for i in range(count)])


def butterfly(tensor, axis):
    count = lax.axis_size(axis)
    if count & (count - 1):
        return lax.psum(tensor, axis)
    bit = 1
    while bit < count:
        tensor = tensor + flip(tensor, axis, bit)
        bit *= 2
    return tensor


def block_owners():
    count = lax.axis_size("mp")
    if count == 4:
        me = lax.axis_index("mp")
        return jnp.stack([me, me ^ 2, me ^ 1, me ^ 3])
    return jnp.arange(count, dtype=jnp.int32)


def gather(rows_local):
    if lax.axis_size("mp") != 4:
        return lax.all_gather(rows_local, "mp", axis=0, tiled=True)
    across = flip(rows_local, "mp", 2)
    beside = flip(rows_local, "mp", 1)
    corner = flip(across, "mp", 1)
    return jnp.concatenate([rows_local, across, beside, corner], axis=0)


def scatter(product, rows, wide):
    count = lax.axis_size("mp")
    if count != 4:
        term = product(0, rows * count)
        term = term if wide else term.astype(bf16)
        return lax.psum_scatter(term, "mp", scatter_dimension=0, tiled=True).astype(f32)
    given = flip(product(2 * rows, 4 * rows).astype(bf16), "mp", 1)
    kept = product(0, 2 * rows) + given.astype(f32)
    return kept[:rows] + flip(kept[rows:].astype(bf16), "mp", 2).astype(f32)


def pairs(line, across=False):
    return [(a * 2 + y, b * 2 + (1 - y if across else y)) for a, b in line for y in (0, 1)]


Y_ALL = pairs([(z, z) for z in range(4)], True)
Y_INNER = pairs([(1, 1), (2, 2)], True)
INWARD = pairs([(0, 1), (3, 2)])
MIDDLE = pairs([(1, 2), (2, 1)])
OUTWARD = pairs([(1, 0), (2, 3)])


def send(tensor, which):
    return lax.ppermute(tensor, "dp", which)


def plus(left, right):
    return (left.astype(f32) + right.astype(f32)).astype(bf16)


def cut(tensor, index):
    both = tensor.reshape(2, tensor.shape[0] // 2, tensor.shape[1])
    return (
        lax.dynamic_index_in_dim(both, index, 0, False),
        lax.dynamic_index_in_dim(both, 1 - index, 0, False),
    )


def join(mine, other, index):
    return jnp.concatenate(
        [jnp.where(index == 0, mine, other), jnp.where(index == 0, other, mine)], axis=0
    )


def sum_y_first(tensor):
    at = lax.axis_index("dp")
    y, z = at % 2, at // 2
    mine, other = cut(tensor, y)
    total = plus(mine, send(other, Y_ALL))
    total = plus(total, send(total, INWARD))
    total = plus(total, send(total, MIDDLE))
    total = jnp.where((z == 1) | (z == 2), total, send(total, OUTWARD))
    return join(total, send(total, Y_ALL), y)


def sum_z_first(tensor):
    at = lax.axis_index("dp")
    z = at // 2
    side = (z == 2).astype(jnp.int32)
    total = plus(tensor, send(tensor, INWARD))
    mine, other = cut(total, side)
    mine = plus(mine, send(other, MIDDLE))
    mine = plus(mine, send(mine, Y_INNER))
    total = join(mine, send(mine, MIDDLE), side)
    return jnp.where((z == 1) | (z == 2), total, send(total, OUTWARD))


def sum_dp(tensor, y_first):
    tensor = tensor.astype(bf16)
    if lax.axis_size("dp") != 8:
        return lax.psum(tensor, "dp").astype(f32)
    return (sum_y_first if y_first else sum_z_first)(tensor).astype(f32)


def on_device(
    tokens,
    patches,
    text_lengths,
    prefix_lengths,
    group_map,
    ratio,
    cotangent,
    q_self,
    k_self,
    v_self,
    o_self,
    q_cross,
    k_cross,
    v_cross,
    o_cross,
    w_gate,
    w_up,
    w_down,
    gain_attn,
    gain_cross,
    gain_mlp,
):
    local_rows = tokens.shape[0]
    examples = text_lengths.shape[0]
    patch = patches.shape[0] // examples
    local_examples = local_rows // SEQ
    batches = 2 if local_examples % 2 == 0 else 1
    each = local_examples // batches
    rows = each * SEQ
    width = q_self.shape[1]

    lens_f = text_lengths.astype(f32)
    robot = (group_map == 0).astype(f32)
    web = 1.0 - robot
    local_counts = jnp.stack([jnp.sum(lens_f * robot), jnp.sum(lens_f * web)])
    counts = butterfly(jnp.broadcast_to(local_counts[:, None], (2, 128)), "dp")[:, 0]
    ratio_f = ratio.astype(f32)
    share = ratio_f / jnp.sum(ratio_f)
    group_scale = share * jnp.sum(counts) / jnp.maximum(counts, 1.0)
    example_scale = robot * group_scale[0] + web * group_scale[1]
    mine = lax.axis_index("mp") * local_examples
    own_scale = lax.dynamic_slice_in_dim(example_scale, mine, local_examples, 0)
    own_length = lax.dynamic_slice_in_dim(text_lengths, mine, local_examples, 0)
    place = jnp.arange(SEQ, dtype=jnp.int32)
    live = (place[None, :] < own_length[:, None]).astype(f32)
    row_weight = (own_scale[:, None] * live).reshape(local_rows)

    owners = block_owners()
    which, lengths, prefixes = [], [], []
    for b in range(batches):
        ids = (
            owners[:, None] * local_examples + b * each + jnp.arange(each, dtype=jnp.int32)[None, :]
        ).reshape(-1).astype(jnp.int32)
        which.append(ids)
        lengths.append(jnp.take(text_lengths, ids))
        prefixes.append(jnp.take(prefix_lengths, ids))

    w_qkv = jnp.concatenate([q_self, k_self, v_self], axis=1)
    w_kv = jnp.concatenate([k_cross, v_cross], axis=1)

    each_batch = range(batches)

    def part(tensor, b):
        return tensor[b * rows : (b + 1) * rows]

    def product(left, right, dot):
        return lambda low, high: dot(left[low:high], right)

    outer = [part(cotangent, b).astype(f32) * part(row_weight, b)[:, None] for b in each_batch]
    x_zero = [part(tokens, b).astype(f32) for b in each_batch]

    norm_one = [normalize(x_zero[b], gain_attn) for b in each_batch]
    full_one = [gather(norm_one[b][0]) for b in each_batch]
    qkv = [dot_nn(full_one[b], w_qkv).astype(bf16) for b in each_batch]
    mixed_self = [self_forward(qkv[b], lengths[b], prefixes[b]) for b in each_batch]
    x_one = [
        x_zero[b] + scatter(product(mixed_self[b], o_self, dot_nn), rows, True) for b in each_batch
    ]
    norm_two = [normalize(x_one[b], gain_cross) for b in each_batch]
    full_two = [gather(norm_two[b][0]) for b in each_batch]
    query = [dot_nn(full_two[b], q_cross).astype(bf16) for b in each_batch]
    kv = dot_nn(patches, w_kv).astype(bf16)
    mixed_cross = [cross_forward(query[b], kv, which[b], patch) for b in each_batch]
    x_two = [
        x_one[b] + scatter(product(mixed_cross[b], o_cross, dot_nn), rows, True)
        for b in each_batch
    ]
    norm_three = [normalize(x_two[b], gain_mlp) for b in each_batch]
    full_three = [gather(norm_three[b][0]) for b in each_batch]
    grad_three = [gather(outer[b].astype(bf16)) for b in each_batch]
    hidden, d_gate, d_up = zip(
        *[mlp(full_three[b], grad_three[b], w_gate, w_up, w_down) for b in each_batch]
    )

    def weight_grad(left, right):
        return sum(dot_tn(left[b], right[b]) for b in each_batch)

    d_wdown = sum_dp(weight_grad(hidden, grad_three), False)
    d_wgate = sum_dp(weight_grad(full_three, d_gate), True)
    d_wup = sum_dp(weight_grad(full_three, d_up), False)

    def mlp_back(b):
        return lambda low, high: (
            dot_nt(d_gate[b][low:high], w_gate) + dot_nt(d_up[b][low:high], w_up)
        )

    back = [
        norm_back(x_two[b], norm_three[b][1], gain_mlp, scatter(mlp_back(b), rows, False))
        for b in each_batch
    ]
    d_gain_mlp = sum(item[1] for item in back)
    grad_two_rows = [outer[b] + back[b][0] for b in each_batch]
    grad_two = [gather(grad_two_rows[b].astype(bf16)) for b in each_batch]
    d_ocross = sum_dp(weight_grad(mixed_cross, grad_two), True)
    d_mixed_cross = [dot_nt(grad_two[b], o_cross).astype(bf16) for b in each_batch]
    d_query, d_kv = [], None
    for b in each_batch:
        dq, d_kv = cross_backward(query[b], kv, d_mixed_cross[b], which[b], patch, d_kv)
        d_query.append(dq)
    d_qcross = sum_dp(weight_grad(full_two, d_query), False)
    d_wkv = sum_dp(dot_tn(patches, d_kv), True)

    back = [
        norm_back(
            x_one[b],
            norm_two[b][1],
            gain_cross,
            scatter(product(d_query[b], q_cross, dot_nt), rows, False),
        )
        for b in each_batch
    ]
    d_gain_cross = sum(item[1] for item in back)
    grad_one_rows = [grad_two_rows[b] + back[b][0] for b in each_batch]
    grad_one = [gather(grad_one_rows[b].astype(bf16)) for b in each_batch]
    d_oself = sum_dp(weight_grad(mixed_self, grad_one), False)
    d_mixed_self = [dot_nt(grad_one[b], o_self).astype(bf16) for b in each_batch]
    d_qkv = [
        self_backward(qkv[b], d_mixed_self[b], lengths[b], prefixes[b]) for b in each_batch
    ]
    d_wqkv = sum_dp(weight_grad(full_one, d_qkv), True)

    back = [
        norm_back(
            x_zero[b],
            norm_one[b][1],
            gain_attn,
            scatter(product(d_qkv[b], w_qkv, dot_nt), rows, False),
        )
        for b in each_batch
    ]
    d_gain_attn = sum(item[1] for item in back)
    grad_input = jnp.concatenate([grad_one_rows[b] + back[b][0] for b in each_batch], axis=0)
    output = jnp.concatenate(
        [
            (x_two[b] + scatter(product(hidden[b], w_down, dot_nn), rows, True)).astype(bf16)
            for b in each_batch
        ],
        axis=0,
    )
    gains = butterfly(butterfly(jnp.stack([d_gain_attn, d_gain_cross, d_gain_mlp]), "mp"), "dp")
    return (
        output,
        grad_input,
        d_wqkv[:, :width],
        d_wqkv[:, width : 2 * width],
        d_wqkv[:, 2 * width :],
        d_oself,
        d_qcross,
        d_wkv[:, :width],
        d_wkv[:, width:],
        d_ocross,
        d_wgate,
        d_wup,
        d_wdown,
        gains[0],
        gains[1],
        gains[2],
    )


def solution(mesh):
    by_rows = P(("dp", "mp"), None)
    columns = P(None, "mp")
    rows = P("mp", None)
    weights = (columns, columns, columns, rows, columns, columns, columns, rows, columns, columns, rows)
    in_specs = (
        (by_rows, P("dp", None), P("dp"), P("dp"), P("dp"), P(), by_rows) + weights + (P(), P(), P())
    )
    out_specs = (by_rows, by_rows) + weights + (P(), P(), P())
    return jax.shard_map(
        on_device, mesh=mesh, in_specs=in_specs, out_specs=out_specs, check_vma=False
    )
```

time: 2400 us -> 1890 us (0.79)
  waiting for transfers between devices: 1590 us -> 816 us
  starting transfers between devices: 0.54 us -> 241 us
  Pallas kernels: 0 us -> 174 us
  matrix products: 449 us -> 349 us
  other arithmetic: 122 us -> 208 us
  blocking collectives: 67 us -> 0 us
  local copies, waits for them, and re-layouts: 146 us -> 84.8 us
    psum x1 -> x0, waiting for transfers between devices: 914 us -> none  [on_device(): lax.psum(d_kcross.astype(jnp.bfloat16), 'dp').astype(jnp.float32)]
    ppermute x0 -> x108, waiting for transfers between devices: none -> 816 us  [the longest x40 440 us: send(): return lax.ppermute(tensor, 'dp', which)]
    reduce_scatter x6 -> x0, waiting for transfers between devices: 502 us -> none  [the longest x3 377 us: collect(): lax.psum_scatter(term(jnp.int32(0), row_count * lax.axis_size('mp')), 'mp...]
    ppermute x0 -> x108, starting transfers between devices: none -> 241 us  [the longest x40 175 us: send(): return lax.ppermute(tensor, 'dp', which)]
    all_gather x6 -> x0, waiting for transfers between devices: 176 us -> none  [the longest x3 89.2 us: spread_grad(): return lax.all_gather(rows_local, 'mp', axis=0, tiled=True)]
    pallas_call x0 -> x10, Pallas kernels: none -> 174 us  [the longest x2 48.9 us: mlp(): pl.pallas_call(mlp_kernel, grid=(units // tile,), in_specs=[whole, whole,...]
    dot_general x43 -> x52, matrix products: 449 us -> 349 us  [the longest x15 131 us: dot_tn(): lax.dot_general(left, right, (((0,), (0,)), ((), ())), preferred_element_...]
    reshape x16 -> x1, local copies, waits for them, and re-layouts: 105 us -> 7.97 us  [cut(): both = tensor.reshape(2, tensor.shape[0] // 2, tensor.shape[1])]
  transfers between devices with their start and end apart: 13 -> 108, of which waited for: 11 -> 37; matrix products, arithmetic and copies ran while one was open for 12% -> 32% of each run, Pallas kernels for 0% -> 8%
where the time goes in v1:
time: 1890 us; the launch traced here: 1880 us
  waiting for transfers between devices  816 us (43%)
  matrix products  349 us (18%)
  starting transfers between devices  241 us (13%)
  other arithmetic  208 us (11%)
  Pallas kernels  174 us (9%)
  local copies, waits for them, and re-layouts  84.8 us (4%)
    ppermute x40, waiting for transfers between devices, send(): return lax.ppermute(tensor, 'dp', which)  440 us
    ppermute x68, waiting for transfers between devices, flip(): return lax.ppermute(tensor, axis, [(i, i ^ bit) for i in range(count)])  376 us
    ppermute x40, starting transfers between devices, send(): return lax.ppermute(tensor, 'dp', which)  175 us
    dot_general x15, matrix products, dot_tn(): lax.dot_general(left, right, (((0,), (0,)), ((), ())), preferred_element_...  131 us
    dot_general x20, matrix products, dot_nt(): lax.dot_general(left, right, (((1,), (1,)), ((), ())), preferred_element_...  115 us
    dot_general x17, matrix products, dot_nn(): return jnp.dot(left, right, preferred_element_type=f32)  103 us
    convert_element_type x24, other arithmetic, plus(): return (left.astype(f32) + right.astype(f32)).astype(bf16)  68.7 us
    ppermute x68, starting transfers between devices, flip(): return lax.ppermute(tensor, axis, [(i, i ^ bit) for i in range(count)])  65.5 us
  transfers between devices with their start and end apart: 108, of which 37 were waited for; matrix products, arithmetic and copies ran while one was open for 32% of the time, Pallas kernels for 8%

profile of v1, /device:TPU:0, one launch (start us, length us, event | category | flops | bytes accessed | tf_op | source)
XLA Modules:
  0.0 1875.2 jit_solution(13817158542756757776)
XLA Ops:
  13.5 42.3 %collective-permute-done.21 = bf16[256,2048]{1,0:T(8,128)(2,1)} collective-permute-done((bf16[256,2048]{1,0:T(8,128)(2,1)}, bf16[256,2048]{1,0:T(8,128)(2,1)}, u32[]{:S(2)}, u32[]{:S(2)}) %collective-permute-start.21) | collective-permute-done | bytes 1048608 | tf_op jit(solution)/shard_map/ppermute | solution.py:302
  116.8 22.0 %collective-permute-done.25 = bf16[256,2048]{1,0:T(8,128)(2,1)S(1)} collective-permute-done((bf16[256,2048]{1,0:T(8,128)(2,1)S(1)}, bf16[256,2048]{1,0:T(8,128)(2,1)S(1)}, u32[]{:S(2)}, u32[]{:S(2)}) %collective-permute-start.25) | collective-permute-done | bytes 1048608 | tf_op jit(solution)/shard_map/ppermute | solution.py:302
  138.8 21.6 %collective-permute-done.4 = bf16[256,2048]{1,0:T(8,128)(2,1)S(1)} collective-permute-done((bf16[256,2048]{1,0:T(8,128)(2,1)S(1)}, bf16[256,2048]{1,0:T(8,128)(2,1)S(1)}, u32[]{:S(2)}, u32[]{:S(2)}) %collective-permute-start.4) | collective-permute-done | bytes 1048608 | tf_op jit(solution)/shard_map/ppermute | solution.py:302
  188.7 22.6 %convert_bitcast_fusion.kv_ref = bf16[4096,1024]{1,0:T(8,128)(2,1)} fusion(bf16[4096,2048]{1,0:T(8,128)(2,1)} %param.24, bf16[2048,512]{1,0:T(8,128)(2,1)S(1)} %copy-done.112, bf16[2048,512]{1,0:T(8,128)(2,1)S(1)} %copy-done.113), kind=kOutput, calls=%fused_computation.10 | convolution fusion | flops 17192452096 | bytes 29360128 | tf_op jit(solution)/shard_map/dot_general | solution.py:20
  279.1 20.9 %collective-permute-done.9 = bf16[256,2048]{1,0:T(8,128)(2,1)S(1)} collective-permute-done((bf16[256,2048]{1,0:T(8,128)(2,1)S(1)}, bf16[256,2048]{1,0:T(8,128)(2,1)S(1)}, u32[]{:S(2)}, u32[]{:S(2)}) %collective-permute-start.9) | collective-permute-done | bytes 1048608 | tf_op jit(solution)/shard_map/ppermute | solution.py:302
  369.7 24.4 %shard_map.326 = (bf16[1024,1280]{1,0:T(8,128)(2,1)}, bf16[1024,1280]{1,0:T(8,128)(2,1)}, bf16[1024,1280]{1,0:T(8,128)(2,1)}) custom-call(bf16[1024,2048]{1,0:T(8,128)(2,1)} %pad_maximum_fusion.4.norm_ref, bf16[1024,2048]{1,0:T(8,128)(2,1)} %pad_maximum_fusion.5.grad_ref, bf16[2048,1280]{1,0:T(8,128)(2,1)} %gate_ref.3, bf16[2048,1280]{1,0:T(8,128)(2,1)} %up_ref.3, ...), custom_call_target="tpu_custom_call" | custom-call | flops 16106127360 | bytes 31981568 | tf_op jit(solution)/shard_map/pallas_call | solution.py:285
  439.6 22.0 %collective-permute-done.20 = bf16[256,2048]{1,0:T(8,128)(2,1)} collective-permute-done((bf16[256,2048]{1,0:T(8,128)(2,1)S(1)}, bf16[256,2048]{1,0:T(8,128)(2,1)}, u32[]{:S(2)}, u32[]{:S(2)}) %collective-permute-start.20) | collective-permute-done | bytes 1048608 | tf_op jit(solution)/shard_map/ppermute | solution.py:302
  461.6 22.4 %collective-permute-done.40 = bf16[256,2048]{1,0:T(8,128)(2,1)S(1)} collective-permute-done((bf16[256,2048]{1,0:T(8,128)(2,1)S(1)}, bf16[256,2048]{1,0:T(8,128)(2,1)S(1)}, u32[]{:S(2)}, u32[]{:S(2)}) %collective-permute-start.40) | collective-permute-done | bytes 1048608 | tf_op jit(solution)/shard_map/ppermute | solution.py:302
  507.1 21.0 %collective-permute-done.31 = bf16[256,2048]{1,0:T(8,128)(2,1)} collective-permute-done((bf16[256,2048]{1,0:T(8,128)(2,1)}, bf16[256,2048]{1,0:T(8,128)(2,1)}, u32[]{:S(2)}, u32[]{:S(2)}) %collective-permute-start.31) | collective-permute-done | bytes 1048608 | tf_op jit(solution)/shard_map/ppermute | solution.py:302
  535.6 24.5 %shard_map.329 = (bf16[1024,1280]{1,0:T(8,128)(2,1)}, bf16[1024,1280]{1,0:T(8,128)(2,1)}, bf16[1024,1280]{1,0:T(8,128)(2,1)}) custom-call(bf16[1024,2048]{1,0:T(8,128)(2,1)} %pad_maximum_fusion.8.norm_ref, bf16[1024,2048]{1,0:T(8,128)(2,1)} %pad_maximum_fusion.9.grad_ref, bf16[2048,1280]{1,0:T(8,128)(2,1)} %gate_ref.3, bf16[2048,1280]{1,0:T(8,128)(2,1)} %up_ref.3, ...), custom_call_target="tpu_custom_call" | custom-call | flops 16106127360 | bytes 31981568 | tf_op jit(solution)/shard_map/pallas_call | solution.py:285
  668.6 21.0 %collective-permute-done.38 = bf16[256,2048]{1,0:T(8,128)(2,1)S(1)} collective-permute-done((bf16[256,2048]{1,0:T(8,128)(2,1)S(1)}, bf16[256,2048]{1,0:T(8,128)(2,1)S(1)}, u32[]{:S(2)}, u32[]{:S(2)}) %collective-permute-start.38) | collective-permute-done | bytes 1048608 | tf_op jit(solution)/shard_map/ppermute | solution.py:302
  741.9 52.1 %collective-permute-done.89 = bf16[1024,1280]{1,0:T(8,128)(2,1)S(1)} collective-permute-done((bf16[1024,1280]{1,0:T(8,128)(2,1)S(1)}, bf16[1024,1280]{1,0:T(8,128)(2,1)S(1)}, u32[]{:S(2)}, u32[]{:S(2)}) %collective-permute-start.89) | collective-permute-done | bytes 2621472 | tf_op jit(solution)/shard_map/ppermute | solution.py:356
  818.5 21.9 %shard_map.330 = (bf16[1024,512]{1,0:T(8,128)(2,1)}, bf16[4096,1024]{1,0:T(8,128)(2,1)}) custom-call(s32[8]{0:T(128)} %copy-done.100, bf16[1024,512]{1,0:T(8,128)(2,1)} %convolution_convert_fusion.17.query_ref, bf16[4096,1024]{1,0:T(8,128)(2,1)} %convert_bitcast_fusion.kv_ref, bf16[1024,512]{1,0:T(8,128)(2,1)} %convolution_convert_fusion.15.grad_ref), custom_call_target="tpu_custom_call" | custom-call | flops 2684354560 | bytes 12582912 | tf_op jit(solution)/shard_map/pallas_call | solution.py:240
  850.2 21.9 %shard_map.332 = (bf16[1024,512]{1,0:T(8,128)(2,1)}, bf16[4096,1024]{1,0:T(8,128)(2,1)}) custom-call(s32[8]{0:T(128)} %copy-done.99, bf16[1024,512]{1,0:T(8,128)(2,1)} %convolution_convert_fusion.16.query_ref, bf16[4096,1024]{1,0:T(8,128)(2,1)} %convert_bitcast_fusion.kv_ref, ...), custom_call_target="tpu_custom_call", output_to_operand_aliasing={{1}: (4, {})} | custom-call | flops 2684354560 | bytes 12582912 | tf_op jit(solution)/shard_map/pallas_call | solution.py:240
  892.1 21.3 %convert_bitcast_fusion.1 = bf16[2048,1024]{0,1:T(8,128)(2,1)} fusion(bf16[4096,1024]{1,0:T(8,128)(2,1)S(1)} %bitcast.138, bf16[4096,2048]{1,0:T(8,128)(2,1)} %param.24), kind=kOutput, calls=%fused_computation.65 | convolution fusion | flops 17181966336 | bytes 29360128 | tf_op jit(solution)/shard_map/dot_general | solution.py:24
  993.4 25.7 %collective-permute-done.78 = bf16[1024,1024]{1,0:T(8,128)(2,1)S(1)} collective-permute-done((bf16[1024,1024]{1,0:T(8,128)(2,1)S(1)}, bf16[1024,1024]{1,0:T(8,128)(2,1)S(1)}, u32[]{:S(2)}, u32[]{:S(2)}) %collective-permute-start.78) | collective-permute-done | bytes 2097184 | tf_op jit(solution)/shard_map/ppermute | solution.py:356
  1027.7 67.1 %collective-permute-start.79 = (bf16[1024,1024]{1,0:T(8,128)(2,1)S(1)}, bf16[1024,1024]{1,0:T(8,128)(2,1)}, u32[]{:S(2)}, u32[]{:S(2)}) collective-permute-start(bf16[1024,1024]{1,0:T(8,128)(2,1)S(1)} %fusion.7), channel_id=1, source_target_pairs={{0,8},{4,12},{24,16},{28,20},{1,9},{5,13},{25,17},{29,21},{2,10},{... | collective-permute-start | bytes 6291464 | tf_op jit(solution)/shard_map/ppermute | solution.py:356
  1290.5 23.2 %collective-permute-start.68 = (bf16[512,2048]{1,0:T(8,128)(2,1)S(1)}, bf16[512,2048]{1,0:T(8,128)(2,1)}, u32[]{:S(2)}, u32[]{:S(2)}) collective-permute-start(bf16[512,2048]{1,0:T(8,128)(2,1)S(1)} %add_convert_fusion.18), channel_id=1, source_target_pairs={{0,8},{4,12},{24,16},{28,20},{1,9},{5,13},{25,17},{29,21},{2,10},{... | collective-permute-start | bytes 6291464 | tf_op jit(solution)/shard_map/ppermute | solution.py:356
  1378.0 70.1 %collective-permute-done.92 = bf16[1024,1280]{1,0:T(8,128)(2,1)} collective-permute-done((bf16[1024,1280]{1,0:T(8,128)(2,1)S(1)}, bf16[1024,1280]{1,0:T(8,128)(2,1)}, u32[]{:S(2)}, u32[]{:S(2)}) %collective-permute-start.92) | collective-permute-done | bytes 2621472 | tf_op jit(solution)/shard_map/ppermute | solution.py:356
  1488.0 44.1 %collective-permute-done.64 = bf16[1024,1536]{1,0:T(8,128)(2,1)} collective-permute-done((bf16[1024,1536]{1,0:T(8,128)(2,1)S(1)}, bf16[1024,1536]{1,0:T(8,128)(2,1)}, u32[]{:S(2)}, u32[]{:S(2)}) %collective-permute-start.64) | collective-permute-done | bytes 3145760 | tf_op jit(solution)/shard_map/ppermute | solution.py:356
  1549.0 21.6 %collective-permute-start.106 = (f32[3,2048]{1,0:T(4,128)S(1)}, f32[3,2048]{1,0:T(4,128)S(1)}, u32[]{:S(2)}, u32[]{:S(2)}) collective-permute-start(f32[3,2048]{1,0:T(4,128)S(1)} %add.538), channel_id=1, source_target_pairs={{0,8},{4,12},{8,0},{12,4},{16,24},{20,28},{24,16},{28,20},{1,9},{5... | collective-permute-start | bytes 73736 | tf_op jit(solution)/shard_map/ppermute | solution.py:302
  1573.3 24.9 %collective-permute-done.106 = f32[3,2048]{1,0:T(4,128)S(1)} collective-permute-done((f32[3,2048]{1,0:T(4,128)S(1)}, f32[3,2048]{1,0:T(4,128)S(1)}, u32[]{:S(2)}, u32[]{:S(2)}) %collective-permute-start.106) | collective-permute-done | bytes 24608 | tf_op jit(solution)/shard_map/ppermute | solution.py:302
  1621.0 63.5 %collective-permute-done.66 = bf16[1024,1536]{1,0:T(8,128)(2,1)} collective-permute-done((bf16[1024,1536]{1,0:T(8,128)(2,1)S(1)}, bf16[1024,1536]{1,0:T(8,128)(2,1)}, u32[]{:S(2)}, u32[]{:S(2)}) %collective-permute-start.66) | collective-permute-done | bytes 3145760 | tf_op jit(solution)/shard_map/ppermute | solution.py:356
  1689.0 144.0 %collective-permute-done.72 = bf16[512,2048]{1,0:T(8,128)(2,1)} collective-permute-done((bf16[512,2048]{1,0:T(8,128)(2,1)S(1)}, bf16[512,2048]{1,0:T(8,128)(2,1)}, u32[]{:S(2)}, u32[]{:S(2)}) %collective-permute-start.72) | collective-permute-done | bytes 2097184 | tf_op jit(solution)/shard_map/ppermute | solution.py:356
  (738 shorter events, 1005.6 us)
Async XLA Ops:
  620.8 261.4 %collective-permute-start.98 = (bf16[1280,2048]{1,0:T(8,128)(2,1)}, bf16[1280,2048]{1,0:T(8,128)(2,1)}, u32[]{:S(2)}, u32[]{:S(2)}) collective-permute-start(bf16[1280,2048]{1,0:T(8,128)(2,1)} %add_convert_fusion.2), channel_id=1, source_target_pairs={{0,8},{4,12},{24,16},{28,20},{1,9},{5,13},{25,17},{29,21},{2,10},{... | collective-permute-start | bytes 15728648 | tf_op jit(solution)/shard_map/ppermute | solution.py:356
  660.3 133.7 %collective-permute-start.89 = (bf16[1024,1280]{1,0:T(8,128)(2,1)S(1)}, bf16[1024,1280]{1,0:T(8,128)(2,1)S(1)}, u32[]{:S(2)}, u32[]{:S(2)}) collective-permute-start(bf16[1024,1280]{1,0:T(8,128)(2,1)S(1)} %fusion.3), channel_id=1, source_target_pairs={{0,8},{4,12},{24,16},{28,20},{1,9},{5,13},{25,17},{29,21},{2,10},{... | collective-permute-start | bytes 7864328 | tf_op jit(solution)/shard_map/ppermute | solution.py:356
  707.1 89.1 %collective-permute-start.54 = (bf16[256,2048]{1,0:T(8,128)(2,1)S(1)}, bf16[256,2048]{1,0:T(8,128)(2,1)S(1)}, u32[]{:S(2)}, u32[]{:S(2)}) collective-permute-start(bf16[256,2048]{1,0:T(8,128)(2,1)S(1)} %get-tuple-element.92), channel_id=1, source_target_pairs={{0,1},{1,0},{2,3},{3,2},{4,5},{5,4},{6,7},{7,6},{8,9},{9,8},{10,11... | collective-permute-start | bytes 3145736 | tf_op jit(solution)/shard_map/ppermute | solution.py:302
  796.2 117.8 %collective-permute-start.93 = (bf16[2048,1280]{1,0:T(8,128)(2,1)}, bf16[2048,1280]{1,0:T(8,128)(2,1)}, u32[]{:S(2)}, u32[]{:S(2)}) collective-permute-start(bf16[2048,1280]{1,0:T(8,128)(2,1)} %add_convert_fusion.4), channel_id=1, source_target_pairs={{0,8},{4,12},{24,16},{28,20},{1,9},{5,13},{25,17},{29,21},{2,10},{... | collective-permute-start | bytes 15728648 | tf_op jit(solution)/shard_map/ppermute | solution.py:356
  803.0 219.6 %collective-permute-start.90 = (bf16[1024,1280]{1,0:T(8,128)(2,1)}, bf16[1024,1280]{1,0:T(8,128)(2,1)}, u32[]{:S(2)}, u32[]{:S(2)}) collective-permute-start(bf16[1024,1280]{1,0:T(8,128)(2,1)} %add_convert_fusion.11), channel_id=1, source_target_pairs={{8,16},{12,20},{16,8},{20,12},{9,17},{13,21},{17,9},{21,13},{10,18... | collective-permute-start | bytes 7864328 | tf_op jit(solution)/shard_map/ppermute | solution.py:356
  810.9 161.2 %collective-permute-start.83 = (bf16[256,2048]{1,0:T(8,128)(2,1)S(1)}, bf16[256,2048]{1,0:T(8,128)(2,1)}, u32[]{:S(2)}, u32[]{:S(2)}) collective-permute-start(bf16[256,2048]{1,0:T(8,128)(2,1)S(1)} %dynamic-slice_bitcast_fusion.4), channel_id=1, source_target_pairs={{0,4},{4,0},{8,12},{12,8},{16,20},{20,16},{24,28},{28,24},{1,5},{5... | collective-permute-start | bytes 3145736 | tf_op jit(solution)/shard_map/ppermute | solution.py:356
  844.2 131.1 %collective-permute-start.44 = (bf16[512,2048]{1,0:T(8,128)(2,1)}, bf16[512,2048]{1,0:T(8,128)(2,1)}, u32[]{:S(2)}, u32[]{:S(2)}) collective-permute-start(bf16[512,2048]{1,0:T(8,128)(2,1)} %convolution_convert_fusion.5), channel_id=1, source_target_pairs={{0,1},{1,0},{2,3},{3,2},{4,5},{5,4},{6,7},{7,6},{8,9},{9,8},{10,11... | collective-permute-start | bytes 6291464 | tf_op jit(solution)/shard_map/ppermute | solution.py:302
  882.2 98.4 %collective-permute-start.56 = (bf16[512,2048]{1,0:T(8,128)(2,1)}, bf16[512,2048]{1,0:T(8,128)(2,1)}, u32[]{:S(2)}, u32[]{:S(2)}) collective-permute-start(bf16[512,2048]{1,0:T(8,128)(2,1)} %convolution_convert_fusion.3), channel_id=1, source_target_pairs={{0,1},{1,0},{2,3},{3,2},{4,5},{5,4},{6,7},{7,6},{8,9},{9,8},{10,11... | collective-permute-start | bytes 6291464 | tf_op jit(solution)/shard_map/ppermute | solution.py:302
  975.3 136.6 %collective-permute-start.99 = (bf16[640,2048]{1,0:T(8,128)(2,1)}, bf16[640,2048]{1,0:T(8,128)(2,1)}, u32[]{:S(2)}, u32[]{:S(2)}) collective-permute-start(bf16[640,2048]{1,0:T(8,128)(2,1)} %dynamic-slice_bitcast_fusion.1), channel_id=1, source_target_pairs={{8,16},{12,20},{16,8},{20,12},{9,17},{13,21},{17,9},{21,13},{10,18... | collective-permute-start | bytes 7864328 | tf_op jit(solution)/shard_map/ppermute | solution.py:356
  1027.7 107.8 %collective-permute-start.79 = (bf16[1024,1024]{1,0:T(8,128)(2,1)S(1)}, bf16[1024,1024]{1,0:T(8,128)(2,1)}, u32[]{:S(2)}, u32[]{:S(2)}) collective-permute-start(bf16[1024,1024]{1,0:T(8,128)(2,1)S(1)} %fusion.7), channel_id=1, source_target_pairs={{0,8},{4,12},{24,16},{28,20},{1,9},{5,13},{25,17},{29,21},{2,10},{... | collective-permute-start | bytes 6291464 | tf_op jit(solution)/shard_map/ppermute | solution.py:356
  1135.5 134.7 %collective-permute-start.91 = (bf16[1024,1280]{1,0:T(8,128)(2,1)S(1)}, bf16[1024,1280]{1,0:T(8,128)(2,1)}, u32[]{:S(2)}, u32[]{:S(2)}) collective-permute-start(bf16[1024,1280]{1,0:T(8,128)(2,1)S(1)} %add_convert_fusion.10), channel_id=1, source_target_pairs={{8,0},{12,4},{16,24},{20,28},{9,1},{13,5},{17,25},{21,29},{10,2},{... | collective-permute-start | bytes 7864328 | tf_op jit(solution)/shard_map/ppermute | solution.py:356
  1165.2 121.1 %collective-permute-start.95 = (bf16[1024,1280]{1,0:T(8,128)(2,1)S(1)}, bf16[1024,1280]{1,0:T(8,128)(2,1)}, u32[]{:S(2)}, u32[]{:S(2)}) collective-permute-start(bf16[1024,1280]{1,0:T(8,128)(2,1)S(1)} %fusion.2), channel_id=1, source_target_pairs={{8,12},{12,8},{16,20},{20,16},{9,13},{13,9},{17,21},{21,17},{10,14... | collective-permute-start | bytes 7864328 | tf_op jit(solution)/shard_map/ppermute | solution.py:356
  1192.4 90.6 %collective-permute-start.76 = (bf16[1024,512]{1,0:T(8,128)(2,1)}, bf16[1024,512]{1,0:T(8,128)(2,1)}, u32[]{:S(2)}, u32[]{:S(2)}) collective-permute-start(bf16[1024,512]{1,0:T(8,128)(2,1)} %add_convert_fusion.23), channel_id=1, source_target_pairs={{8,16},{12,20},{16,8},{20,12},{9,17},{13,21},{17,9},{21,13},{10,18... | collective-permute-start | bytes 3145736 | tf_op jit(solution)/shard_map/ppermute | solution.py:356
  1194.1 122.3 %collective-permute-start.80 = (bf16[1024,1024]{1,0:T(8,128)(2,1)}, bf16[1024,1024]{1,0:T(8,128)(2,1)}, u32[]{:S(2)}, u32[]{:S(2)}) collective-permute-start(bf16[1024,1024]{1,0:T(8,128)(2,1)} %add_convert_fusion.14), channel_id=1, source_target_pairs={{8,16},{12,20},{16,8},{20,12},{9,17},{13,21},{17,9},{21,13},{10,18... | collective-permute-start | bytes 6291464 | tf_op jit(solution)/shard_map/ppermute | solution.py:356
  1270.2 101.2 %collective-permute-start.101 = (bf16[640,2048]{1,0:T(8,128)(2,1)S(1)}, bf16[640,2048]{1,0:T(8,128)(2,1)}, u32[]{:S(2)}, u32[]{:S(2)}) collective-permute-start(bf16[640,2048]{1,0:T(8,128)(2,1)S(1)} %add_convert_fusion.8), channel_id=1, source_target_pairs={{8,16},{12,20},{16,8},{20,12},{9,17},{13,21},{17,9},{21,13},{10,18... | collective-permute-start | bytes 7864328 | tf_op jit(solution)/shard_map/ppermute | solution.py:356
  1322.1 131.9 %collective-permute-start.63 = (bf16[1024,1536]{1,0:T(8,128)(2,1)}, bf16[1024,1536]{1,0:T(8,128)(2,1)}, u32[]{:S(2)}, u32[]{:S(2)}) collective-permute-start(bf16[1024,1536]{1,0:T(8,128)(2,1)} %dynamic-slice_bitcast_fusion), channel_id=1, source_target_pairs={{0,4},{4,0},{8,12},{12,8},{16,20},{20,16},{24,28},{28,24},{1,5},{5... | collective-permute-start | bytes 9437192 | tf_op jit(solution)/shard_map/ppermute | solution.py:356
  1329.5 118.6 %collective-permute-start.92 = (bf16[1024,1280]{1,0:T(8,128)(2,1)S(1)}, bf16[1024,1280]{1,0:T(8,128)(2,1)}, u32[]{:S(2)}, u32[]{:S(2)}) collective-permute-start(bf16[1024,1280]{1,0:T(8,128)(2,1)S(1)} %broadcast_select_fusion.7), channel_id=1, source_target_pairs={{0,4},{4,0},{8,12},{12,8},{16,20},{20,16},{24,28},{28,24},{1,5},{5... | collective-permute-start | bytes 7864328 | tf_op jit(solution)/shard_map/ppermute | solution.py:356
  1357.2 102.2 %collective-permute-start.96 = (bf16[1024,1280]{1,0:T(8,128)(2,1)}, bf16[1024,1280]{1,0:T(8,128)(2,1)}, u32[]{:S(2)}, u32[]{:S(2)}) collective-permute-start(bf16[1024,1280]{1,0:T(8,128)(2,1)} %add_convert_fusion.9), channel_id=1, source_target_pairs={{8,16},{12,20},{16,8},{20,12},{9,17},{13,21},{17,9},{21,13},{10,18... | collective-permute-start | bytes 7864328 | tf_op jit(solution)/shard_map/ppermute | solution.py:356
  1365.9 175.3 %collective-permute-start.81 = (bf16[1024,1024]{1,0:T(8,128)(2,1)S(1)}, bf16[1024,1024]{1,0:T(8,128)(2,1)}, u32[]{:S(2)}, u32[]{:S(2)}) collective-permute-start(bf16[1024,1024]{1,0:T(8,128)(2,1)S(1)} %add_convert_fusion.13), channel_id=1, source_target_pairs={{8,0},{12,4},{16,24},{20,28},{9,1},{13,5},{17,25},{21,29},{10,2},{... | collective-permute-start | bytes 6291464 | tf_op jit(solution)/shard_map/ppermute | solution.py:356
  1371.4 111.4 %collective-permute-start.50 = (bf16[256,2048]{1,0:T(8,128)(2,1)}, bf16[256,2048]{1,0:T(8,128)(2,1)S(1)}, u32[]{:S(2)}, u32[]{:S(2)}) collective-permute-start(bf16[256,2048]{1,0:T(8,128)(2,1)} %slice.527), channel_id=1, source_target_pairs={{0,2},{1,3},{2,0},{3,1},{4,6},{5,7},{6,4},{7,5},{8,10},{9,11},{10,... | collective-permute-start | bytes 3145736 | tf_op jit(solution)/shard_map/ppermute | solution.py:302
  1482.9 354.6 %collective-permute-start.102 = (bf16[1280,2048]{1,0:T(8,128)(2,1)}, bf16[1280,2048]{1,0:T(8,128)(2,1)}, u32[]{:S(2)}, u32[]{:S(2)}) collective-permute-start(bf16[1280,2048]{1,0:T(8,128)(2,1)} %pad_maximum_fusion.1), channel_id=1, source_target_pairs={{8,0},{12,4},{16,24},{20,28},{9,1},{13,5},{17,25},{21,29},{10,2},{... | collective-permute-start | bytes 15728648 | tf_op jit(solution)/shard_map/ppermute | solution.py:356
  1611.4 234.9 %collective-permute-start.97 = (bf16[2048,1280]{1,0:T(8,128)(2,1)}, bf16[2048,1280]{1,0:T(8,128)(2,1)}, u32[]{:S(2)}, u32[]{:S(2)}) collective-permute-start(bf16[2048,1280]{1,0:T(8,128)(2,1)} %pad_maximum_fusion), channel_id=1, source_target_pairs={{8,0},{12,4},{16,24},{20,28},{9,1},{13,5},{17,25},{21,29},{10,2},{... | collective-permute-start | bytes 15728648 | tf_op jit(solution)/shard_map/ppermute | solution.py:356
  1613.7 219.3 %collective-permute-start.72 = (bf16[512,2048]{1,0:T(8,128)(2,1)S(1)}, bf16[512,2048]{1,0:T(8,128)(2,1)}, u32[]{:S(2)}, u32[]{:S(2)}) collective-permute-start(bf16[512,2048]{1,0:T(8,128)(2,1)S(1)} %pad_maximum_fusion.16), channel_id=1, source_target_pairs={{8,0},{12,4},{16,24},{20,28},{9,1},{13,5},{17,25},{21,29},{10,2},{... | collective-permute-start | bytes 6291464 | tf_op jit(solution)/shard_map/ppermute | solution.py:356
  1688.5 167.0 %collective-permute-start.67 = (bf16[1024,1536]{1,0:T(8,128)(2,1)}, bf16[1024,1536]{1,0:T(8,128)(2,1)}, u32[]{:S(2)}, u32[]{:S(2)}) collective-permute-start(bf16[1024,1536]{1,0:T(8,128)(2,1)} %broadcast_select_fusion), channel_id=1, source_target_pairs={{0,4},{4,0},{8,12},{12,8},{16,20},{20,16},{24,28},{28,24},{1,5},{5... | collective-permute-start | bytes 9437192 | tf_op jit(solution)/shard_map/ppermute | solution.py:356
  (250 other events, 7067.2 us)

commit v2 on v1

v2 whole, which is shorter than its diff:
```python
from functools import partial

import jax
import jax.numpy as jnp
from jax import lax
from jax.experimental import pallas as pl
from jax.experimental.pallas import tpu as pltpu
from jax.sharding import PartitionSpec as P

HEAD = 64
SEQ = 128
PAIR = 2 * HEAD
epsilon = 1e-06
f32 = jnp.float32
bf16 = jnp.bfloat16
VMEM_LIMIT = 56 * 1024 * 1024
MESH = pl.DeviceIdType.MESH


def dot_nn(left, right):
    return jnp.dot(left, right, preferred_element_type=f32)


def dot_tn(left, right):
    return lax.dot_general(left, right, (((0,), (0,)), ((), ())), preferred_element_type=f32)


def dot_nt(left, right):
    return lax.dot_general(left, right, (((1,), (1,)), ((), ())), preferred_element_type=f32)


def normalize(values_in, gain):
    row_scale = lax.rsqrt(jnp.mean(values_in * values_in, axis=-1, keepdims=True) + epsilon)
    return ((values_in * row_scale * gain).astype(bf16), row_scale)


def norm_back(values_in, row_scale, gain, incoming):
    weighted = incoming * gain
    inner = jnp.mean(weighted * values_in, axis=-1, keepdims=True)
    return (
        row_scale * weighted - values_in * row_scale**3 * inner,
        jnp.sum(incoming * values_in * row_scale, axis=0),
    )


def first_head():
    return lax.broadcasted_iota(jnp.int32, (SEQ, PAIR), 1) < HEAD


def stack_pair(rows, first):
    zero = jnp.zeros_like(rows)
    return jnp.concatenate([jnp.where(first, rows, zero), jnp.where(first, zero, rows)], axis=0)


def unstack_pair(stacked, first):
    return jnp.where(first, stacked[:SEQ], stacked[SEQ:])


def self_mask(length, prefix):
    query_at = lax.broadcasted_iota(jnp.int32, (2 * SEQ, SEQ), 0) % SEQ
    key_at = lax.broadcasted_iota(jnp.int32, (2 * SEQ, SEQ), 1)
    return (key_at < length) & ((key_at <= query_at) | (key_at < prefix))


def pair_probs(stacked_query, keys, mask):
    scores = dot_nt(stacked_query, keys)
    if mask is not None:
        scores = jnp.where(mask, scores, -1e30)
    expd = jnp.exp(scores - jnp.max(scores, axis=-1, keepdims=True))
    return expd * (1.0 / jnp.sum(expd, axis=-1, keepdims=True))


def pair_forward(query, keys, values, mask, first):
    scaled = stack_pair(query * jnp.asarray(HEAD**-0.5, bf16), first)
    probs = pair_probs(scaled, keys, mask)
    return unstack_pair(dot_nn(probs.astype(bf16), values), first).astype(bf16)


def pair_backward(grad, query, keys, values, mask, first):
    scaled = stack_pair(query * jnp.asarray(HEAD**-0.5, bf16), first)
    probs = pair_probs(scaled, keys, mask)
    grads = stack_pair(grad, first)
    d_probs = dot_nt(grads, values)
    d_scores = (
        probs * (d_probs - jnp.sum(probs * d_probs, axis=-1, keepdims=True))
    ).astype(bf16)
    d_query = unstack_pair(dot_nn(d_scores, keys), first) * HEAD**-0.5
    d_keys = dot_tn(d_scores, scaled)
    d_values = dot_tn(probs.astype(bf16), grads)
    return d_query.astype(bf16), d_keys.astype(bf16), d_values.astype(bf16)


def lanes(part, width, pair):
    return slice(part * width + pair * PAIR, part * width + (pair + 1) * PAIR)


def self_forward_kernel(length_ref, prefix_ref, qkv_ref, out_ref):
    at = pl.program_id(0)
    width = out_ref.shape[1]
    first = first_head()
    mask = self_mask(length_ref[at], prefix_ref[at])
    for pair in range(width // PAIR):
        out_ref[:, lanes(0, width, pair)] = pair_forward(
            qkv_ref[:, lanes(0, width, pair)],
            qkv_ref[:, lanes(1, width, pair)],
            qkv_ref[:, lanes(2, width, pair)],
            mask,
            first,
        )


def self_backward_kernel(length_ref, prefix_ref, qkv_ref, grad_ref, out_ref):
    at = pl.program_id(0)
    width = grad_ref.shape[1]
    first = first_head()
    mask = self_mask(length_ref[at], prefix_ref[at])
    for pair in range(width // PAIR):
        for part, value in enumerate(
            pair_backward(
                grad_ref[:, lanes(0, width, pair)],
                qkv_ref[:, lanes(0, width, pair)],
                qkv_ref[:, lanes(1, width, pair)],
                qkv_ref[:, lanes(2, width, pair)],
                mask,
                first,
            )
        ):
            out_ref[:, lanes(part, width, pair)] = value


def cross_forward_kernel(which_ref, query_ref, key_ref, value_ref, out_ref):
    width = out_ref.shape[1]
    first = first_head()
    for pair in range(width // PAIR):
        at = lanes(0, width, pair)
        out_ref[:, at] = pair_forward(
            query_ref[:, at], key_ref[:, at], value_ref[:, at], None, first
        )


def cross_backward_kernel(which_ref, query_ref, key_ref, value_ref, grad_ref, *rest):
    d_query_ref, d_key_ref, d_value_ref = rest[-3:]
    width = query_ref.shape[1]
    first = first_head()
    for pair in range(width // PAIR):
        at = lanes(0, width, pair)
        d_query_ref[:, at], d_key_ref[:, at], d_value_ref[:, at] = pair_backward(
            grad_ref[:, at], query_ref[:, at], key_ref[:, at], value_ref[:, at], None, first
        )


def params():
    return pltpu.CompilerParams(vmem_limit_bytes=ROOM)


def by_row(width):
    return pl.BlockSpec((SEQ, width), lambda i, *_: (i, 0))


def attention_cost(examples, width, keys, dots, moved):
    return pl.CostEstimate(
        flops=dots * 2 * examples * SEQ * keys * width * 2,
        bytes_accessed=moved,
        transcendentals=examples * SEQ * keys * width // HEAD,
    )


def self_forward(qkv, length, prefix):
    rows, triple = qkv.shape
    width = triple // 3
    return pl.pallas_call(
        self_forward_kernel,
        grid_spec=pltpu.PrefetchScalarGridSpec(
            num_scalar_prefetch=2,
            grid=(rows // SEQ,),
            in_specs=[by_row(triple)],
            out_specs=by_row(width),
        ),
        out_shape=jax.ShapeDtypeStruct((rows, width), bf16),
        compiler_params=params(),
        cost_estimate=attention_cost(rows // SEQ, width, SEQ, 2, rows * width * 8),
    )(length, prefix, qkv)


def self_backward(qkv, grad, length, prefix):
    rows, triple = qkv.shape
    width = triple // 3
    return pl.pallas_call(
        self_backward_kernel,
        grid_spec=pltpu.PrefetchScalarGridSpec(
            num_scalar_prefetch=2,
            grid=(rows // SEQ,),
            in_specs=[by_row(triple), by_row(width)],
            out_specs=by_row(triple),
        ),
        out_shape=jax.ShapeDtypeStruct((rows, triple), bf16),
        compiler_params=params(),
        cost_estimate=attention_cost(rows // SEQ, width, SEQ, 5, rows * width * 14),
    )(length, prefix, qkv, grad)


def cross_forward(query, keys, values, which, patch):
    rows, width = query.shape
    by_patch = pl.BlockSpec((patch, width), lambda i, which: (which[i], 0))
    return pl.pallas_call(
        cross_forward_kernel,
        grid_spec=pltpu.PrefetchScalarGridSpec(
            num_scalar_prefetch=1,
            grid=(rows // SEQ,),
            in_specs=[by_row(width), by_patch, by_patch],
            out_specs=by_row(width),
        ),
        out_shape=jax.ShapeDtypeStruct((rows, width), bf16),
        compiler_params=params(),
        cost_estimate=attention_cost(rows // SEQ, width, patch, 2, rows * width * 12),
    )(which, query, keys, values)


def cross_backward(query, keys, values, grad, which, patch, earlier):
    rows, width = query.shape
    by_patch = pl.BlockSpec((patch, width), lambda i, which: (which[i], 0))
    in_specs = [by_row(width), by_patch, by_patch, by_row(width)]
    operands = [which, query, keys, values, grad]
    aliases = {}
    for at, item in enumerate(earlier):
        in_specs.append(pl.BlockSpec(memory_space=pl.ANY))
        aliases[len(operands)] = 1 + at
        operands.append(item)
    whole = jax.ShapeDtypeStruct(keys.shape, bf16)
    return pl.pallas_call(
        cross_backward_kernel,
        grid_spec=pltpu.PrefetchScalarGridSpec(
            num_scalar_prefetch=1,
            grid=(rows // SEQ,),
            in_specs=in_specs,
            out_specs=[by_row(width), by_patch, by_patch],
        ),
        out_shape=[jax.ShapeDtypeStruct((rows, width), bf16), whole, whole],
        input_output_aliases=aliases,
        compiler_params=params(),
        cost_estimate=attention_cost(rows // SEQ, width, patch, 5, rows * width * 24),
    )(*operands)


def other_core():
    me = lax.axis_index("mp")
    return me + 1 - 2 * lax.rem(me, 2)


def meet(partner):
    barrier = pltpu.get_barrier_semaphore()
    pl.semaphore_signal(barrier, inc=1, device_id={"mp": partner}, device_id_type=MESH)
    pl.semaphore_wait(barrier, 1)


def to_partner(source, target, send_sem, recv_sem, partner):
    return pltpu.make_async_remote_copy(
        src_ref=source,
        dst_ref=target,
        send_sem=send_sem,
        recv_sem=recv_sem,
        device_id={"mp": partner},
        device_id_type=MESH,
    )


def columns_of(weight, tile, size, transposed):
    at = pl.ds(pl.multiple_of(tile * size, size), size)
    return weight[at, :] if transposed else weight[:, at]


def gathered_kernel(transposed, size, own, beside, across, weight, full, out, corner, sems, local):
    dot = dot_nt if transposed else dot_nn
    rows = own.shape[0]
    blocks = (own, beside, across, corner)
    partner = other_core()
    given = to_partner(across, corner, sems.at[0], sems.at[1], partner)
    keep = [
        pltpu.make_async_copy(block, full.at[pl.ds(at * rows, rows)], local.at[at])
        for at, block in enumerate(blocks)
    ]
    meet(partner)
    given.start()
    for at in range(3):
        keep[at].start()

    def multiply(places):
        @pl.loop(0, out.shape[1] // size)
        def _(tile):
            right = columns_of(weight, tile, size, transposed)
            to = pl.ds(pl.multiple_of(tile * size, size), size)
            for at in places:
                out[at * rows : (at + 1) * rows, to] = dot(blocks[at][...], right).astype(bf16)

    multiply((0, 1, 2))
    given.wait()
    keep[3].start()
    multiply((3,))
    for at in range(4):
        keep[at].wait()


IN_VMEM = pl.BlockSpec(memory_space=pltpu.VMEM)
ROOM = 24 * 1024 * 1024


def gathered_dot(own, arrived, weight, transposed, ident):
    if lax.axis_size("mp") != 4:
        dot = dot_nt if transposed else dot_nn
        return arrived, dot(arrived, weight).astype(bf16)
    across, beside = arrived
    rows, model = own.shape
    units = weight.shape[0 if transposed else 1]
    return pl.pallas_call(
        partial(gathered_kernel, transposed, 512),
        in_specs=[IN_VMEM] * 4,
        out_specs=[pl.BlockSpec(memory_space=pl.ANY), IN_VMEM],
        out_shape=[
            jax.ShapeDtypeStruct((4 * rows, model), bf16),
            jax.ShapeDtypeStruct((4 * rows, units), bf16),
        ],
        scratch_shapes=[
            pltpu.VMEM((rows, model), bf16),
            pltpu.SemaphoreType.DMA((2,)),
            pltpu.SemaphoreType.DMA((4,)),
        ],
        compiler_params=pltpu.CompilerParams(
            collective_id=ident, has_side_effects=True, vmem_limit_bytes=ROOM
        ),
        cost_estimate=pl.CostEstimate(
            flops=8 * rows * model * units,
            bytes_accessed=14 * rows * model + 4 * model * units + 8 * rows * units,
            transcendentals=0,
        ),
    )(own, beside, across, weight)


def scattered_kernel(transposed, count, size, *refs):
    dot = dot_nt if transposed else dot_nn
    lefts, weights = refs[:count], refs[count : 2 * count]
    kept, passed, ready, landed, send_sem, recv_sem = refs[2 * count :]
    rows, model = kept.shape
    tiles = model // size
    partner = other_core()

    def given(tile):
        return to_partner(
            ready.at[tile], landed.at[tile], send_sem.at[tile], recv_sem.at[tile], partner
        )

    def block(at, tile):
        return sum(
            dot(
                left[at * rows : (at + 1) * rows, :],
                columns_of(weight, tile, size, transposed),
            )
            for left, weight in zip(lefts, weights)
        )

    meet(partner)

    @pl.loop(0, tiles)
    def _(tile):
        ready[tile, :rows, :] = block(1, tile).astype(bf16)
        ready[tile, rows:, :] = block(3, tile).astype(bf16)
        given(tile).start()

    @pl.loop(0, tiles)
    def _(tile):
        mine = block(0, tile)
        across = block(2, tile)
        given(tile).wait()
        to = pl.ds(pl.multiple_of(tile * size, size), size)
        kept[:, to] = mine + landed[tile, :rows, :].astype(f32)
        passed[:, to] = (across + landed[tile, rows:, :].astype(f32)).astype(bf16)


def scattered_dot(lefts, weights, transposed, wide, ident):
    if lax.axis_size("mp") != 4:
        dot = dot_nt if transposed else dot_nn
        term = sum(dot(left, weight) for left, weight in zip(lefts, weights))
        return (term if wide else term.astype(bf16),)
    rows = lefts[0].shape[0] // 4
    model = weights[0].shape[0 if transposed else 1]
    size = 512
    tiles = model // size
    depth = sum(item.shape[1] for item in lefts)
    return pl.pallas_call(
        partial(scattered_kernel, transposed, len(lefts), size),
        in_specs=[IN_VMEM] * (2 * len(lefts)),
        out_specs=[IN_VMEM, IN_VMEM],
        out_shape=[
            jax.ShapeDtypeStruct((rows, model), f32),
            jax.ShapeDtypeStruct((rows, model), bf16),
        ],
        scratch_shapes=[
            pltpu.VMEM((tiles, 2 * rows, size), bf16),
            pltpu.VMEM((tiles, 2 * rows, size), bf16),
            pltpu.SemaphoreType.DMA((tiles,)),
            pltpu.SemaphoreType.DMA((tiles,)),
        ],
        compiler_params=pltpu.CompilerParams(
            collective_id=ident,
            has_side_effects=True,
            vmem_limit_bytes=ROOM if depth < 2048 else 2 * ROOM,
        ),
        cost_estimate=pl.CostEstimate(
            flops=8 * rows * model * depth,
            bytes_accessed=8 * rows * depth + 4 * model * depth + 14 * rows * model,
            transcendentals=0,
        ),
    )(*lefts, *weights)


def mlp_rows(norm, grad, gate_ref, up_ref, down_ref):
    curve = 0.7978845608028654
    gate = dot_nn(norm, gate_ref[...])
    up = dot_nn(norm, up_ref[...])
    d_hidden = dot_nt(grad, down_ref[...])
    square = gate * gate
    bend = jnp.tanh(curve * gate * (1.0 + 0.044715 * square))
    half = 0.5 * (1.0 + bend)
    value = gate * half
    slope = half + 0.5 * curve * gate * (1.0 - bend * bend) * (1.0 + 0.134145 * square)
    return (
        (value * up).astype(bf16),
        (d_hidden * up * slope).astype(bf16),
        (d_hidden * value).astype(bf16),
    )


def mlp_kernel(norm_ref, grad_ref, gate_ref, up_ref, down_ref, hidden_ref, d_gate_ref, d_up_ref):
    rows = norm_ref.shape[0]
    step = min(rows, 256)
    for start in range(0, rows, step):
        at = slice(start, start + step)
        hidden_ref[at, :], d_gate_ref[at, :], d_up_ref[at, :] = mlp_rows(
            norm_ref[at, :], grad_ref[at, :], gate_ref, up_ref, down_ref
        )


def gathered_mlp_kernel(tiles, *refs):
    norms, grads = refs[:3], refs[3:6]
    gate_ref, up_ref, down_ref = refs[6:9]
    full_norm, full_grad, hidden_ref, d_gate_ref, d_up_ref = refs[9:14]
    corner_norm, corner_grad, sems, local = refs[14:]
    tile = pl.program_id(0)
    rows = norms[0].shape[0]
    partner = other_core()
    norms = (*norms, corner_norm)
    grads = (*grads, corner_grad)

    def given(at):
        source, target = ((norms[2], corner_norm), (grads[2], corner_grad))[at]
        return to_partner(source, target, sems.at[2 * at], sems.at[2 * at + 1], partner)

    def keep(which, at):
        source, target = ((norms, full_norm), (grads, full_grad))[which]
        return pltpu.make_async_copy(
            source[at], target.at[pl.ds(at * rows, rows)], local.at[which, at]
        )

    @pl.when(tile == 0)
    def _():
        meet(partner)
        for which in range(2):
            given(which).start()
        for which in range(2):
            for at in range(3):
                keep(which, at).start()

    for at in range(4):
        if at == 3:

            @pl.when(tile == 0)
            def _():
                for which in range(2):
                    given(which).wait()
                    keep(which, 3).start()

        place = slice(at * rows, (at + 1) * rows)
        hidden_ref[place, :], d_gate_ref[place, :], d_up_ref[place, :] = mlp_rows(
            norms[at][...], grads[at][...], gate_ref, up_ref, down_ref
        )

    @pl.when(tile == tiles - 1)
    def _():
        for which in range(2):
            for at in range(4):
                keep(which, at).wait()


def gathered_mlp(own_norm, arrived_norm, own_grad, arrived_grad, w_gate, w_up, w_down, ident):
    model, units = w_gate.shape
    if lax.axis_size("mp") != 4:
        return (
            arrived_norm,
            arrived_grad,
            *mlp(arrived_norm, arrived_grad, w_gate, w_up, w_down),
        )
    rows = own_norm.shape[0]
    tile = 256
    whole = pl.BlockSpec((rows, model), lambda i: (0, 0))
    columns = pl.BlockSpec((model, tile), lambda i: (0, i))
    out = pl.BlockSpec((4 * rows, tile), lambda i: (0, i))
    full = pl.BlockSpec(memory_space=pl.ANY)
    shape = jax.ShapeDtypeStruct((4 * rows, units), bf16)
    full_shape = jax.ShapeDtypeStruct((4 * rows, model), bf16)
    return pl.pallas_call(
        partial(gathered_mlp_kernel, units // tile),
        grid=(units // tile,),
        in_specs=[whole] * 6 + [columns, columns, pl.BlockSpec((tile, model), lambda i: (i, 0))],
        out_specs=[full, full, out, out, out],
        out_shape=[full_shape, full_shape, shape, shape, shape],
        scratch_shapes=[
            pltpu.VMEM((rows, model), bf16),
            pltpu.VMEM((rows, model), bf16),
            pltpu.SemaphoreType.DMA((4,)),
            pltpu.SemaphoreType.DMA((2, 4)),
        ],
        compiler_params=pltpu.CompilerParams(
            collective_id=ident, has_side_effects=True, vmem_limit_bytes=VMEM_LIMIT
        ),
        cost_estimate=pl.CostEstimate(
            flops=24 * rows * model * units,
            bytes_accessed=28 * rows * model + 6 * model * units + 24 * rows * units,
            transcendentals=4 * rows * units,
        ),
    )(
        own_norm,
        arrived_norm[1],
        arrived_norm[0],
        own_grad,
        arrived_grad[1],
        arrived_grad[0],
        w_gate,
        w_up,
        w_down,
    )


def mlp(norm, grad, w_gate, w_up, w_down):
    rows, model = norm.shape
    units = w_gate.shape[1]
    tile = 256 if units % 256 == 0 else units
    whole = pl.BlockSpec((rows, model), lambda i: (0, 0))
    columns = pl.BlockSpec((model, tile), lambda i: (0, i))
    out = pl.BlockSpec((rows, tile), lambda i: (0, i))
    shape = jax.ShapeDtypeStruct((rows, units), bf16)
    return pl.pallas_call(
        mlp_kernel,
        grid=(units // tile,),
        in_specs=[whole, whole, columns, columns, pl.BlockSpec((tile, model), lambda i: (i, 0))],
        out_specs=[out, out, out],
        out_shape=[shape, shape, shape],
        compiler_params=params(),
        cost_estimate=pl.CostEstimate(
            flops=6 * rows * model * units,
            bytes_accessed=4 * rows * model + 6 * model * units + 6 * rows * units,
            transcendentals=rows * units,
        ),
    )(norm, grad, w_gate, w_up, w_down)


def flip(tensor, axis, bit):
    count = lax.axis_size(axis)
    return lax.ppermute(tensor, axis, [(i, i ^ bit) for i in range(count)])


def butterfly(tensor, axis):
    count = lax.axis_size(axis)
    if count & (count - 1):
        return lax.psum(tensor, axis)
    bit = 1
    while bit < count:
        tensor = tensor + flip(tensor, axis, bit)
        bit *= 2
    return tensor


def block_owners():
    blocks = jnp.arange(lax.axis_size("mp"), dtype=jnp.int32)
    return lax.axis_index("mp") ^ blocks if lax.axis_size("mp") == 4 else blocks


def fence(*values):
    return lax.optimization_barrier(values)


def gather_start(rows_local):
    if lax.axis_size("mp") != 4:
        return lax.all_gather(rows_local, "mp", axis=0, tiled=True)
    return flip(rows_local, "mp", 2), flip(rows_local, "mp", 1)


def scatter_move(sent):
    if lax.axis_size("mp") != 4:
        return None, lax.psum_scatter(sent[0], "mp", scatter_dimension=0, tiled=True)
    return sent[0], flip(sent[1], "mp", 2)


def scatter_end(arrived):
    if lax.axis_size("mp") != 4:
        return arrived[1].astype(f32)
    return arrived[0] + arrived[1].astype(f32)


CHUNK = 128
WIDE = 512
CYCLE = 4
LANDINGS = 7


class Late:
    def __init__(self, make):
        self.make = make

    def start(self):
        self.make().start()

    def wait(self):
        self.make().wait()

    def wait_send(self):
        self.make().wait_send()

    def wait_recv(self):
        self.make().wait_recv()


def sum_kernel(cycles, x_ref, out_ref, land, send_sem, recv_sem, local_sem):
    at = lax.axis_index("dp")
    y = lax.rem(at, 2)
    z = lax.div(at, 2)
    inner = (z == 1) | (z == 2)
    outer = (z == 0) | (z == 3)
    beside = z * 2 + (1 - y)
    along = at + jnp.where(lax.rem(z, 2) == 0, 2, -2)
    facing = (3 - z) * 2 + y
    side = z - 1

    barrier = pltpu.get_barrier_semaphore()

    def greet(target):
        pl.semaphore_signal(barrier, inc=1, device_id={"dp": target}, device_id_type=MESH)

    greet(beside)
    greet(along)

    @pl.when(inner)
    def _():
        greet(facing)
        pl.semaphore_wait(barrier, 3)

    @pl.when(outer)
    def _():
        pl.semaphore_wait(barrier, 2)

    def row(stream, cycle, index):
        start = ((stream * cycles + cycle) * CYCLE + index) * CHUNK
        return pl.ds(pl.multiple_of(start, CHUNK), CHUNK)

    def remote(stream, cycle, slot, source, target, device):
        return Late(
            lambda: pltpu.make_async_remote_copy(
                src_ref=source,
                dst_ref=target,
                send_sem=send_sem.at[stream, cycle, slot],
                recv_sem=recv_sem.at[stream, cycle, slot],
                device_id={"dp": device},
                device_id_type=MESH,
            )
        )

    def add(place, landing):
        @pl.loop(0, CHUNK // 32)
        def _(step):
            rows = pl.ds(pl.multiple_of(step * 32, 32), 32)
            x = x_ref.at[place]
            x[rows, :] = (x[rows, :].astype(f32) + landing[rows, :].astype(f32)).astype(bf16)

    def stages(stream, cycle):
        mine = row(stream, cycle, y)
        other = row(stream, cycle, 1 - y)
        low = row(stream, cycle, 2)
        high = row(stream, cycle, 3)
        own = row(stream, cycle, 2 + side)
        given = row(stream, cycle, 3 - side)
        landing = [land.at[stream, cycle, i] for i in range(LANDINGS)]

        def copy(slot, source, target, device):
            return remote(stream, cycle, slot, source, target, device)

        def keep(place, slot):
            return Late(
                lambda: pltpu.make_async_copy(
                    x_ref.at[place], out_ref.at[place], local_sem.at[stream, cycle, slot]
                )
            )

        def everyone(descriptor, after):
            def finish():
                descriptor.wait()
                after()

            return descriptor.start, finish

        def inward(descriptor, place, landed):
            def start():
                pl.when(outer)(descriptor.start)

            def finish():
                pl.when(outer)(descriptor.wait_send)

                @pl.when(inner)
                def _():
                    descriptor.wait_recv()
                    add(place, landed)

            return start, finish

        def between(descriptor, after, local=None):
            def start():
                @pl.when(inner)
                def _():
                    descriptor.start()
                    if local is not None:
                        local.start()

            def finish():
                @pl.when(inner)
                def _():
                    descriptor.wait()
                    if local is not None:
                        local.wait()
                    after()

            return start, finish

        def outward(descriptor, local=None):
            def start():
                @pl.when(inner)
                def _():
                    descriptor.start()
                    if local is not None:
                        local.start()

            def finish():
                @pl.when(inner)
                def _():
                    descriptor.wait_send()
                    if local is not None:
                        local.wait()

                pl.when(outer)(descriptor.wait_recv)

            return start, finish

        def nothing():
            return None

        x, out = x_ref, out_ref
        return [
            (0, inward(copy(0, x.at[low], landing[0], along), low, landing[0])),
            (1, inward(copy(1, x.at[high], landing[1], along), high, landing[1])),
            (2, between(copy(2, x.at[given], landing[2], facing), lambda: add(own, landing[2]))),
            (3, between(copy(3, x.at[own], landing[3], beside), lambda: add(own, landing[3]))),
            (4, between(copy(4, x.at[own], out.at[own], facing), nothing, keep(own, 0))),
            (5, outward(copy(5, out.at[low], out.at[low], along))),
            (6, outward(copy(6, out.at[high], out.at[high], along))),
            (1, everyone(copy(7, x.at[other], landing[4], beside), lambda: add(mine, landing[4]))),
            (2, inward(copy(8, x.at[mine], landing[5], along), mine, landing[5])),
            (3, between(copy(9, x.at[mine], landing[6], facing), lambda: add(mine, landing[6]))),
            (4, outward(copy(10, x.at[mine], out.at[mine], along), keep(mine, 1))),
            (5, everyone(copy(11, out.at[mine], out.at[mine], beside), nothing)),
        ]

    def body(step, carry):
        for phase in range(3):
            for stream in range(2):

                def each(back, offset, what):
                    cycle = step - back

                    @pl.when((cycle >= 0) & (cycle < cycles))
                    def _():
                        for when, (start, finish) in stages(stream, cycle):
                            if when == offset:
                                (start if what == 0 else finish)()

                for offset in range(7):
                    if (offset + 1) % 3 == phase:
                        each((offset + 1) // 3, offset, 1)
                for offset in range(7):
                    if offset % 3 == phase:
                        each(offset // 3, offset, 0)
        return carry

    lax.fori_loop(0, cycles + 3, body, 0)


def sum_chunks(stack):
    cycles = stack.shape[0] // (CHUNK * CYCLE * 2)
    size = stack.shape[0] * WIDE * 2
    return pl.pallas_call(
        partial(sum_kernel, cycles),
        in_specs=[pl.BlockSpec(memory_space=pltpu.VMEM)],
        out_specs=pl.BlockSpec(memory_space=pl.ANY),
        out_shape=jax.ShapeDtypeStruct(stack.shape, bf16),
        scratch_shapes=[
            pltpu.VMEM((2, cycles, LANDINGS, CHUNK, WIDE), bf16),
            pltpu.SemaphoreType.DMA((2, cycles, 12)),
            pltpu.SemaphoreType.DMA((2, cycles, 12)),
            pltpu.SemaphoreType.DMA((2, cycles, 2)),
        ],
        compiler_params=pltpu.CompilerParams(
            collective_id=0, has_side_effects=True, vmem_limit_bytes=63 * 1024 * 1024
        ),
        cost_estimate=pl.CostEstimate(
            flops=size, bytes_accessed=4 * size, transcendentals=0
        ),
    )(stack)


def to_chunks(tensor):
    height, width = tensor.shape
    return [tensor[:, at : at + WIDE] for at in range(0, width, WIDE)]


def chunked(tensors):
    size = sum(item.size for item in tensors)
    fits = size % (CHUNK * WIDE * CYCLE * 2) == 0 and all(
        item.shape[0] % CHUNK == 0 and item.shape[1] % WIDE == 0 for item in tensors
    )
    return lax.axis_size("dp") == 8 and fits


def sum_dp_start(tensors):
    low = [item.astype(bf16) for item in tensors]
    if not chunked(low):
        return lax.psum(low, "dp")
    return sum_chunks(jnp.concatenate([piece for item in low for piece in to_chunks(item)], axis=0))


def sum_dp_end(total, tensors):
    if not chunked(tensors):
        return [item.astype(f32) for item in total]
    out, at = [], 0
    for item in tensors:
        height, width = item.shape
        pieces = []
        for _ in range(width // WIDE):
            pieces.append(total[at : at + height])
            at += height
        out.append(jnp.concatenate(pieces, axis=1).astype(f32))
    return out


def on_device(
    tokens,
    patches,
    text_lengths,
    prefix_lengths,
    group_map,
    ratio,
    cotangent,
    q_self,
    k_self,
    v_self,
    o_self,
    q_cross,
    k_cross,
    v_cross,
    o_cross,
    w_gate,
    w_up,
    w_down,
    gain_attn,
    gain_cross,
    gain_mlp,
):
    local_rows = tokens.shape[0]
    examples = text_lengths.shape[0]
    patch = patches.shape[0] // examples
    local_examples = local_rows // SEQ
    batches = 2 if local_examples % 2 == 0 else 1
    each = local_examples // batches
    rows = each * SEQ
    width = q_self.shape[1]

    lens_f = text_lengths.astype(f32)
    robot = (group_map == 0).astype(f32)
    web = 1.0 - robot
    local_counts = jnp.stack([jnp.sum(lens_f * robot), jnp.sum(lens_f * web)])
    counts = butterfly(jnp.broadcast_to(local_counts[:, None], (2, 128)), "dp")[:, 0]
    ratio_f = ratio.astype(f32)
    share = ratio_f / jnp.sum(ratio_f)
    group_scale = share * jnp.sum(counts) / jnp.maximum(counts, 1.0)
    example_scale = robot * group_scale[0] + web * group_scale[1]
    mine = lax.axis_index("mp") * local_examples
    own_scale = lax.dynamic_slice_in_dim(example_scale, mine, local_examples, 0)
    own_length = lax.dynamic_slice_in_dim(text_lengths, mine, local_examples, 0)
    place = jnp.arange(SEQ, dtype=jnp.int32)
    live = (place[None, :] < own_length[:, None]).astype(f32)
    row_weight = (own_scale[:, None] * live).reshape(local_rows)

    owners = block_owners()
    which, lengths, prefixes = [], [], []
    for b in range(batches):
        ids = (
            owners[:, None] * local_examples + b * each + jnp.arange(each, dtype=jnp.int32)[None, :]
        ).reshape(-1).astype(jnp.int32)
        which.append(ids)
        lengths.append(jnp.take(text_lengths, ids))
        prefixes.append(jnp.take(prefix_lengths, ids))

    w_qkv = jnp.concatenate([q_self, k_self, v_self], axis=1)

    each_batch = range(batches)
    last = batches - 1

    def part(tensor, b):
        return tensor[b * rows : (b + 1) * rows]

    def product(left, right, dot):
        return lambda low, high: dot(left[low:high], right)

    outer = [part(cotangent, b).astype(f32) * part(row_weight, b)[:, None] for b in each_batch]
    outer_low = [item.astype(bf16) for item in outer]
    x_zero = [part(tokens, b).astype(f32) for b in each_batch]
    norm_one = [normalize(x_zero[b], gain_attn) for b in each_batch]
    scale_one = [item[1] for item in norm_one]
    norm_one = [item[0] for item in norm_one]

    none = [None] * batches
    full_one, qkv, mixed_self, x_one, norm_two, scale_two = ([None] * batches for _ in range(6))
    full_two, query, mixed_cross, x_two, norm_three, scale_three = (
        [None] * batches for _ in range(6)
    )
    full_three, grad_three, hidden, d_gate, d_up, back_three = ([None] * batches for _ in range(6))
    grad_two_rows, grad_two, d_query, grad_one_rows, grad_one, d_qkv = (
        [None] * batches for _ in range(6)
    )
    gain_mlp_parts, gain_cross_parts, gain_attn_parts, grad_input, output = (
        [None] * batches for _ in range(5)
    )

    def self_block(b, arrived):
        full_one[b], qkv[b] = gathered_dot(norm_one[b], arrived, w_qkv, False, 1)
        mixed_self[b] = self_forward(qkv[b], lengths[b], prefixes[b])
        return scattered_dot([mixed_self[b]], [o_self], False, True, 2)

    def self_norm(b, arrived):
        x_one[b] = x_zero[b] + scatter_end(arrived)
        norm_two[b], scale_two[b] = normalize(x_one[b], gain_cross)

    def cross_block(b, arrived, keys, values):
        full_two[b], query[b] = gathered_dot(norm_two[b], arrived, q_cross, False, 3)
        mixed_cross[b] = cross_forward(query[b], keys, values, which[b], patch)
        return scattered_dot([mixed_cross[b]], [o_cross], False, True, 4)

    def cross_norm(b, arrived):
        x_two[b] = x_one[b] + scatter_end(arrived)
        norm_three[b], scale_three[b] = normalize(x_two[b], gain_mlp)

    def mlp_block(b, arrived_norm, arrived_grad):
        full_three[b], grad_three[b], hidden[b], d_gate[b], d_up[b] = gathered_mlp(
            norm_three[b], arrived_norm, outer_low[b], arrived_grad, w_gate, w_up, w_down, 5
        )

    def mlp_back(b):
        return scattered_dot([d_gate[b], d_up[b]], [w_gate, w_up], True, False, 6)

    def mlp_norm_back(b, arrived):
        back, gain_mlp_parts[b] = norm_back(
            x_two[b], scale_three[b], gain_mlp, scatter_end(arrived)
        )
        grad_two_rows[b] = outer[b] + back
        return grad_two_rows[b].astype(bf16)

    def cross_back(b, own, arrived, keys, values, earlier):
        grad_two[b], d_mixed = gathered_dot(own, arrived, o_cross, True, 7)
        d_query[b], *d_kv = cross_backward(
            query[b], keys, values, d_mixed, which[b], patch, earlier
        )
        return scattered_dot([d_query[b]], [q_cross], True, False, 8), d_kv

    def cross_norm_back(b, arrived):
        back, gain_cross_parts[b] = norm_back(
            x_one[b], scale_two[b], gain_cross, scatter_end(arrived)
        )
        grad_one_rows[b] = grad_two_rows[b] + back
        return grad_one_rows[b].astype(bf16)

    def self_back(b, own, arrived):
        grad_one[b], d_mixed = gathered_dot(own, arrived, o_self, True, 9)
        d_qkv[b] = self_backward(qkv[b], d_mixed, lengths[b], prefixes[b])
        return scattered_dot([d_qkv[b]], [w_qkv], True, False, 10)

    def self_norm_back(b, arrived):
        back, gain_attn_parts[b] = norm_back(
            x_zero[b], scale_one[b], gain_attn, scatter_end(arrived)
        )
        grad_input[b] = grad_one_rows[b] + back

    def project_out(b):
        return scattered_dot([hidden[b]], [w_down], False, True, 11)

    def weight_grad(left, right):
        return sum(dot_tn(left[b], right[b]) for b in each_batch)

    def move_self(b, sent):
        return scatter_move(sent, product(mixed_self[b], o_self, dot_nn), rows)

    def move_cross(b, sent):
        return scatter_move(sent, product(mixed_cross[b], o_cross, dot_nn), rows)

    def mlp_product(b):
        return lambda low, high: (
            dot_nt(d_gate[b][low:high], w_gate) + dot_nt(d_up[b][low:high], w_up)
        )

    def move_mlp(b, sent):
        return scatter_move(sent, mlp_product(b), rows)

    def move_cross_back(b, sent):
        return scatter_move(sent, product(d_query[b], q_cross, dot_nt), rows)

    def move_self_back(b, sent):
        return scatter_move(sent, product(d_qkv[b], w_qkv, dot_nt), rows)

    def move_out(b, sent):
        return scatter_move(sent, product(hidden[b], w_down, dot_nn), rows)

    sent = list(none)
    got = list(none)
    back = list(none)
    grads = list(none)
    own = list(none)
    shown = list(none)
    if batches == 2:
        got[0] = gather_start(norm_one[0])
        got[0], norm_one[1], w_qkv, outer_low, outer, which, lengths, prefixes = fence(
            got[0], norm_one[1], w_qkv, outer_low, outer, which, lengths, prefixes
        )
        got[1] = gather_start(norm_one[1])
        sent[0] = self_block(0, got[0])
        sent[0], got[1], outer_low = fence(sent[0], got[1], outer_low)
        grads[0] = gather_start(outer_low[0])
        sent[1] = self_block(1, got[1])
        sent, grads[0], k_cross = fence(sent, grads[0], k_cross)
        back[0] = scatter_move(sent[0])
        keys = dot_nn(patches, k_cross).astype(bf16)
        back[0], sent[1], keys, v_cross = fence(back[0], sent[1], keys, v_cross)
        back[1] = scatter_move(sent[1])
        self_norm(0, back[0])
        values = dot_nn(patches, v_cross).astype(bf16)
        norm_two[0], back[1], values = fence(norm_two[0], back[1], values)
        got[0] = gather_start(norm_two[0])
        self_norm(1, back[1])
        norm_two[1], got[0], outer_low = fence(norm_two[1], got[0], outer_low)
        got[1] = gather_start(norm_two[1])
        sent[0] = cross_block(0, got[0], keys, values)
        sent[0], got[1] = fence(sent[0], got[1])
        back[0] = scatter_move(sent[0])
        sent[1] = cross_block(1, got[1], keys, values)
        sent[1], back[0] = fence(sent[1], back[0])
        back[1] = scatter_move(sent[1])
        cross_norm(0, back[0])
        norm_three[0], back[1], outer_low = fence(norm_three[0], back[1], outer_low)
        got[0] = gather_start(norm_three[0])
        cross_norm(1, back[1])
        got[0], outer_low, norm_three[1] = fence(got[0], outer_low, norm_three[1])
        got[1] = gather_start(norm_three[1])
        mlp_block(0, got[0], grads[0])
        got[1], d_gate[0], d_up[0], outer_low[1] = fence(
            got[1], d_gate[0], d_up[0], outer_low[1]
        )
        grads[1] = gather_start(outer_low[1])
        sent[0] = mlp_back(0)
        grads[1], got[1], sent[0] = fence(grads[1], got[1], sent[0])
        back[0] = scatter_move(sent[0])
        mlp_block(1, got[1], grads[1])
        back[0], d_gate[1], d_up[1], hidden = fence(back[0], d_gate[1], d_up[1], hidden)
        own[0] = mlp_norm_back(0, back[0])
        got[0] = gather_start(own[0])
        sent[1] = mlp_back(1)
        d_wdown = weight_grad(hidden, grad_three)
        own[0], got[0], sent[1], d_gate, d_up, d_wdown = fence(
            own[0], got[0], sent[1], d_gate, d_up, d_wdown
        )
        back[1] = scatter_move(sent[1])
        d_wgate = weight_grad(full_three, d_gate)
        d_wup = weight_grad(full_three, d_up)
        back[1], d_wgate, d_wup, d_wdown = fence(back[1], d_wgate, d_wup, d_wdown)
        d_mlp = lax.psum([item.astype(bf16) for item in (d_wdown, d_wgate, d_wup)], "dp")
        own[1] = mlp_norm_back(1, back[1])
        got[1] = gather_start(own[1])
        sent[0], d_kv = cross_back(0, own[0], got[0], keys, values, ())
        own[1], got[1], sent[0], d_kv = fence(own[1], got[1], sent[0], d_kv)
        back[0] = scatter_move(sent[0])
        sent[1], d_kv = cross_back(1, own[1], got[1], keys, values, d_kv)
        sent[1], back[0], d_kv, mixed_cross, hidden = fence(
            sent[1], back[0], d_kv, mixed_cross, hidden
        )
        back[1] = scatter_move(sent[1])
        own[0] = cross_norm_back(0, back[0])
        d_ocross = weight_grad(mixed_cross, grad_two)
        d_qcross = weight_grad(full_two, d_query)
        shown[0] = project_out(0)
        own[0], back[1], d_kv, d_ocross, d_qcross, shown[0] = fence(
            own[0], back[1], d_kv, d_ocross, d_qcross, shown[0]
        )
        got[0] = gather_start(own[0])
        own[1] = cross_norm_back(1, back[1])
        d_kcross = dot_tn(patches, d_kv[0])
        d_vcross = dot_tn(patches, d_kv[1])
        got[0], own[1], d_kcross, d_vcross, hidden = fence(
            got[0], own[1], d_kcross, d_vcross, hidden
        )
        got[1] = gather_start(own[1])
        sent[0] = self_back(0, own[0], got[0])
        got[1], sent[0] = fence(got[1], sent[0])
        back[0] = scatter_move(sent[0])
        sent[1] = self_back(1, own[1], got[1])
        back[0], sent[1], mixed_self, hidden = fence(back[0], sent[1], mixed_self, hidden)
        back[1] = scatter_move(sent[1])
        self_norm_back(0, back[0])
        d_oself = weight_grad(mixed_self, grad_one)
        d_wqkv = weight_grad(full_one, d_qkv)
        shown[1] = project_out(1)
        back[1], grad_input[0], d_wqkv, d_oself, shown = fence(
            back[1], grad_input[0], d_wqkv, d_oself, shown
        )
        self_norm_back(1, back[1])
    else:
        sent[0] = self_block(0, gather_start(norm_one[0]))
        self_norm(0, scatter_move(sent[0]))
        keys = dot_nn(patches, k_cross).astype(bf16)
        values = dot_nn(patches, v_cross).astype(bf16)
        sent[0] = cross_block(0, gather_start(norm_two[0]), keys, values)
        cross_norm(0, scatter_move(sent[0]))
        mlp_block(0, gather_start(norm_three[0]), gather_start(outer_low[0]))
        own[0] = mlp_norm_back(0, scatter_move(mlp_back(0)))
        sent[0], d_kv = cross_back(0, own[0], gather_start(own[0]), keys, values, ())
        own[0] = cross_norm_back(0, scatter_move(sent[0]))
        sent[0] = self_back(0, own[0], gather_start(own[0]))
        self_norm_back(0, scatter_move(sent[0]))
        d_wdown = weight_grad(hidden, grad_three)
        d_wgate = weight_grad(full_three, d_gate)
        d_wup = weight_grad(full_three, d_up)
        d_kcross = dot_tn(patches, d_kv[0])
        d_vcross = dot_tn(patches, d_kv[1])
        d_wqkv = weight_grad(full_one, d_qkv)
        d_qcross = weight_grad(full_two, d_query)
        d_oself = weight_grad(mixed_self, grad_one)
        d_ocross = weight_grad(mixed_cross, grad_two)
        d_mlp = lax.psum([item.astype(bf16) for item in (d_wdown, d_wgate, d_wup)], "dp")
        shown = [project_out(0)]
    back = [scatter_move(shown[b]) for b in each_batch]
    gains = jnp.stack(
        [sum(parts) for parts in (gain_attn_parts, gain_cross_parts, gain_mlp_parts)]
    )
    summed = sum_dp_start([d_ocross, d_qcross, d_kcross, d_vcross, d_oself, d_wqkv])
    summed, d_mlp, back, gains = fence(summed, d_mlp, back, gains)
    gains = butterfly(butterfly(gains, "mp"), "dp")
    d_ocross, d_qcross, d_kcross, d_vcross, d_oself, d_wqkv = sum_dp_end(
        summed, [d_ocross, d_qcross, d_kcross, d_vcross, d_oself, d_wqkv]
    )
    output = jnp.concatenate(
        [(x_two[b] + scatter_end(back[b])).astype(bf16) for b in each_batch], axis=0
    )
    grad_input = jnp.concatenate(grad_input, axis=0)
    d_wdown, d_wgate, d_wup = [item.astype(f32) for item in d_mlp]
    return (
        output,
        grad_input,
        d_wqkv[:, :width],
        d_wqkv[:, width : 2 * width],
        d_wqkv[:, 2 * width :],
        d_oself,
        d_qcross,
        d_kcross,
        d_vcross,
        d_ocross,
        d_wgate,
        d_wup,
        d_wdown,
        gains[0],
        gains[1],
        gains[2],
    )


def solution(mesh):
    by_rows = P(("dp", "mp"), None)
    columns = P(None, "mp")
    rows = P("mp", None)
    weights = (columns, columns, columns, rows, columns, columns, columns, rows, columns, columns, rows)
    in_specs = (
        (by_rows, P("dp", None), P("dp"), P("dp"), P("dp"), P(), by_rows) + weights + (P(), P(), P())
    )
    out_specs = (by_rows, by_rows) + weights + (P(), P(), P())
    return jax.shard_map(
        on_device, mesh=mesh, in_specs=in_specs, out_specs=out_specs, check_vma=False
    )
```

time: 1890 us -> 1310 us (0.69)
  waiting for transfers between devices: 816 us -> 111 us
  Pallas kernels: 174 us -> 837 us
  matrix products: 349 us -> 142 us
  starting transfers between devices: 241 us -> 38.3 us
  other arithmetic: 208 us -> 91.3 us
    pallas_call x2 -> x23, Pallas kernels: 48.9 us -> 730 us  [the longest x1 523 us: sum_chunks(): pl.pallas_call(partial(sum_kernel, cycles), in_specs=[pl.BlockSpec(memory...]
    ppermute x40 -> x0, waiting for transfers between devices: 440 us -> none  [send(): return lax.ppermute(tensor, 'dp', which)]
    ppermute x68 -> x44, waiting for transfers between devices: 376 us -> 111 us  [flip(): return lax.ppermute(tensor, axis, [(i, i ^ bit) for i in range(count)])]
    ppermute x40 -> x0, starting transfers between devices: 175 us -> none  [send(): return lax.ppermute(tensor, 'dp', which)]
    dot_general x20 -> x0, matrix products: 115 us -> none  [dot_nt(): lax.dot_general(left, right, (((1,), (1,)), ((), ())), preferred_element_...]
    dot_general x17 -> x2, matrix products: 103 us -> 25.1 us  [dot_nn(): return jnp.dot(left, right, preferred_element_type=f32)]
    convert_element_type x35 -> x13, other arithmetic: 126 us -> 49.3 us  [the longest x4 19.5 us: sum_dp_end(): out.append(jnp.concatenate(pieces, axis=1).astype(f32))]
    unnamed x335 -> x317, local copies, waits for them, and re-layouts: 20.6 us -> 48.9 us
  transfers between devices with their start and end apart: 108 -> 45, of which waited for: 37 -> 14; matrix products, arithmetic and copies ran while one was open for 32% -> 18% of each run, Pallas kernels for 8% -> 64%
where the time goes in v2:
time: 1310 us; the launch traced here: 1300 us
  Pallas kernels  837 us (64%)
  matrix products  142 us (11%)
  waiting for transfers between devices  111 us (8%)
  other arithmetic  91.3 us (7%)
  local copies, waits for them, and re-layouts  66.9 us (5%)
  starting transfers between devices  38.3 us (3%)
  between operations  16.4 us (1%)
    pallas_call x1, Pallas kernels, sum_chunks(): pl.pallas_call(partial(sum_kernel, cycles), in_specs=[pl.BlockSpec(memory...  523 us
    dot_general x16, matrix products, dot_tn(): lax.dot_general(left, right, (((0,), (0,)), ((), ())), preferred_element_...  117 us
    ppermute x44, waiting for transfers between devices, flip(): return lax.ppermute(tensor, axis, [(i, i ^ bit) for i in range(count)])  111 us
    pallas_call x12, Pallas kernels, scattered_dot(): pl.pallas_call(partial(scattered_kernel, transposed, len(lefts), size), i...  105 us
    pallas_call x2, Pallas kernels, gathered_mlp(): pl.pallas_call(partial(gathered_mlp_kernel, units // tile), grid=(units /...  57.6 us
    unnamed x317, local copies, waits for them, and re-layouts  48.9 us
    pallas_call x8, Pallas kernels, gathered_dot(): pl.pallas_call(partial(gathered_kernel, transposed, 512), in_specs=[IN_VM...  44.2 us
    pallas_call x2, Pallas kernels, cross_backward(): pl.pallas_call(cross_backward_kernel, grid_spec=pltpu.PrefetchScalarGridS...  39.2 us
  transfers between devices with their start and end apart: 45, of which 14 were waited for; matrix products, arithmetic and copies ran while one was open for 18% of the time, Pallas kernels for 64%

profile of v2, /device:TPU:0, one launch (start us, length us, event | category | flops | bytes accessed | tf_op | source)
XLA Modules:
  0.0 1303.6 jit_solution(9842030398048505679)
XLA Ops:
  45.3 10.0 shard_map.324
  96.9 12.4 fusion.key_ref
  109.4 10.8 collective-permute-done.9
  121.3 12.6 fusion.1.value_ref
  146.2 21.1 %collective-permute-done.11.across = bf16[256,2048]{1,0:T(8,128)(2,1)S(1)} collective-permute-done((bf16[256,2048]{1,0:T(8,128)(2,1)S(1)}, bf16[256,2048]{1,0:T(8,128)(2,1)S(1)}, u32[]{:S(2)}, u32[]{:S(2)}) %collective-permute-start.11) | collective-permute-done | bytes 1048608 | tf_op jit(solution)/shard_map/ppermute | solution.py:567
  172.7 9.6 shard_map.331.refs_0_
  215.3 21.2 %collective-permute-done.16 = bf16[256,2048]{1,0:T(8,128)(2,1)S(1)} collective-permute-done((bf16[256,2048]{1,0:T(8,128)(2,1)S(1)}, bf16[256,2048]{1,0:T(8,128)(2,1)S(1)}, u32[]{:S(2)}, u32[]{:S(2)}) %collective-permute-start.16) | collective-permute-done | bytes 1048608 | tf_op jit(solution)/shard_map/ppermute | solution.py:567
  240.5 19.0 %collective-permute-done.17.refs_2_ = bf16[256,2048]{1,0:T(8,128)(2,1)S(1)} collective-permute-done((bf16[256,2048]{1,0:T(8,128)(2,1)S(1)}, bf16[256,2048]{1,0:T(8,128)(2,1)S(1)}, u32[]{:S(2)}, u32[]{:S(2)}) %collective-permute-start.17) | collective-permute-done | bytes 1048608 | tf_op jit(solution)/shard_map/ppermute | solution.py:567
  262.6 28.8 %shard_map.336 = (bf16[1024,2048]{1,0:T(8,128)(2,1)}, bf16[1024,2048]{1,0:T(8,128)(2,1)}, bf16[1024,1280]{1,0:T(8,128)(2,1)}, bf16[1024,1280]{1,0:T(8,128)(2,1)}, bf16[1024,1280]{1,0:T(8,128)(2,1)}) custom-call(bf16[256,2048]{1,0:T(8,128)(2,1)} %copy-done.100, bf16[256,2048]{1,0:T(8,128)(2,1)} %copy-done.128, bf16[256,2048]{1,0:T(8,128)(2,1)} %copy-done.127, ...), custom_call_target="tpu_custom_call" | custom-call | flops 16106127360 | bytes 38273024 | tf_op jit(solution)/shard_map/pallas_call | solution.py:509
  294.5 17.8 %shard_map.337 = (f32[256,2048]{1,0:T(8,128)S(1)}, bf16[256,2048]{1,0:T(8,128)(2,1)S(1)}) custom-call(bf16[1024,1280]{1,0:T(8,128)(2,1)S(1)} %copy-done.69, bf16[1024,1280]{1,0:T(8,128)(2,1)} %get-tuple-element.333.refs_1_, bf16[2048,1280]{1,0:T(8,128)(2,1)} %refs_2_.3, bf16[2048,1280]{1,0:T(8,128)(2,1)} %refs_3_.3), custom_call_target="tpu_custom_call" | custom-call | flops 10737418240 | bytes 33554432 | tf_op jit(solution)/shard_map/pallas_call | solution.py:388
  318.7 28.8 %shard_map.338 = (bf16[1024,2048]{1,0:T(8,128)(2,1)}, bf16[1024,2048]{1,0:T(8,128)(2,1)}, bf16[1024,1280]{1,0:T(8,128)(2,1)}, bf16[1024,1280]{1,0:T(8,128)(2,1)}, bf16[1024,1280]{1,0:T(8,128)(2,1)}) custom-call(bf16[256,2048]{1,0:T(8,128)(2,1)} %copy-done.99, bf16[256,2048]{1,0:T(8,128)(2,1)} %copy-done.126, bf16[256,2048]{1,0:T(8,128)(2,1)} %copy-done.125, ...), custom_call_target="tpu_custom_call" | custom-call | flops 16106127360 | bytes 38273024 | tf_op jit(solution)/shard_map/pallas_call | solution.py:509
  366.5 19.4 %shard_map.339 = (f32[256,2048]{1,0:T(8,128)S(1)}, bf16[256,2048]{1,0:T(8,128)(2,1)}) custom-call(bf16[1024,1280]{1,0:T(8,128)(2,1)S(1)} %copy-done.71, bf16[1024,1280]{1,0:T(8,128)(2,1)} %get-tuple-element.334.refs_1_, bf16[2048,1280]{1,0:T(8,128)(2,1)} %refs_2_.3, bf16[2048,1280]{1,0:T(8,128)(2,1)} %refs_3_.3), custom_call_target="tpu_custom_call" | custom-call | flops 10737418240 | bytes 33554432 | tf_op jit(solution)/shard_map/pallas_call | solution.py:388
  401.8 10.2 convolution_add_fusion.1
  418.6 10.1 convolution_add_fusion
  437.0 19.6 %shard_map.341 = (bf16[1024,512]{1,0:T(8,128)(2,1)S(1)}, bf16[4096,512]{1,0:T(8,128)(2,1)S(1)}, bf16[4096,512]{1,0:T(8,128)(2,1)S(1)}) custom-call(s32[8]{0:T(128)S(1)} %add.290.which_ref, bf16[1024,512]{1,0:T(8,128)(2,1)S(1)} %get-tuple-element.266.query_ref, bf16[4096,512]{1,0:T(8,128)(2,1)S(1)} %copy-done.3, bf16[4096,512]{1,0:T(8,128)(2,1)S(1)} %copy-done.6, ...), custom_call_target="tpu_custom_call" | custom-call | flops 2684354560 | bytes 12582912 | tf_op jit(solution)/shard_map/pallas_call | solution.py:230
  483.9 19.6 %shard_map.344 = (bf16[1024,512]{1,0:T(8,128)(2,1)S(1)}, bf16[4096,512]{1,0:T(8,128)(2,1)S(1)}, bf16[4096,512]{1,0:T(8,128)(2,1)S(1)}) custom-call(s32[8]{0:T(128)S(1)} %add.295.which_ref, bf16[1024,512]{1,0:T(8,128)(2,1)S(1)} %copy-done.33, bf16[4096,512]{1,0:T(8,128)(2,1)S(1)} %copy-done.4, ...), custom_call_target="tpu_custom_call", output_to_operand_aliasing={{1}: (5, {}), {2}: (6, {})} | custom-call | flops 2684354560 | bytes 12582912 | tf_op jit(solution)/shard_map/pallas_call | solution.py:230
  544.4 13.7 %convolution_bitcast_fusion.1 = bf16[2048,512]{1,0:T(8,128)(2,1)} fusion(bf16[4096,512]{1,0:T(8,128)(2,1)S(1)} %copy-done.23, bf16[4096,2048]{1,0:T(8,128)(2,1)} %param.24), kind=kOutput, calls=%fused_computation.28 | convolution fusion | flops 8589934592 | bytes 23068672 | tf_op jit(solution)/shard_map/dot_general | solution.py:25
  558.1 14.1 %convolution_bitcast_fusion = bf16[2048,512]{1,0:T(8,128)(2,1)} fusion(bf16[4096,512]{1,0:T(8,128)(2,1)S(1)} %copy-done.27, bf16[4096,2048]{1,0:T(8,128)(2,1)} %param.24), kind=kOutput, calls=%fused_computation.27 | convolution fusion | flops 8589934592 | bytes 23068672 | tf_op jit(solution)/shard_map/dot_general | solution.py:25
  587.1 17.0 %shard_map.348.refs_0_ = bf16[1024,1536]{1,0:T(8,128)(2,1)S(1)} custom-call(s32[8]{0:T(128)S(1)} %copy-done.49, s32[8]{0:T(128)S(1)} %copy-done.47, bf16[1024,1536]{1,0:T(8,128)(2,1)S(1)} %copy-done.11, bf16[1024,512]{1,0:T(8,128)(2,1)S(1)} %get-tuple-element.388.grad_ref), custom_call_target="tpu_custom_call" | custom-call | flops 1342177280 | bytes 7340032 | tf_op jit(solution)/shard_map/pallas_call | solution.py:188
  619.6 17.0 %shard_map.351.refs_0_ = bf16[1024,1536]{1,0:T(8,128)(2,1)S(1)} custom-call(s32[8]{0:T(128)S(1)} %copy-done.45, s32[8]{0:T(128)S(1)} %copy-done.43, bf16[1024,1536]{1,0:T(8,128)(2,1)S(1)} %copy-done.9, bf16[1024,512]{1,0:T(8,128)(2,1)S(1)} %get-tuple-element.395.grad_ref), custom_call_target="tpu_custom_call" | custom-call | flops 1342177280 | bytes 7340032 | tf_op jit(solution)/shard_map/pallas_call | solution.py:188
  636.6 9.6 fusion.37
  646.2 12.9 convolution_add_fusion.3
  706.5 523.1 %shard_map.354 = bf16[16384,512]{1,0:T(8,128)(2,1)} custom-call(bf16[16384,512]{1,0:T(8,128)(2,1)} %slice_dynamic-update-slice_fusion.x_ref), custom_call_target="tpu_custom_call" | custom-call | flops 16777216 | bytes 67108864 | tf_op jit(solution)/shard_map/pallas_call | solution.py:805
  1250.1 9.9 fusion.29
  (528 shorter events, 398.8 us)
Async XLA Ops:
  7.2 1228.5 %all-reduce.3.cloned.1.call-start = ((), (), s32[]{:S(2)}) async-start(), calls=%async_computation | async-start | bytes 31457280 | tf_op jit(solution)/shard_map/psum | solution.py:1096
  10.6 34.0 %collective-permute-start = (bf16[256,2048]{1,0:T(8,128)(2,1)S(1)}, bf16[256,2048]{1,0:T(8,128)(2,1)}, u32[]{:S(2)}, u32[]{:S(2)}) collective-permute-start(bf16[256,2048]{1,0:T(8,128)(2,1)S(1)} %get-tuple-element.488.own), channel_id=1, source_target_pairs={{0,2},{1,3},{2,0},{3,1},{4,6},{5,7},{6,4},{7,5},{8,10},{9,11},{10,... | collective-permute-start | bytes 3145736 | tf_op jit(solution)/shard_map/ppermute | solution.py:567
  13.6 31.0 %collective-permute-start.1 = (bf16[256,2048]{1,0:T(8,128)(2,1)S(1)}, bf16[256,2048]{1,0:T(8,128)(2,1)}, u32[]{:S(2)}, u32[]{:S(2)}) collective-permute-start(bf16[256,2048]{1,0:T(8,128)(2,1)S(1)} %get-tuple-element.488.own), channel_id=1, source_target_pairs={{0,1},{1,0},{2,3},{3,2},{4,5},{5,4},{6,7},{7,6},{8,9},{9,8},{10,11... | collective-permute-start | bytes 3145736 | tf_op jit(solution)/shard_map/ppermute | solution.py:567
  44.7 25.4 %collective-permute-start.5 = (bf16[256,2048]{1,0:T(8,128)(2,1)S(1)}, bf16[256,2048]{1,0:T(8,128)(2,1)S(1)}, u32[]{:S(2)}, u32[]{:S(2)}) collective-permute-start(bf16[256,2048]{1,0:T(8,128)(2,1)S(1)} %get-tuple-element.234.own), channel_id=1, source_target_pairs={{0,2},{1,3},{2,0},{3,1},{4,6},{5,7},{6,4},{7,5},{8,10},{9,11},{10,... | collective-permute-start | bytes 3145736 | tf_op jit(solution)/shard_map/ppermute | solution.py:567
  70.1 25.3 %collective-permute-start.7 = (bf16[256,2048]{1,0:T(8,128)(2,1)S(1)}, bf16[256,2048]{1,0:T(8,128)(2,1)S(1)}, u32[]{:S(2)}, u32[]{:S(2)}) collective-permute-start(bf16[256,2048]{1,0:T(8,128)(2,1)S(1)} %get-tuple-element.293.refs_3_), channel_id=1, source_target_pairs={{0,2},{1,3},{2,0},{3,1},{4,6},{5,7},{6,4},{7,5},{8,10},{9,11},{10,... | collective-permute-start | bytes 3145736 | tf_op jit(solution)/shard_map/ppermute | solution.py:567
  260.8 30.5 %collective-permute-start.19 = (bf16[256,2048]{1,0:T(8,128)(2,1)S(1)}, bf16[256,2048]{1,0:T(8,128)(2,1)S(1)}, u32[]{:S(2)}, u32[]{:S(2)}) collective-permute-start(bf16[256,2048]{1,0:T(8,128)(2,1)S(1)} %multiply_convert_fusion.refs_0_), channel_id=1, source_target_pairs={{0,2},{1,3},{2,0},{3,1},{4,6},{5,7},{6,4},{7,5},{8,10},{9,11},{10,... | collective-permute-start | bytes 3145736 | tf_op jit(solution)/shard_map/ppermute | solution.py:567
  262.6 28.8 %collective-permute-start.20 = (bf16[256,2048]{1,0:T(8,128)(2,1)S(1)}, bf16[256,2048]{1,0:T(8,128)(2,1)S(1)}, u32[]{:S(2)}, u32[]{:S(2)}) collective-permute-start(bf16[256,2048]{1,0:T(8,128)(2,1)S(1)} %multiply_convert_fusion.refs_0_), channel_id=1, source_target_pairs={{0,1},{1,0},{2,3},{3,2},{4,5},{5,4},{6,7},{7,6},{8,9},{9,8},{10,11... | collective-permute-start | bytes 3145736 | tf_op jit(solution)/shard_map/ppermute | solution.py:567
  291.4 25.7 %collective-permute-start.21 = (bf16[256,2048]{1,0:T(8,128)(2,1)}, bf16[256,2048]{1,0:T(8,128)(2,1)S(1)}, u32[]{:S(2)}, u32[]{:S(2)}) collective-permute-start(bf16[256,2048]{1,0:T(8,128)(2,1)} %get-tuple-element.299.refs_3_), channel_id=1, source_target_pairs={{0,2},{1,3},{2,0},{3,1},{4,6},{5,7},{6,4},{7,5},{8,10},{9,11},{10,... | collective-permute-start | bytes 3145736 | tf_op jit(solution)/shard_map/ppermute | solution.py:567
  318.4 29.1 %collective-permute-start.23 = (bf16[256,2048]{1,0:T(8,128)(2,1)S(1)}, bf16[256,2048]{1,0:T(8,128)(2,1)S(1)}, u32[]{:S(2)}, u32[]{:S(2)}) collective-permute-start(bf16[256,2048]{1,0:T(8,128)(2,1)S(1)} %get-tuple-element.307), channel_id=1, source_target_pairs={{0,2},{1,3},{2,0},{3,1},{4,6},{5,7},{6,4},{7,5},{8,10},{9,11},{10,... | collective-permute-start | bytes 3145736 | tf_op jit(solution)/shard_map/ppermute | solution.py:567
  351.2 34.6 %collective-permute-start.24 = (bf16[256,2048]{1,0:T(8,128)(2,1)S(1)}, bf16[256,2048]{1,0:T(8,128)(2,1)S(1)}, u32[]{:S(2)}, u32[]{:S(2)}) collective-permute-start(bf16[256,2048]{1,0:T(8,128)(2,1)S(1)} %get-tuple-element.338.own), channel_id=1, source_target_pairs={{0,2},{1,3},{2,0},{3,1},{4,6},{5,7},{6,4},{7,5},{8,10},{9,11},{10,... | collective-permute-start | bytes 3145736 | tf_op jit(solution)/shard_map/ppermute | solution.py:567
  353.0 32.9 %collective-permute-start.25 = (bf16[256,2048]{1,0:T(8,128)(2,1)S(1)}, bf16[256,2048]{1,0:T(8,128)(2,1)S(1)}, u32[]{:S(2)}, u32[]{:S(2)}) collective-permute-start(bf16[256,2048]{1,0:T(8,128)(2,1)S(1)} %get-tuple-element.338.own), channel_id=1, source_target_pairs={{0,1},{1,0},{2,3},{3,2},{4,5},{5,4},{6,7},{7,6},{8,9},{9,8},{10,11... | collective-permute-start | bytes 3145736 | tf_op jit(solution)/shard_map/ppermute | solution.py:567
  385.9 42.8 %collective-permute-start.26 = (bf16[256,2048]{1,0:T(8,128)(2,1)}, bf16[256,2048]{1,0:T(8,128)(2,1)}, u32[]{:S(2)}, u32[]{:S(2)}) collective-permute-start(bf16[256,2048]{1,0:T(8,128)(2,1)} %get-tuple-element.328), channel_id=1, source_target_pairs={{0,2},{1,3},{2,0},{3,1},{4,6},{5,7},{6,4},{7,5},{8,10},{9,11},{10,... | collective-permute-start | bytes 3145736 | tf_op jit(solution)/shard_map/ppermute | solution.py:567
  435.6 33.2 %collective-permute-start.27 = (bf16[256,2048]{1,0:T(8,128)(2,1)}, bf16[256,2048]{1,0:T(8,128)(2,1)}, u32[]{:S(2)}, u32[]{:S(2)}) collective-permute-start(bf16[256,2048]{1,0:T(8,128)(2,1)} %get-tuple-element.347.own), channel_id=1, source_target_pairs={{0,2},{1,3},{2,0},{3,1},{4,6},{5,7},{6,4},{7,5},{8,10},{9,11},{10,... | collective-permute-start | bytes 3145736 | tf_op jit(solution)/shard_map/ppermute | solution.py:567
  436.4 32.5 %collective-permute-start.28 = (bf16[256,2048]{1,0:T(8,128)(2,1)}, bf16[256,2048]{1,0:T(8,128)(2,1)}, u32[]{:S(2)}, u32[]{:S(2)}) collective-permute-start(bf16[256,2048]{1,0:T(8,128)(2,1)} %get-tuple-element.347.own), channel_id=1, source_target_pairs={{0,1},{1,0},{2,3},{3,2},{4,5},{5,4},{6,7},{7,6},{8,9},{9,8},{10,11... | collective-permute-start | bytes 3145736 | tf_op jit(solution)/shard_map/ppermute | solution.py:567
  468.9 45.7 %collective-permute-start.29 = (bf16[256,2048]{1,0:T(8,128)(2,1)S(1)}, bf16[256,2048]{1,0:T(8,128)(2,1)S(1)}, u32[]{:S(2)}, u32[]{:S(2)}) collective-permute-start(bf16[256,2048]{1,0:T(8,128)(2,1)S(1)} %get-tuple-element.357), channel_id=1, source_target_pairs={{0,2},{1,3},{2,0},{3,1},{4,6},{5,7},{6,4},{7,5},{8,10},{9,11},{10,... | collective-permute-start | bytes 3145736 | tf_op jit(solution)/shard_map/ppermute | solution.py:567
  515.5 25.3 %collective-permute-start.30 = (bf16[256,2048]{1,0:T(8,128)(2,1)S(1)}, bf16[256,2048]{1,0:T(8,128)(2,1)S(1)}, u32[]{:S(2)}, u32[]{:S(2)}) collective-permute-start(bf16[256,2048]{1,0:T(8,128)(2,1)S(1)} %get-tuple-element.363), channel_id=1, source_target_pairs={{0,2},{1,3},{2,0},{3,1},{4,6},{5,7},{6,4},{7,5},{8,10},{9,11},{10,... | collective-permute-start | bytes 3145736 | tf_op jit(solution)/shard_map/ppermute | solution.py:567
  540.8 38.5 %collective-permute-start.31 = (bf16[256,2048]{1,0:T(8,128)(2,1)S(1)}, bf16[256,2048]{1,0:T(8,128)(2,1)S(1)}, u32[]{:S(2)}, u32[]{:S(2)}) collective-permute-start(bf16[256,2048]{1,0:T(8,128)(2,1)S(1)} %get-tuple-element.377.own), channel_id=1, source_target_pairs={{0,2},{1,3},{2,0},{3,1},{4,6},{5,7},{6,4},{7,5},{8,10},{9,11},{10,... | collective-permute-start | bytes 3145736 | tf_op jit(solution)/shard_map/ppermute | solution.py:567
  541.8 37.5 %collective-permute-start.32 = (bf16[256,2048]{1,0:T(8,128)(2,1)S(1)}, bf16[256,2048]{1,0:T(8,128)(2,1)}, u32[]{:S(2)}, u32[]{:S(2)}) collective-permute-start(bf16[256,2048]{1,0:T(8,128)(2,1)S(1)} %get-tuple-element.377.own), channel_id=1, source_target_pairs={{0,1},{1,0},{2,3},{3,2},{4,5},{5,4},{6,7},{7,6},{8,9},{9,8},{10,11... | collective-permute-start | bytes 3145736 | tf_op jit(solution)/shard_map/ppermute | solution.py:567
  579.3 35.6 %collective-permute-start.33 = (bf16[256,2048]{1,0:T(8,128)(2,1)S(1)}, bf16[256,2048]{1,0:T(8,128)(2,1)S(1)}, u32[]{:S(2)}, u32[]{:S(2)}) collective-permute-start(bf16[256,2048]{1,0:T(8,128)(2,1)S(1)} %get-tuple-element.385.own), channel_id=1, source_target_pairs={{0,2},{1,3},{2,0},{3,1},{4,6},{5,7},{6,4},{7,5},{8,10},{9,11},{10,... | collective-permute-start | bytes 3145736 | tf_op jit(solution)/shard_map/ppermute | solution.py:567
  580.3 34.5 %collective-permute-start.34 = (bf16[256,2048]{1,0:T(8,128)(2,1)S(1)}, bf16[256,2048]{1,0:T(8,128)(2,1)S(1)}, u32[]{:S(2)}, u32[]{:S(2)}) collective-permute-start(bf16[256,2048]{1,0:T(8,128)(2,1)S(1)} %get-tuple-element.385.own), channel_id=1, source_target_pairs={{0,1},{1,0},{2,3},{3,2},{4,5},{5,4},{6,7},{7,6},{8,9},{9,8},{10,11... | collective-permute-start | bytes 3145736 | tf_op jit(solution)/shard_map/ppermute | solution.py:567
  614.9 55.3 %collective-permute-start.35 = (bf16[256,2048]{1,0:T(8,128)(2,1)S(1)}, bf16[256,2048]{1,0:T(8,128)(2,1)S(1)}, u32[]{:S(2)}, u32[]{:S(2)}) collective-permute-start(bf16[256,2048]{1,0:T(8,128)(2,1)S(1)} %get-tuple-element.392), channel_id=1, source_target_pairs={{0,2},{1,3},{2,0},{3,1},{4,6},{5,7},{6,4},{7,5},{8,10},{9,11},{10,... | collective-permute-start | bytes 3145736 | tf_op jit(solution)/shard_map/ppermute | solution.py:567
  670.2 25.5 %collective-permute-start.36 = (bf16[256,2048]{1,0:T(8,128)(2,1)S(1)}, bf16[256,2048]{1,0:T(8,128)(2,1)S(1)}, u32[]{:S(2)}, u32[]{:S(2)}) collective-permute-start(bf16[256,2048]{1,0:T(8,128)(2,1)S(1)} %get-tuple-element.400), channel_id=1, source_target_pairs={{0,2},{1,3},{2,0},{3,1},{4,6},{5,7},{6,4},{7,5},{8,10},{9,11},{10,... | collective-permute-start | bytes 3145736 | tf_op jit(solution)/shard_map/ppermute | solution.py:567
  695.7 540.1 %collective-permute-start.37 = (bf16[256,2048]{1,0:T(8,128)(2,1)}, bf16[256,2048]{1,0:T(8,128)(2,1)}, u32[]{:S(2)}, u32[]{:S(2)}) collective-permute-start(bf16[256,2048]{1,0:T(8,128)(2,1)} %get-tuple-element.420), channel_id=1, source_target_pairs={{0,2},{1,3},{2,0},{3,1},{4,6},{5,7},{6,4},{7,5},{8,10},{9,11},{10,... | collective-permute-start | bytes 3145736 | tf_op jit(solution)/shard_map/ppermute | solution.py:567
  696.7 539.1 %collective-permute-start.38 = (bf16[256,2048]{1,0:T(8,128)(2,1)}, bf16[256,2048]{1,0:T(8,128)(2,1)}, u32[]{:S(2)}, u32[]{:S(2)}) collective-permute-start(bf16[256,2048]{1,0:T(8,128)(2,1)} %get-tuple-element.422), channel_id=1, source_target_pairs={{0,2},{1,3},{2,0},{3,1},{4,6},{5,7},{6,4},{7,5},{8,10},{9,11},{10,... | collective-permute-start | bytes 3145736 | tf_op jit(solution)/shard_map/ppermute | solution.py:567
  (173 other events, 2669.3 us)
Sparse Core Ops, SparseCore 0:
  469.0 610.5 all-reduce.2

commit v3 on v2

--- a/solution.py
+++ b/solution.py
@@ -605,10 +605,12 @@
     return arrived[0] + arrived[1].astype(f32)
 
 
-CHUNK = 128
-WIDE = 512
-CYCLE = 4
+CHUNK = 256
+WIDE = 256
 LANDINGS = 7
+PERIOD = 9
+PAIRED = 6
+LAST_HOP = (8, 9, 11, 13, 15, 16)
 
 
 class Late:
@@ -628,7 +630,27 @@
         self.make().wait_recv()
 
 
-def sum_kernel(cycles, x_ref, out_ref, land, send_sem, recv_sem, local_sem):
+def sum_kernel(cycles, open_count, paired_count, *refs):
+    inputs, refs = refs[: open_count + 2 * paired_count], refs[open_count + 2 * paired_count :]
+    open_in = inputs[:open_count]
+    paired_in = inputs[open_count : open_count + paired_count]
+    arrived_in = inputs[open_count + paired_count :]
+    open_out, paired_out = refs[:2]
+    (
+        opened,
+        paired,
+        open_land,
+        paired_land,
+        open_send,
+        open_recv,
+        open_local,
+        paired_send,
+        paired_recv,
+        paired_local,
+        fill_sem,
+        ring,
+        ring_sem,
+    ) = refs[2:]
     at = lax.axis_index("dp")
     y = lax.rem(at, 2)
     z = lax.div(at, 2)
@@ -638,6 +660,7 @@
     along = at + jnp.where(lax.rem(z, 2) == 0, 2, -2)
     facing = (3 - z) * 2 + y
     side = z - 1
+    paired_chunks = paired.shape[0] // CHUNK
 
     barrier = pltpu.get_barrier_semaphore()
 
@@ -646,6 +669,16 @@
 
     greet(beside)
     greet(along)
+
+    fills = []
+    for sources, target in ((open_in, opened), (paired_in, paired)):
+        start = 0
+        for source in sources:
+            place = target.at[pl.ds(start, source.shape[0])]
+            fills.append(pltpu.make_async_copy(source, place, fill_sem.at[len(fills)]))
+            start += source.shape[0]
+    for fill in fills:
+        fill.start()
 
     @pl.when(inner)
     def _():
@@ -656,17 +689,16 @@
     def _():
         pl.semaphore_wait(barrier, 2)
 
-    def row(stream, cycle, index):
-        start = ((stream * cycles + cycle) * CYCLE + index) * CHUNK
-        return pl.ds(pl.multiple_of(start, CHUNK), CHUNK)
-
-    def remote(stream, cycle, slot, source, target, device):
+    for fill in fills:
+        fill.wait()
+
+    def remote(source, target, send_sem, recv_sem, device):
         return Late(
             lambda: pltpu.make_async_remote_copy(
                 src_ref=source,
                 dst_ref=target,
-                send_sem=send_sem.at[stream, cycle, slot],
-                recv_sem=recv_sem.at[stream, cycle, slot],
+                send_sem=send_sem,
+                recv_sem=recv_sem,
                 device_id={"dp": device},
                 device_id_type=MESH,
             )
@@ -676,184 +708,352 @@
         @pl.loop(0, CHUNK // 32)
         def _(step):
             rows = pl.ds(pl.multiple_of(step * 32, 32), 32)
-            x = x_ref.at[place]
-            x[rows, :] = (x[rows, :].astype(f32) + landing[rows, :].astype(f32)).astype(bf16)
-
-    def stages(stream, cycle):
-        mine = row(stream, cycle, y)
-        other = row(stream, cycle, 1 - y)
-        low = row(stream, cycle, 2)
-        high = row(stream, cycle, 3)
-        own = row(stream, cycle, 2 + side)
-        given = row(stream, cycle, 3 - side)
-        landing = [land.at[stream, cycle, i] for i in range(LANDINGS)]
+            place[rows, :] = (
+                place[rows, :].astype(f32) + landing[rows, :].astype(f32)
+            ).astype(bf16)
+
+    def everyone(descriptor, after):
+        def finish():
+            descriptor.wait()
+            after()
+
+        return descriptor.start, finish
+
+    def inward(descriptor, place, landed):
+        def start():
+            pl.when(outer)(descriptor.start)
+
+        def finish():
+            pl.when(outer)(descriptor.wait_send)
+
+            @pl.when(inner)
+            def _():
+                descriptor.wait_recv()
+                add(place, landed)
+
+        return start, finish
+
+    def between(descriptor, after, local=None):
+        def start():
+            @pl.when(inner)
+            def _():
+                descriptor.start()
+                if local is not None:
+                    local.start()
+
+        def finish():
+            @pl.when(inner)
+            def _():
+                descriptor.wait()
+                if local is not None:
+                    local.wait()
+                after()
+
+        return start, finish
+
+    def outward(descriptor, local=None):
+        def start():
+            @pl.when(inner)
+            def _():
+                descriptor.start()
+                if local is not None:
+                    local.start()
+
+        def finish():
+            @pl.when(inner)
+            def _():
+                descriptor.wait_send()
+                if local is not None:
+                    local.wait()
+
+            pl.when(outer)(descriptor.wait_recv)
+
+        return start, finish
+
+    def nothing():
+        return None
+
+    def rows_of(index):
+        return pl.ds(pl.multiple_of(index * CHUNK, CHUNK), CHUNK)
+
+    def open_stages(stream, cycle):
+        first = (stream * cycles + cycle) * 4
+        x = [opened.at[rows_of(first + i)] for i in (y, 1 - y, 2, 3, 2 + side, 3 - side)]
+        out = [open_out.at[rows_of(first + i)] for i in (y, 1 - y, 2, 3, 2 + side, 3 - side)]
+        mine, other, low, high, own, given = range(6)
+        land = [open_land.at[stream, cycle, i] for i in range(LANDINGS)]
 
         def copy(slot, source, target, device):
-            return remote(stream, cycle, slot, source, target, device)
-
-        def keep(place, slot):
+            return remote(
+                source,
+                target,
+                open_send.at[stream, cycle, slot],
+                open_recv.at[stream, cycle, slot],
+                device,
+            )
+
+        def keep(which, slot):
             return Late(
                 lambda: pltpu.make_async_copy(
-                    x_ref.at[place], out_ref.at[place], local_sem.at[stream, cycle, slot]
+                    x[which], out[which], open_local.at[stream, cycle, slot]
                 )
             )
 
-        def everyone(descriptor, after):
-            def finish():
-                descriptor.wait()
-                after()
-
-            return descriptor.start, finish
-
-        def inward(descriptor, place, landed):
-            def start():
-                pl.when(outer)(descriptor.start)
-
-            def finish():
-                pl.when(outer)(descriptor.wait_send)
-
-                @pl.when(inner)
-                def _():
-                    descriptor.wait_recv()
-                    add(place, landed)
-
-            return start, finish
-
-        def between(descriptor, after, local=None):
-            def start():
-                @pl.when(inner)
-                def _():
-                    descriptor.start()
-                    if local is not None:
-                        local.start()
-
-            def finish():
-                @pl.when(inner)
-                def _():
-                    descriptor.wait()
-                    if local is not None:
-                        local.wait()
-                    after()
-
-            return start, finish
-
-        def outward(descriptor, local=None):
-            def start():
-                @pl.when(inner)
-                def _():
-                    descriptor.start()
-                    if local is not None:
-                        local.start()
-
-            def finish():
-                @pl.when(inner)
-                def _():
-                    descriptor.wait_send()
-                    if local is not None:
-                        local.wait()
-
-                pl.when(outer)(descriptor.wait_recv)
-
-            return start, finish
-
-        def nothing():
-            return None
-
-        x, out = x_ref, out_ref
         return [
-            (0, inward(copy(0, x.at[low], landing[0], along), low, landing[0])),
-            (1, inward(copy(1, x.at[high], landing[1], along), high, landing[1])),
-            (2, between(copy(2, x.at[given], landing[2], facing), lambda: add(own, landing[2]))),
-            (3, between(copy(3, x.at[own], landing[3], beside), lambda: add(own, landing[3]))),
-            (4, between(copy(4, x.at[own], out.at[own], facing), nothing, keep(own, 0))),
-            (5, outward(copy(5, out.at[low], out.at[low], along))),
-            (6, outward(copy(6, out.at[high], out.at[high], along))),
-            (1, everyone(copy(7, x.at[other], landing[4], beside), lambda: add(mine, landing[4]))),
-            (2, inward(copy(8, x.at[mine], landing[5], along), mine, landing[5])),
-            (3, between(copy(9, x.at[mine], landing[6], facing), lambda: add(mine, landing[6]))),
-            (4, outward(copy(10, x.at[mine], out.at[mine], along), keep(mine, 1))),
-            (5, everyone(copy(11, out.at[mine], out.at[mine], beside), nothing)),
+            (0, inward(copy(0, x[low], land[0], along), x[low], land[0])),
+            (1, inward(copy(1, x[high], land[1], along), x[high], land[1])),
+            (2, between(copy(2, x[given], land[2], facing), lambda: add(x[own], land[2]))),
+            (3, between(copy(3, x[own], land[3], beside), lambda: add(x[own], land[3]))),
+            (4, between(copy(4, x[own], out[own], facing), nothing, keep(own, 0))),
+            (5, outward(copy(5, out[low], out[low], along))),
+            (6, outward(copy(6, out[high], out[high], along))),
+            (1, everyone(copy(7, x[other], land[4], beside), lambda: add(x[mine], land[4]))),
+            (2, inward(copy(8, x[mine], land[5], along), x[mine], land[5])),
+            (3, between(copy(9, x[mine], land[6], facing), lambda: add(x[mine], land[6]))),
+            (4, outward(copy(10, x[mine], out[mine], along), keep(mine, 1))),
+            (5, everyone(copy(11, out[mine], out[mine], beside), nothing)),
         ]
 
+    def paired_stages(stream, cycle, index):
+        chunk = (stream * cycles + cycle) * PAIRED + index
+        x = paired.at[rows_of(chunk)]
+        out = paired_out.at[y, rows_of(chunk)]
+        land = [paired_land.at[chunk, i] for i in range(2)]
+
+        def copy(slot, source, target, device):
+            return remote(
+                source, target, paired_send.at[chunk, slot], paired_recv.at[chunk, slot], device
+            )
+
+        keep = Late(lambda: pltpu.make_async_copy(x, out, paired_local.at[chunk]))
+        slot, slot_sem = ring.at[stream, index], ring_sem.at[stream, index]
+
+        def fetch():
+            begin = 0
+            for source in arrived_in:
+                count = source.shape[0] // CHUNK
+
+                @pl.when((chunk >= begin) & (chunk < begin + count))
+                def _(source=source, begin=begin):
+                    pltpu.make_async_copy(
+                        source.at[rows_of(chunk - begin)], slot, slot_sem
+                    ).start()
+
+                begin += count
+
+        def fetched():
+            pltpu.make_async_copy(arrived_in[0].at[rows_of(0)], slot, slot_sem).wait()
+            add(x, slot)
+
+        return [
+            (2 + index, (fetch, fetched)),
+            (3 + index, inward(copy(0, x, land[0], along), x, land[0])),
+            (5 + index, between(copy(1, x, land[1], facing), lambda: add(x, land[1]))),
+            (7 + index, outward(copy(2, x, out, along), keep)),
+            (LAST_HOP[index], everyone(copy(3, out, out, beside), nothing)),
+        ]
+
+    offsets = range(max(LAST_HOP) + 1)
+
+    def run(step, stream, offset, back, what):
+        cycle = step - back
+
+        @pl.when((cycle >= 0) & (cycle < cycles))
+        def _():
+            for when, pair in open_stages(stream, cycle):
+                if when == offset:
+                    pair[what]()
+            for index in range(PAIRED):
+                chunk = (stream * cycles + cycle) * PAIRED + index
+
+                def each(index=index):
+                    for when, pair in paired_stages(stream, cycle, index):
+                        if when == offset:
+                            pair[what]()
+
+                if offset in (2 + index, 3 + index, 5 + index, 7 + index, LAST_HOP[index]):
+                    pl.when(chunk < paired_chunks)(each)
+
     def body(step, carry):
-        for phase in range(3):
-            for stream in range(2):
-
-                def each(back, offset, what):
-                    cycle = step - back
-
-                    @pl.when((cycle >= 0) & (cycle < cycles))
-                    def _():
-                        for when, (start, finish) in stages(stream, cycle):
-                            if when == offset:
-                                (start if what == 0 else finish)()
-
-                for offset in range(7):
-                    if (offset + 1) % 3 == phase:
-                        each((offset + 1) // 3, offset, 1)
-                for offset in range(7):
-                    if offset % 3 == phase:
-                        each(offset // 3, offset, 0)
+        for phase in range(PERIOD):
+
+            @pl.loop(0, 2)
+            def _(stream):
+                for offset in offsets:
+                    if (offset + 1) % PERIOD == phase:
+                        run(step, stream, offset, (offset + 1) // PERIOD, 1)
+                for offset in offsets:
+                    if offset % PERIOD == phase:
+                        run(step, stream, offset, offset // PERIOD, 0)
+
         return carry
 
-    lax.fori_loop(0, cycles + 3, body, 0)
-
-
-def sum_chunks(stack):
-    cycles = stack.shape[0] // (CHUNK * CYCLE * 2)
-    size = stack.shape[0] * WIDE * 2
+    lax.fori_loop(0, cycles + 2, body, 0)
+
+
+def sum_chunks(opened, paired, arrived):
+    open_rows = sum(item.shape[0] for item in opened)
+    paired_rows = sum(item.shape[0] for item in paired)
+    cycles = open_rows // (CHUNK * 8)
+    chunks = paired_rows // CHUNK
+    assert cycles * CHUNK * 8 == open_rows and chunks <= 2 * cycles * PAIRED
     return pl.pallas_call(
-        partial(sum_kernel, cycles),
-        in_specs=[pl.BlockSpec(memory_space=pltpu.VMEM)],
-        out_specs=pl.BlockSpec(memory_space=pl.ANY),
-        out_shape=jax.ShapeDtypeStruct(stack.shape, bf16),
+        partial(sum_kernel, cycles, len(opened), len(paired)),
+        in_specs=[pl.BlockSpec(memory_space=pl.ANY)] * (len(opened) + 2 * len(paired)),
+        out_specs=[pl.BlockSpec(memory_space=pl.ANY)] * 2,
+        out_shape=[
+            jax.ShapeDtypeStruct((open_rows, WIDE), bf16),
+            jax.ShapeDtypeStruct((2, paired_rows, WIDE), bf16),
+        ],
         scratch_shapes=[
+            pltpu.VMEM((open_rows, WIDE), bf16),
+            pltpu.VMEM((paired_rows, WIDE), bf16),
             pltpu.VMEM((2, cycles, LANDINGS, CHUNK, WIDE), bf16),
+            pltpu.VMEM((chunks, 2, CHUNK, WIDE), bf16),
             pltpu.SemaphoreType.DMA((2, cycles, 12)),
             pltpu.SemaphoreType.DMA((2, cycles, 12)),
             pltpu.SemaphoreType.DMA((2, cycles, 2)),
+            pltpu.SemaphoreType.DMA((chunks, 4)),
+            pltpu.SemaphoreType.DMA((chunks, 4)),
+            pltpu.SemaphoreType.DMA((chunks,)),
+            pltpu.SemaphoreType.DMA((len(opened) + len(paired),)),
+            pltpu.VMEM((2, PAIRED, CHUNK, WIDE), bf16),
+            pltpu.SemaphoreType.DMA((2, PAIRED)),
         ],
         compiler_params=pltpu.CompilerParams(
             collective_id=0, has_side_effects=True, vmem_limit_bytes=63 * 1024 * 1024
         ),
         cost_estimate=pl.CostEstimate(
-            flops=size, bytes_accessed=4 * size, transcendentals=0
-        ),
-    )(stack)
-
-
-def to_chunks(tensor):
-    height, width = tensor.shape
-    return [tensor[:, at : at + WIDE] for at in range(0, width, WIDE)]
-
-
-def chunked(tensors):
-    size = sum(item.size for item in tensors)
-    fits = size % (CHUNK * WIDE * CYCLE * 2) == 0 and all(
-        item.shape[0] % CHUNK == 0 and item.shape[1] % WIDE == 0 for item in tensors
-    )
-    return lax.axis_size("dp") == 8 and fits
-
-
-def sum_dp_start(tensors):
-    low = [item.astype(bf16) for item in tensors]
-    if not chunked(low):
-        return lax.psum(low, "dp")
-    return sum_chunks(jnp.concatenate([piece for item in low for piece in to_chunks(item)], axis=0))
-
-
-def sum_dp_end(total, tensors):
-    if not chunked(tensors):
-        return [item.astype(f32) for item in total]
-    out, at = [], 0
-    for item in tensors:
-        height, width = item.shape
-        pieces = []
-        for _ in range(width // WIDE):
-            pieces.append(total[at : at + height])
-            at += height
-        out.append(jnp.concatenate(pieces, axis=1).astype(f32))
-    return out
+            flops=open_rows * WIDE * 4,
+            bytes_accessed=(open_rows + 2 * paired_rows) * WIDE * 8,
+            transcendentals=0,
+        ),
+    )(*opened, *paired, *arrived)
+
+
+def weight_grad_kernel(count, *refs):
+    lefts, rights, out = refs[:count], refs[count : 2 * count], refs[-1]
+    total = sum(dot_tn(left[...], right[...]) for left, right in zip(lefts, rights))
+    for piece in range(out.shape[1]):
+        out[0, piece] = total[:, piece * WIDE : (piece + 1) * WIDE].astype(bf16)
+
+
+def weight_grad(lefts, rights):
+    depth, height = lefts[0].shape
+    width = rights[0].shape[1]
+    half, pieces = height // 2, width // WIDE
+    tile = half if half <= 640 else 512
+    steps = half // tile
+    count = len(lefts)
+    return pl.pallas_call(
+        partial(weight_grad_kernel, count),
+        grid=(2 * steps,),
+        in_specs=[pl.BlockSpec((depth, tile), lambda i: (0, i))] * count
+        + [pl.BlockSpec((depth, width), lambda i: (0, 0))] * count,
+        out_specs=pl.BlockSpec((1, pieces, tile, WIDE), lambda i: (i // steps, 0, i % steps, 0)),
+        out_shape=jax.ShapeDtypeStruct((2, pieces, half, WIDE), bf16),
+        compiler_params=pltpu.CompilerParams(vmem_limit_bytes=VMEM_LIMIT),
+        cost_estimate=pl.CostEstimate(
+            flops=2 * count * depth * height * width,
+            bytes_accessed=2 * (count * depth * (height + width) + height * width),
+            transcendentals=0,
+        ),
+    )(*lefts, *rights)
+
+
+def side_grads_kernel(steps, count, y_ref, *refs):
+    lefts, rights = refs[:count], refs[count : 2 * count]
+    total = sum(dot_tn(left[...], right[...]) for left, right in zip(lefts, rights))
+    for turn, out in enumerate(refs[-2:]):
+
+        @pl.when(pl.program_id(0) // steps == turn)
+        def _():
+            for piece in range(out.shape[0]):
+                out[piece] = total[:, piece * WIDE : (piece + 1) * WIDE].astype(bf16)
+
+
+def side_grads(lefts, rights):
+    depth, height = lefts[0].shape
+    width = rights[0].shape[1]
+    half, pieces = height // 2, width // WIDE
+    tile = half if half <= 640 else 512
+    steps = half // tile
+    count = len(lefts)
+    y = (lax.axis_index("dp") % 2).astype(jnp.int32).reshape(1)
+
+    def left_at(i, y):
+        owner = (i // steps) * y[0] + (1 - i // steps) * (1 - y[0])
+        return (0, owner * steps + i % steps)
+
+    shape = jax.ShapeDtypeStruct((pieces, half, WIDE), bf16)
+    return pl.pallas_call(
+        partial(side_grads_kernel, steps, count),
+        grid_spec=pltpu.PrefetchScalarGridSpec(
+            num_scalar_prefetch=1,
+            grid=(2 * steps,),
+            in_specs=[pl.BlockSpec((depth, tile), left_at)] * count
+            + [pl.BlockSpec((depth, width), lambda i, y: (0, 0))] * count,
+            out_specs=[
+                pl.BlockSpec((pieces, tile, WIDE), lambda i, y: (0, jnp.minimum(i, steps - 1), 0)),
+                pl.BlockSpec((pieces, tile, WIDE), lambda i, y: (0, jnp.maximum(i - steps, 0), 0)),
+            ],
+        ),
+        out_shape=[shape, shape],
+        compiler_params=pltpu.CompilerParams(vmem_limit_bytes=VMEM_LIMIT),
+        cost_estimate=pl.CostEstimate(
+            flops=2 * count * depth * height * width,
+            bytes_accessed=2 * (count * depth * (height + width) + height * width),
+            transcendentals=0,
+        ),
+    )(y, *lefts, *rights)
+
+
+def stacked(grads):
+    return grads.reshape(-1, WIDE)
+
+
+def unpack_kernel(pieces, *refs):
+    count = len(refs) // (pieces + 1)
+    for at in range(count):
+        out = refs[count * pieces + at]
+        for piece in range(pieces):
+            out[:, piece * WIDE : (piece + 1) * WIDE] = refs[at * pieces + piece][0].astype(f32)
+
+
+def unpack(height, width, tile, *places):
+    half, pieces = height // 2, width // WIDE
+    steps = half // tile
+
+    def piece_spec(first, second, piece):
+        begin, step = first[1] // tile, (second[1] - first[1]) // tile
+        assert first[1] % tile == 0 and second[1] % tile == 0
+        return pl.BlockSpec(
+            (1, tile, WIDE),
+            lambda i, j: (
+                first[0] + i * (second[0] - first[0]),
+                begin + i * step + piece * steps + j,
+                0,
+            ),
+        )
+
+    count = len(places)
+    return pl.pallas_call(
+        partial(unpack_kernel, pieces),
+        grid=(2, steps),
+        in_specs=[
+            piece_spec(first, second, piece)
+            for _, first, second in places
+            for piece in range(pieces)
+        ],
+        out_specs=[pl.BlockSpec((tile, width), lambda i, j: (i * steps + j, 0))] * count,
+        out_shape=[jax.ShapeDtypeStruct((height, width), f32)] * count,
+        compiler_params=pltpu.CompilerParams(vmem_limit_bytes=60 * 1024 * 1024),
+        cost_estimate=pl.CostEstimate(
+            flops=count * height * width,
+            bytes_accessed=6 * count * height * width,
+            transcendentals=0,
+        ),
+    )(*[stack for stack, _, _ in places for _ in range(pieces)])
 
 
 def on_device(
@@ -883,7 +1083,8 @@
     examples = text_lengths.shape[0]
     patch = patches.shape[0] // examples
     local_examples = local_rows // SEQ
-    batches = 2 if local_examples % 2 == 0 else 1
+    fast = lax.axis_size("mp") == 4 and lax.axis_size("dp") == 8 and local_examples % 2 == 0
+    batches = 2 if fast else 1
     each = local_examples // batches
     rows = each * SEQ
     width = q_self.shape[1]
@@ -1006,39 +1207,13 @@
     def project_out(b):
         return scattered_dot([hidden[b]], [w_down], False, True, 11)
 
-    def weight_grad(left, right):
-        return sum(dot_tn(left[b], right[b]) for b in each_batch)
-
-    def move_self(b, sent):
-        return scatter_move(sent, product(mixed_self[b], o_self, dot_nn), rows)
-
-    def move_cross(b, sent):
-        return scatter_move(sent, product(mixed_cross[b], o_cross, dot_nn), rows)
-
-    def mlp_product(b):
-        return lambda low, high: (
-            dot_nt(d_gate[b][low:high], w_gate) + dot_nt(d_up[b][low:high], w_up)
-        )
-
-    def move_mlp(b, sent):
-        return scatter_move(sent, mlp_product(b), rows)
-
-    def move_cross_back(b, sent):
-        return scatter_move(sent, product(d_query[b], q_cross, dot_nt), rows)
-
-    def move_self_back(b, sent):
-        return scatter_move(sent, product(d_qkv[b], w_qkv, dot_nt), rows)
-
-    def move_out(b, sent):
-        return scatter_move(sent, product(hidden[b], w_down, dot_nn), rows)
-
     sent = list(none)
     got = list(none)
     back = list(none)
     grads = list(none)
     own = list(none)
     shown = list(none)
-    if batches == 2:
+    if fast:
         got[0] = gather_start(norm_one[0])
         got[0], norm_one[1], w_qkv, outer_low, outer, which, lengths, prefixes = fence(
             got[0], norm_one[1], w_qkv, outer_low, outer, which, lengths, prefixes
@@ -1085,54 +1260,69 @@
         own[0] = mlp_norm_back(0, back[0])
         got[0] = gather_start(own[0])
         sent[1] = mlp_back(1)
-        d_wdown = weight_grad(hidden, grad_three)
-        own[0], got[0], sent[1], d_gate, d_up, d_wdown = fence(
-            own[0], got[0], sent[1], d_gate, d_up, d_wdown
+        down_other, down_mine = side_grads(hidden, grad_three)
+        own[0], got[0], sent[1], d_gate, d_up, down_other = fence(
+            own[0], got[0], sent[1], d_gate, d_up, down_other
         )
         back[1] = scatter_move(sent[1])
-        d_wgate = weight_grad(full_three, d_gate)
-        d_wup = weight_grad(full_three, d_up)
-        back[1], d_wgate, d_wup, d_wdown = fence(back[1], d_wgate, d_wup, d_wdown)
-        d_mlp = lax.psum([item.astype(bf16) for item in (d_wdown, d_wgate, d_wup)], "dp")
+        down_sent = flip(down_other, "dp", 1)
+        gate_other, gate_mine = side_grads(full_three, d_gate)
+        up_other, up_mine = side_grads(full_three, d_up)
+        back[1], gate_other, up_other = fence(back[1], gate_other, up_other)
         own[1] = mlp_norm_back(1, back[1])
         got[1] = gather_start(own[1])
+        gate_sent = flip(gate_other, "dp", 1)
         sent[0], d_kv = cross_back(0, own[0], got[0], keys, values, ())
-        own[1], got[1], sent[0], d_kv = fence(own[1], got[1], sent[0], d_kv)
+        own[1], got[1], sent[0], d_kv, down_sent, up_other = fence(
+            own[1], got[1], sent[0], d_kv, down_sent, up_other
+        )
         back[0] = scatter_move(sent[0])
+        up_sent = flip(up_other, "dp", 1)
         sent[1], d_kv = cross_back(1, own[1], got[1], keys, values, d_kv)
         sent[1], back[0], d_kv, mixed_cross, hidden = fence(
             sent[1], back[0], d_kv, mixed_cross, hidden
         )
         back[1] = scatter_move(sent[1])
         own[0] = cross_norm_back(0, back[0])
-        d_ocross = weight_grad(mixed_cross, grad_two)
-        d_qcross = weight_grad(full_two, d_query)
+        o_other, o_mine = side_grads(mixed_cross, grad_two)
+        q_other, q_mine = side_grads(full_two, d_query)
         shown[0] = project_out(0)
-        own[0], back[1], d_kv, d_ocross, d_qcross, shown[0] = fence(
-            own[0], back[1], d_kv, d_ocross, d_qcross, shown[0]
+        own[0], back[1], d_kv, o_other, q_other, shown[0], gate_sent, down_mine = fence(
+            own[0], back[1], d_kv, o_other, q_other, shown[0], gate_sent, down_mine
         )
         got[0] = gather_start(own[0])
+        o_sent, q_sent = flip(o_other, "dp", 1), flip(q_other, "dp", 1)
         own[1] = cross_norm_back(1, back[1])
-        d_kcross = dot_tn(patches, d_kv[0])
-        d_vcross = dot_tn(patches, d_kv[1])
-        got[0], own[1], d_kcross, d_vcross, hidden = fence(
-            got[0], own[1], d_kcross, d_vcross, hidden
+        k_other, k_mine = side_grads([patches], [d_kv[0]])
+        v_other, v_mine = side_grads([patches], [d_kv[1]])
+        got[0], own[1], k_other, v_other, hidden, up_sent, gate_mine = fence(
+            got[0], own[1], k_other, v_other, hidden, up_sent, gate_mine
         )
         got[1] = gather_start(own[1])
+        k_sent, v_sent = flip(k_other, "dp", 1), flip(v_other, "dp", 1)
         sent[0] = self_back(0, own[0], got[0])
-        got[1], sent[0] = fence(got[1], sent[0])
+        got[1], sent[0], o_sent, q_sent, up_mine = fence(got[1], sent[0], o_sent, q_sent, up_mine)
         back[0] = scatter_move(sent[0])
         sent[1] = self_back(1, own[1], got[1])
-        back[0], sent[1], mixed_self, hidden = fence(back[0], sent[1], mixed_self, hidden)
+        back[0], sent[1], mixed_self, hidden, o_mine, q_mine = fence(
+            back[0], sent[1], mixed_self, hidden, o_mine, q_mine
+        )
         back[1] = scatter_move(sent[1])
         self_norm_back(0, back[0])
         d_oself = weight_grad(mixed_self, grad_one)
         d_wqkv = weight_grad(full_one, d_qkv)
         shown[1] = project_out(1)
-        back[1], grad_input[0], d_wqkv, d_oself, shown = fence(
-            back[1], grad_input[0], d_wqkv, d_oself, shown
+        back[1], grad_input[0], d_wqkv, d_oself, shown, k_sent, v_sent = fence(
+            back[1], grad_input[0], d_wqkv, d_oself, shown, k_sent, v_sent
         )
         self_norm_back(1, back[1])
+        back = [scatter_move(shown[b]) for b in each_batch]
+        opened = [d_wqkv, d_oself]
+        paired = [down_mine, gate_mine, up_mine, q_mine, k_mine, v_mine, o_mine]
+        arrived = [down_sent, gate_sent, up_sent, q_sent, k_sent, v_sent, o_sent]
+        open_sum, paired_sum = sum_chunks(
+            *([stacked(item) for item in items] for items in (opened, paired, arrived))
+        )
     else:
         sent[0] = self_block(0, gather_start(norm_one[0]))
         self_norm(0, scatter_move(sent[0]))
@@ -1146,38 +1336,77 @@
         own[0] = cross_norm_back(0, scatter_move(sent[0]))
         sent[0] = self_back(0, own[0], gather_start(own[0]))
         self_norm_back(0, scatter_move(sent[0]))
-        d_wdown = weight_grad(hidden, grad_three)
-        d_wgate = weight_grad(full_three, d_gate)
-        d_wup = weight_grad(full_three, d_up)
-        d_kcross = dot_tn(patches, d_kv[0])
-        d_vcross = dot_tn(patches, d_kv[1])
-        d_wqkv = weight_grad(full_one, d_qkv)
-        d_qcross = weight_grad(full_two, d_query)
-        d_oself = weight_grad(mixed_self, grad_one)
-        d_ocross = weight_grad(mixed_cross, grad_two)
-        d_mlp = lax.psum([item.astype(bf16) for item in (d_wdown, d_wgate, d_wup)], "dp")
-        shown = [project_out(0)]
-    back = [scatter_move(shown[b]) for b in each_batch]
+        sums = lax.psum(
+            [
+                item.astype(bf16)
+                for item in (
+                    dot_tn(full_one[0], d_qkv[0]),
+                    dot_tn(mixed_self[0], grad_one[0]),
+                    dot_tn(full_two[0], d_query[0]),
+                    dot_tn(patches, d_kv[0]),
+                    dot_tn(patches, d_kv[1]),
+                    dot_tn(mixed_cross[0], grad_two[0]),
+                    dot_tn(full_three[0], d_gate[0]),
+                    dot_tn(full_three[0], d_up[0]),
+                    dot_tn(hidden[0], grad_three[0]),
+                )
+            ],
+            "dp",
+        )
+        back = [scatter_move(project_out(0))]
     gains = jnp.stack(
         [sum(parts) for parts in (gain_attn_parts, gain_cross_parts, gain_mlp_parts)]
     )
-    summed = sum_dp_start([d_ocross, d_qcross, d_kcross, d_vcross, d_oself, d_wqkv])
-    summed, d_mlp, back, gains = fence(summed, d_mlp, back, gains)
-    gains = butterfly(butterfly(gains, "mp"), "dp")
-    d_ocross, d_qcross, d_kcross, d_vcross, d_oself, d_wqkv = sum_dp_end(
-        summed, [d_ocross, d_qcross, d_kcross, d_vcross, d_oself, d_wqkv]
-    )
+    if fast:
+        open_sum, paired_sum, back, gains = fence(open_sum, paired_sum, back, gains)
+
+        whole = open_sum[None]
+        half = q_self.shape[0] // 2
+        pieces = width // WIDE
+        places, start = [], 0
+        for weight in (w_down, w_gate, w_up, q_cross, k_cross, v_cross, o_cross):
+            places.append((paired_sum, (0, start), (1, start)))
+            start += weight.size // WIDE // 2
+        self_places = [
+            (whole, (0, at * pieces * half), (0, (3 + at) * pieces * half)) for at in range(3)
+        ]
+        start = w_qkv.size // WIDE
+        o_place = (whole, (0, start), (0, start + o_self.size // WIDE // 2))
+        groups = [
+            unpack(*w_down.shape, w_down.shape[0] // 4, places[0]),
+            unpack(*w_gate.shape, 256, *places[1:3]),
+            unpack(*q_self.shape, 256, *places[3:6], *self_places),
+            unpack(*o_self.shape, o_self.shape[0] // 4, places[6], o_place),
+        ]
+        gains = gains + flip(gains, "mp", 1)
+        for at, (axis, bit) in enumerate((("mp", 2), ("dp", 1), ("dp", 2), ("dp", 4))):
+            arrived, groups[at] = fence(flip(gains, axis, bit), groups[at])
+            gains = gains + arrived
+        (d_wdown,), (d_wgate, d_wup), shared, (d_ocross, d_oself) = groups
+        d_qcross, d_kcross, d_vcross, *d_self = shared
+    else:
+        (
+            d_wqkv,
+            d_oself,
+            d_qcross,
+            d_kcross,
+            d_vcross,
+            d_ocross,
+            d_wgate,
+            d_wup,
+            d_wdown,
+        ) = [item.astype(f32) for item in sums]
+        d_self = [d_wqkv[:, at * width : (at + 1) * width] for at in range(3)]
     output = jnp.concatenate(
         [(x_two[b] + scatter_end(back[b])).astype(bf16) for b in each_batch], axis=0
     )
     grad_input = jnp.concatenate(grad_input, axis=0)
-    d_wdown, d_wgate, d_wup = [item.astype(f32) for item in d_mlp]
+    if not fast:
+        gains = butterfly(butterfly(gains, "mp"), "dp")
     return (
         output,
         grad_input,
-        d_wqkv[:, :width],
-        d_wqkv[:, width : 2 * width],
-        d_wqkv[:, 2 * width :],
+        *d_self,
         d_oself,
         d_qcross,
         d_kcross,

time: 1310 us -> 1240 us (0.947)
  matrix products: 142 us -> 25.1 us
  Pallas kernels: 837 us -> 941 us
  local copies, waits for them, and re-layouts: 66.9 us -> 31.7 us
  other arithmetic: 91.3 us -> 71.1 us
  between operations: 16.4 us -> 2.69 us
    dot_general x16 -> x0, matrix products: 117 us -> none  [dot_tn(): lax.dot_general(left, right, (((0,), (0,)), ((), ())), preferred_element_...]
    pallas_call x1 -> x14, Pallas kernels: 523 us -> 630 us  [the longest x1 461 us: sum_chunks(): pl.pallas_call(partial(sum_kernel, cycles, len(opened), len(paired)), in_...]
    convert_element_type x7 -> x0, other arithmetic: 35.7 us -> none  [the longest x4 19.5 us: sum_dp_end(): out.append(jnp.concatenate(pieces, axis=1).astype(f32))]
    unnamed x317 -> x208, local copies, waits for them, and re-layouts: 48.9 us -> 27.6 us
    ppermute x44 -> x51, waiting for transfers between devices: 111 us -> 122 us  [flip(): return lax.ppermute(tensor, axis, [(i, i ^ bit) for i in range(count)])]
    ppermute x44 -> x51, starting transfers between devices: 38.2 us -> 40.3 us  [flip(): return lax.ppermute(tensor, axis, [(i, i ^ bit) for i in range(count)])]
  transfers between devices with their start and end apart: 45 -> 51, of which waited for: 14 -> 16; matrix products, arithmetic and copies ran while one was open for 18% -> 7% of each run, Pallas kernels for 64% -> 76%
where the time goes in v3:
time: 1240 us; the launch traced here: 1230 us
  Pallas kernels  941 us (76%)
  waiting for transfers between devices  122 us (10%)
  other arithmetic  71.1 us (6%)
  starting transfers between devices  40.3 us (3%)
  local copies, waits for them, and re-layouts  31.7 us (3%)
  matrix products  25.1 us (2%)
    pallas_call x1, Pallas kernels, sum_chunks(): pl.pallas_call(partial(sum_kernel, cycles, len(opened), len(paired)), in_...  461 us
    ppermute x51, waiting for transfers between devices, flip(): return lax.ppermute(tensor, axis, [(i, i ^ bit) for i in range(count)])  122 us
    pallas_call x12, Pallas kernels, scattered_dot(): pl.pallas_call(partial(scattered_kernel, transposed, len(lefts), size), i...  104 us
    pallas_call x7, Pallas kernels, side_grads(): pl.pallas_call(partial(side_grads_kernel, steps, count), grid_spec=pltpu....  101 us
    pallas_call x2, Pallas kernels, gathered_mlp(): pl.pallas_call(partial(gathered_mlp_kernel, units // tile), grid=(units /...  57.7 us
    pallas_call x8, Pallas kernels, gathered_dot(): pl.pallas_call(partial(gathered_kernel, transposed, 512), in_specs=[IN_VM...  41.6 us
    ppermute x51, starting transfers between devices, flip(): return lax.ppermute(tensor, axis, [(i, i ^ bit) for i in range(count)])  40.3 us
    pallas_call x2, Pallas kernels, cross_backward(): pl.pallas_call(cross_backward_kernel, grid_spec=pltpu.PrefetchScalarGridS...  39.6 us
  transfers between devices with their start and end apart: 51, of which 16 were waited for; matrix products, arithmetic and copies ran while one was open for 7% of the time, Pallas kernels for 76%

profile of v3, /device:TPU:0, one launch (start us, length us, event | category | flops | bytes accessed | tf_op | source)
XLA Modules:
  0.0 1234.5 jit_solution(14293819394547635392)
XLA Ops:
  90.3 12.5 %fusion.key_ref = bf16[4096,512]{1,0:T(8,128)(2,1)S(1)} fusion(bf16[4096,2048]{1,0:T(8,128)(2,1)} %refs_0_.3, bf16[2048,512]{1,0:T(8,128)(2,1)S(1)} %copy-done.94), kind=kOutput, calls=%fused_computation.7 | convolution fusion | flops 8592031744 | bytes 23068672 | tf_op jit(solution)/shard_map/dot_general | solution.py:21
  102.8 11.2 collective-permute-done.9
  114.7 12.7 %fusion.1.value_ref = bf16[4096,512]{1,0:T(8,128)(2,1)S(1)} fusion(bf16[4096,2048]{1,0:T(8,128)(2,1)} %refs_0_.3, bf16[2048,512]{1,0:T(8,128)(2,1)S(1)} %copy-done.95), kind=kOutput, calls=%fused_computation.8 | convolution fusion | flops 8592031744 | bytes 23068672 | tf_op jit(solution)/shard_map/dot_general | solution.py:21
  140.5 22.9 %collective-permute-done.11.across = bf16[256,2048]{1,0:T(8,128)(2,1)S(1)} collective-permute-done((bf16[256,2048]{1,0:T(8,128)(2,1)S(1)}, bf16[256,2048]{1,0:T(8,128)(2,1)S(1)}, u32[]{:S(2)}, u32[]{:S(2)}) %collective-permute-start.11) | collective-permute-done | bytes 1048608 | tf_op jit(solution)/shard_map/ppermute | solution.py:567
  215.0 22.7 %collective-permute-done.16 = bf16[256,2048]{1,0:T(8,128)(2,1)S(1)} collective-permute-done((bf16[256,2048]{1,0:T(8,128)(2,1)S(1)}, bf16[256,2048]{1,0:T(8,128)(2,1)S(1)}, u32[]{:S(2)}, u32[]{:S(2)}) %collective-permute-start.16) | collective-permute-done | bytes 1048608 | tf_op jit(solution)/shard_map/ppermute | solution.py:567
  240.4 22.9 %collective-permute-done.17.refs_2_ = bf16[256,2048]{1,0:T(8,128)(2,1)S(1)} collective-permute-done((bf16[256,2048]{1,0:T(8,128)(2,1)S(1)}, bf16[256,2048]{1,0:T(8,128)(2,1)S(1)}, u32[]{:S(2)}, u32[]{:S(2)}) %collective-permute-start.17) | collective-permute-done | bytes 1048608 | tf_op jit(solution)/shard_map/ppermute | solution.py:567
  264.3 28.9 %shard_map.336 = (bf16[1024,2048]{1,0:T(8,128)(2,1)}, bf16[1024,2048]{1,0:T(8,128)(2,1)}, bf16[1024,1280]{1,0:T(8,128)(2,1)}, bf16[1024,1280]{1,0:T(8,128)(2,1)}, bf16[1024,1280]{1,0:T(8,128)(2,1)}) custom-call(bf16[256,2048]{1,0:T(8,128)(2,1)} %copy-done.76, bf16[256,2048]{1,0:T(8,128)(2,1)} %copy-done.100, bf16[256,2048]{1,0:T(8,128)(2,1)} %copy-done.101, ...), custom_call_target="tpu_custom_call" | custom-call | flops 16106127360 | bytes 38273024 | tf_op jit(solution)/shard_map/pallas_call | solution.py:509
  298.2 17.8 %shard_map.337 = (f32[256,2048]{1,0:T(8,128)S(1)}, bf16[256,2048]{1,0:T(8,128)(2,1)S(1)}) custom-call(bf16[1024,1280]{1,0:T(8,128)(2,1)S(1)} %copy-done.54, bf16[1024,1280]{1,0:T(8,128)(2,1)} %get-tuple-element.386.refs_1_.refs_2_, bf16[2048,1280]{1,0:T(8,128)(2,1)} %refs_2_.3, bf16[2048,1280]{1,0:T(8,128)(2,1)} %refs_3_.3), custom_call_target="tpu_custom_call" | custom-call | flops 10737418240 | bytes 33554432 | tf_op jit(solution)/shard_map/pallas_call | solution.py:388
  322.1 28.8 %shard_map.338 = (bf16[1024,2048]{1,0:T(8,128)(2,1)}, bf16[1024,2048]{1,0:T(8,128)(2,1)}, bf16[1024,1280]{1,0:T(8,128)(2,1)}, bf16[1024,1280]{1,0:T(8,128)(2,1)}, bf16[1024,1280]{1,0:T(8,128)(2,1)}) custom-call(bf16[256,2048]{1,0:T(8,128)(2,1)} %copy-done.75, bf16[256,2048]{1,0:T(8,128)(2,1)} %copy-done.98, bf16[256,2048]{1,0:T(8,128)(2,1)} %copy-done.99, ...), custom_call_target="tpu_custom_call" | custom-call | flops 16106127360 | bytes 38273024 | tf_op jit(solution)/shard_map/pallas_call | solution.py:509
  358.3 17.9 %shard_map.339 = (f32[256,2048]{1,0:T(8,128)S(1)}, bf16[256,2048]{1,0:T(8,128)(2,1)S(1)}) custom-call(bf16[1024,1280]{1,0:T(8,128)(2,1)S(1)} %copy-done.55, bf16[1024,1280]{1,0:T(8,128)(2,1)} %get-tuple-element.387.refs_1_.refs_3_, bf16[2048,1280]{1,0:T(8,128)(2,1)} %refs_2_.3, bf16[2048,1280]{1,0:T(8,128)(2,1)} %refs_3_.3), custom_call_target="tpu_custom_call" | custom-call | flops 10737418240 | bytes 33554432 | tf_op jit(solution)/shard_map/pallas_call | solution.py:388
  377.1 18.4 %shard_map.340 = (bf16[8,640,256]{2,1,0:T(8,128)(2,1)}, bf16[8,640,256]{2,1,0:T(8,128)(2,1)}) custom-call(s32[1]{0:T(128)} %bitcast.9.y_ref, bf16[1024,1280]{1,0:T(8,128)(2,1)} %get-tuple-element.429.refs_0_, bf16[1024,1280]{1,0:T(8,128)(2,1)} %get-tuple-element.475.refs_1_.refs_0_, bf16[1024,2048]{1,0:T(8,128)(2,1)} %get-tuple-element.376.refs_2_, ...), custom_call_target="tpu_custom_call" | custom-call | flops 10737418240 | bytes 18874368 | tf_op jit(solution)/shard_map/pallas_call | solution.py:989
  397.1 17.1 %shard_map.341 = (bf16[5,1024,256]{2,1,0:T(8,128)(2,1)}, bf16[5,1024,256]{2,1,0:T(8,128)(2,1)}) custom-call(s32[1]{0:T(128)} %bitcast.9.y_ref, bf16[1024,2048]{1,0:T(8,128)(2,1)} %get-tuple-element.381.refs_0_, bf16[1024,2048]{1,0:T(8,128)(2,1)} %get-tuple-element.382.refs_1_, bf16[1024,1280]{1,0:T(8,128)(2,1)} %get-tuple-element.383.refs_0_.refs_2_, ...), custom_call_target="tpu_custom_call" | custom-call | flops 10737418240 | bytes 18874368 | tf_op jit(solution)/shard_map/pallas_call | solution.py:989
  414.2 17.3 %shard_map.342 = (bf16[5,1024,256]{2,1,0:T(8,128)(2,1)}, bf16[5,1024,256]{2,1,0:T(8,128)(2,1)}) custom-call(s32[1]{0:T(128)} %bitcast.9.y_ref, bf16[1024,2048]{1,0:T(8,128)(2,1)} %get-tuple-element.381.refs_0_, bf16[1024,2048]{1,0:T(8,128)(2,1)} %get-tuple-element.382.refs_1_, bf16[1024,1280]{1,0:T(8,128)(2,1)} %get-tuple-element.386.refs_1_.refs_2_, ...), custom_call_target="tpu_custom_call" | custom-call | flops 10737418240 | bytes 18874368 | tf_op jit(solution)/shard_map/pallas_call | solution.py:989
  443.3 19.6 %shard_map.344 = (bf16[1024,512]{1,0:T(8,128)(2,1)S(1)}, bf16[4096,512]{1,0:T(8,128)(2,1)S(1)}, bf16[4096,512]{1,0:T(8,128)(2,1)S(1)}) custom-call(s32[8]{0:T(128)S(1)} %add.273.which_ref, bf16[1024,512]{1,0:T(8,128)(2,1)S(1)} %get-tuple-element.317.query_ref, bf16[4096,512]{1,0:T(8,128)(2,1)S(1)} %copy-done.3, bf16[4096,512]{1,0:T(8,128)(2,1)S(1)} %copy-done.5, ...), custom_call_target="tpu_custom_call" | custom-call | flops 2684354560 | bytes 12582912 | tf_op jit(solution)/shard_map/pallas_call | solution.py:230
  474.8 20.0 %shard_map.347 = (bf16[1024,512]{1,0:T(8,128)(2,1)S(1)}, bf16[4096,512]{1,0:T(8,128)(2,1)S(1)}, bf16[4096,512]{1,0:T(8,128)(2,1)S(1)}) custom-call(s32[8]{0:T(128)S(1)} %add.278.which_ref, bf16[1024,512]{1,0:T(8,128)(2,1)S(1)} %get-tuple-element.324.query_ref, bf16[4096,512]{1,0:T(8,128)(2,1)S(1)} %copy-done.3, ...), custom_call_target="tpu_custom_call", output_to_operand_aliasing={{1}: (5, {}), {2}: (6, {})} | custom-call | flops 2684354560 | bytes 12582912 | tf_op jit(solution)/shard_map/pallas_call | solution.py:230
  527.2 10.1 shard_map.349
  546.4 14.5 %shard_map.352 = (bf16[2,1024,256]{2,1,0:T(8,128)(2,1)}, bf16[2,1024,256]{2,1,0:T(8,128)(2,1)}) custom-call(s32[1]{0:T(128)} %bitcast.9.y_ref, bf16[4096,2048]{1,0:T(8,128)(2,1)} %refs_0_.3, bf16[4096,512]{1,0:T(8,128)(2,1)} %copy-done.13), custom_call_target="tpu_custom_call" | custom-call | flops 8589934592 | bytes 23068672 | tf_op jit(solution)/shard_map/pallas_call | solution.py:989
  565.2 14.6 %shard_map.353 = (bf16[2,1024,256]{2,1,0:T(8,128)(2,1)}, bf16[2,1024,256]{2,1,0:T(8,128)(2,1)}) custom-call(s32[1]{0:T(128)} %bitcast.9.y_ref, bf16[4096,2048]{1,0:T(8,128)(2,1)} %refs_0_.3, bf16[4096,512]{1,0:T(8,128)(2,1)} %copy-done.14), custom_call_target="tpu_custom_call" | custom-call | flops 8589934592 | bytes 23068672 | tf_op jit(solution)/shard_map/pallas_call | solution.py:989
  592.6 17.0 %shard_map.355.refs_0_.refs_2_ = bf16[1024,1536]{1,0:T(8,128)(2,1)S(1)} custom-call(s32[8]{0:T(128)S(1)} %get-tuple-element.277.length_ref, s32[8]{0:T(128)S(1)} %copy-done.30, bf16[1024,1536]{1,0:T(8,128)(2,1)S(1)} %copy-done.9, bf16[1024,512]{1,0:T(8,128)(2,1)S(1)} %get-tuple-element.447.grad_ref), custom_call_target="tpu_custom_call" | custom-call | flops 1342177280 | bytes 7340032 | tf_op jit(solution)/shard_map/pallas_call | solution.py:188
  635.2 17.0 %shard_map.358.refs_0_.refs_3_ = bf16[1024,1536]{1,0:T(8,128)(2,1)S(1)} custom-call(s32[8]{0:T(128)S(1)} %copy-done.28, s32[8]{0:T(128)S(1)} %copy-done.26, bf16[1024,1536]{1,0:T(8,128)(2,1)S(1)} %copy-done.7, bf16[1024,512]{1,0:T(8,128)(2,1)S(1)} %get-tuple-element.457.grad_ref), custom_call_target="tpu_custom_call" | custom-call | flops 1342177280 | bytes 7340032 | tf_op jit(solution)/shard_map/pallas_call | solution.py:188
  662.6 19.4 %shard_map.360 = bf16[2,6,1024,256]{3,2,1,0:T(8,128)(2,1)} custom-call(bf16[1024,2048]{1,0:T(8,128)(2,1)} %copy-done.50, bf16[1024,2048]{1,0:T(8,128)(2,1)} %copy-done.51, bf16[1024,1536]{1,0:T(8,128)(2,1)} %copy-done.15, bf16[1024,1536]{1,0:T(8,128)(2,1)} %copy-done.16), custom_call_target="tpu_custom_call" | custom-call | flops 12884901888 | bytes 20971520 | tf_op jit(solution)/shard_map/pallas_call | solution.py:948
  715.3 460.5 %shard_map.363 = (bf16[16384,256]{1,0:T(8,128)(2,1)}, bf16[2,23552,256]{2,1,0:T(8,128)(2,1)}) custom-call(bf16[12288,256]{1,0:T(8,128)(2,1)} %bitcast.58, bf16[4096,256]{1,0:T(8,128)(2,1)} %bitcast.62, bf16[5120,256]{1,0:T(8,128)(2,1)} %bitcast.59, bf16[5120,256]{1,0:T(8,128)(2,1)} %bitcast.60, bf16[5120,256]{1,0:T(8,128)(2,1)} %bitcast.61, ...), custom_call_target="tpu_custom_call" | custom-call | flops 16777216 | bytes 130023424 | tf_op jit(solution)/shard_map/pallas_call | solution.py:900
  1192.5 12.3 shard_map.365
  1208.3 14.0 %shard_map.366 = (f32[2048,512]{1,0:T(8,128)}, f32[2048,512]{1,0:T(8,128)}, f32[2048,512]{1,0:T(8,128)}, f32[2048,512]{1,0:T(8,128)}, f32[2048,512]{1,0:T(8,128)}, /*index=5*/f32[2048,512]{1,0:T(8,128)}) custom-call(bf16[2,23552,256]{2,1,0:T(8,128)(2,1)} %get-tuple-element.510.refs_0_.refs_1_.refs_2_.refs_3_.refs_4_.refs_5_.refs_6_.refs_7_.refs_8_.refs_9_, ...), custom_call_target="tpu_custom_call" | custom-call | flops 6291456 | bytes 37748736 | tf_op jit(solution)/shard_map/pallas_call | solution.py:1040
  (411 shorter events, 362.0 us)
Async XLA Ops:
  4.1 33.9 %collective-permute-start.1 = (bf16[256,2048]{1,0:T(8,128)(2,1)S(1)}, bf16[256,2048]{1,0:T(8,128)(2,1)}, u32[]{:S(2)}, u32[]{:S(2)}) collective-permute-start(bf16[256,2048]{1,0:T(8,128)(2,1)S(1)} %get-tuple-element.570.own), channel_id=1, source_target_pairs={{0,1},{1,0},{2,3},{3,2},{4,5},{5,4},{6,7},{7,6},{8,9},{9,8},{10,11... | collective-permute-start | bytes 3145736 | tf_op jit(solution)/shard_map/ppermute | solution.py:567
  4.6 33.4 %collective-permute-start = (bf16[256,2048]{1,0:T(8,128)(2,1)S(1)}, bf16[256,2048]{1,0:T(8,128)(2,1)}, u32[]{:S(2)}, u32[]{:S(2)}) collective-permute-start(bf16[256,2048]{1,0:T(8,128)(2,1)S(1)} %get-tuple-element.570.own), channel_id=1, source_target_pairs={{0,2},{1,3},{2,0},{3,1},{4,6},{5,7},{6,4},{7,5},{8,10},{9,11},{10,... | collective-permute-start | bytes 3145736 | tf_op jit(solution)/shard_map/ppermute | solution.py:567
  263.3 29.9 %collective-permute-start.19 = (bf16[256,2048]{1,0:T(8,128)(2,1)S(1)}, bf16[256,2048]{1,0:T(8,128)(2,1)S(1)}, u32[]{:S(2)}, u32[]{:S(2)}) collective-permute-start(bf16[256,2048]{1,0:T(8,128)(2,1)S(1)} %multiply_convert_fusion.refs_0_), channel_id=1, source_target_pairs={{0,2},{1,3},{2,0},{3,1},{4,6},{5,7},{6,4},{7,5},{8,10},{9,11},{10,... | collective-permute-start | bytes 3145736 | tf_op jit(solution)/shard_map/ppermute | solution.py:567
  357.1 38.4 %collective-permute-start.25 = (bf16[256,2048]{1,0:T(8,128)(2,1)S(1)}, bf16[256,2048]{1,0:T(8,128)(2,1)S(1)}, u32[]{:S(2)}, u32[]{:S(2)}) collective-permute-start(bf16[256,2048]{1,0:T(8,128)(2,1)S(1)} %get-tuple-element.391.own), channel_id=1, source_target_pairs={{0,1},{1,0},{2,3},{3,2},{4,5},{5,4},{6,7},{7,6},{8,9},{9,8},{10,11... | collective-permute-start | bytes 3145736 | tf_op jit(solution)/shard_map/ppermute | solution.py:567
  357.2 38.3 %collective-permute-start.24 = (bf16[256,2048]{1,0:T(8,128)(2,1)S(1)}, bf16[256,2048]{1,0:T(8,128)(2,1)S(1)}, u32[]{:S(2)}, u32[]{:S(2)}) collective-permute-start(bf16[256,2048]{1,0:T(8,128)(2,1)S(1)} %get-tuple-element.391.own), channel_id=1, source_target_pairs={{0,2},{1,3},{2,0},{3,1},{4,6},{5,7},{6,4},{7,5},{8,10},{9,11},{10,... | collective-permute-start | bytes 3145736 | tf_op jit(solution)/shard_map/ppermute | solution.py:567
  395.5 36.0 %collective-permute-start.26 = (bf16[256,2048]{1,0:T(8,128)(2,1)}, bf16[256,2048]{1,0:T(8,128)(2,1)}, u32[]{:S(2)}, u32[]{:S(2)}) collective-permute-start(bf16[256,2048]{1,0:T(8,128)(2,1)} %copy-done.42), channel_id=1, source_target_pairs={{0,2},{1,3},{2,0},{3,1},{4,6},{5,7},{6,4},{7,5},{8,10},{9,11},{10,... | collective-permute-start | bytes 3145736 | tf_op jit(solution)/shard_map/ppermute | solution.py:567
  396.6 73.1 %collective-permute-start.29 = (bf16[8,640,256]{2,1,0:T(8,128)(2,1)}, bf16[8,640,256]{2,1,0:T(8,128)(2,1)}, u32[]{:S(2)}, u32[]{:S(2)}) collective-permute-start(bf16[8,640,256]{2,1,0:T(8,128)(2,1)} %get-tuple-element.400), channel_id=1, source_target_pairs={{0,4},{4,0},{8,12},{12,8},{16,20},{20,16},{24,28},{28,24},{1,5},{5... | collective-permute-start | bytes 7864328 | tf_op jit(solution)/shard_map/ppermute | solution.py:567
  438.2 31.5 %collective-permute-start.28 = (bf16[256,2048]{1,0:T(8,128)(2,1)S(1)}, bf16[256,2048]{1,0:T(8,128)(2,1)S(1)}, u32[]{:S(2)}, u32[]{:S(2)}) collective-permute-start(bf16[256,2048]{1,0:T(8,128)(2,1)S(1)} %get-tuple-element.402.own), channel_id=1, source_target_pairs={{0,1},{1,0},{2,3},{3,2},{4,5},{5,4},{6,7},{7,6},{8,9},{9,8},{10,11... | collective-permute-start | bytes 3145736 | tf_op jit(solution)/shard_map/ppermute | solution.py:567
  438.2 31.5 %collective-permute-start.27 = (bf16[256,2048]{1,0:T(8,128)(2,1)S(1)}, bf16[256,2048]{1,0:T(8,128)(2,1)S(1)}, u32[]{:S(2)}, u32[]{:S(2)}) collective-permute-start(bf16[256,2048]{1,0:T(8,128)(2,1)S(1)} %get-tuple-element.402.own), channel_id=1, source_target_pairs={{0,2},{1,3},{2,0},{3,1},{4,6},{5,7},{6,4},{7,5},{8,10},{9,11},{10,... | collective-permute-start | bytes 3145736 | tf_op jit(solution)/shard_map/ppermute | solution.py:567
  468.1 73.9 %collective-permute-start.32 = (bf16[5,1024,256]{2,1,0:T(8,128)(2,1)}, bf16[5,1024,256]{2,1,0:T(8,128)(2,1)}, u32[]{:S(2)}, u32[]{:S(2)}) collective-permute-start(bf16[5,1024,256]{2,1,0:T(8,128)(2,1)} %get-tuple-element.432), channel_id=1, source_target_pairs={{0,4},{4,0},{8,12},{12,8},{16,20},{20,16},{24,28},{28,24},{1,5},{5... | collective-permute-start | bytes 7864328 | tf_op jit(solution)/shard_map/ppermute | solution.py:567
  469.7 41.4 %collective-permute-start.30 = (bf16[256,2048]{1,0:T(8,128)(2,1)S(1)}, bf16[256,2048]{1,0:T(8,128)(2,1)}, u32[]{:S(2)}, u32[]{:S(2)}) collective-permute-start(bf16[256,2048]{1,0:T(8,128)(2,1)S(1)} %get-tuple-element.412), channel_id=1, source_target_pairs={{0,2},{1,3},{2,0},{3,1},{4,6},{5,7},{6,4},{7,5},{8,10},{9,11},{10,... | collective-permute-start | bytes 3145736 | tf_op jit(solution)/shard_map/ppermute | solution.py:567
  470.8 113.6 %collective-permute-start.35 = (bf16[5,1024,256]{2,1,0:T(8,128)(2,1)}, bf16[5,1024,256]{2,1,0:T(8,128)(2,1)}, u32[]{:S(2)}, u32[]{:S(2)}) collective-permute-start(bf16[5,1024,256]{2,1,0:T(8,128)(2,1)} %get-tuple-element.442), channel_id=1, source_target_pairs={{0,4},{4,0},{8,12},{12,8},{16,20},{20,16},{24,28},{28,24},{1,5},{5... | collective-permute-start | bytes 7864328 | tf_op jit(solution)/shard_map/ppermute | solution.py:567
  511.1 30.9 %collective-permute-start.31 = (bf16[256,2048]{1,0:T(8,128)(2,1)S(1)}, bf16[256,2048]{1,0:T(8,128)(2,1)S(1)}, u32[]{:S(2)}, u32[]{:S(2)}) collective-permute-start(bf16[256,2048]{1,0:T(8,128)(2,1)S(1)} %get-tuple-element.418), channel_id=1, source_target_pairs={{0,2},{1,3},{2,0},{3,1},{4,6},{5,7},{6,4},{7,5},{8,10},{9,11},{10,... | collective-permute-start | bytes 3145736 | tf_op jit(solution)/shard_map/ppermute | solution.py:567
  542.0 42.4 %collective-permute-start.34 = (bf16[256,2048]{1,0:T(8,128)(2,1)S(1)}, bf16[256,2048]{1,0:T(8,128)(2,1)S(1)}, u32[]{:S(2)}, u32[]{:S(2)}) collective-permute-start(bf16[256,2048]{1,0:T(8,128)(2,1)S(1)} %get-tuple-element.434.own), channel_id=1, source_target_pairs={{0,1},{1,0},{2,3},{3,2},{4,5},{5,4},{6,7},{7,6},{8,9},{9,8},{10,11... | collective-permute-start | bytes 3145736 | tf_op jit(solution)/shard_map/ppermute | solution.py:567
  542.6 41.8 %collective-permute-start.33 = (bf16[256,2048]{1,0:T(8,128)(2,1)S(1)}, bf16[256,2048]{1,0:T(8,128)(2,1)S(1)}, u32[]{:S(2)}, u32[]{:S(2)}) collective-permute-start(bf16[256,2048]{1,0:T(8,128)(2,1)S(1)} %get-tuple-element.434.own), channel_id=1, source_target_pairs={{0,2},{1,3},{2,0},{3,1},{4,6},{5,7},{6,4},{7,5},{8,10},{9,11},{10,... | collective-permute-start | bytes 3145736 | tf_op jit(solution)/shard_map/ppermute | solution.py:567
  543.6 79.0 %collective-permute-start.38 = (bf16[8,256,256]{2,1,0:T(8,128)(2,1)}, bf16[8,256,256]{2,1,0:T(8,128)(2,1)}, u32[]{:S(2)}, u32[]{:S(2)}) collective-permute-start(bf16[8,256,256]{2,1,0:T(8,128)(2,1)} %get-tuple-element.450), channel_id=1, source_target_pairs={{0,4},{4,0},{8,12},{12,8},{16,20},{20,16},{24,28},{28,24},{1,5},{5... | collective-permute-start | bytes 3145736 | tf_op jit(solution)/shard_map/ppermute | solution.py:567
  545.1 84.2 %collective-permute-start.39 = (bf16[2,1024,256]{2,1,0:T(8,128)(2,1)}, bf16[2,1024,256]{2,1,0:T(8,128)(2,1)}, u32[]{:S(2)}, u32[]{:S(2)}) collective-permute-start(bf16[2,1024,256]{2,1,0:T(8,128)(2,1)} %get-tuple-element.451), channel_id=1, source_target_pairs={{0,4},{4,0},{8,12},{12,8},{16,20},{20,16},{24,28},{28,24},{1,5},{5... | collective-permute-start | bytes 3145736 | tf_op jit(solution)/shard_map/ppermute | solution.py:567
  584.4 44.9 %collective-permute-start.37 = (bf16[256,2048]{1,0:T(8,128)(2,1)}, bf16[256,2048]{1,0:T(8,128)(2,1)S(1)}, u32[]{:S(2)}, u32[]{:S(2)}) collective-permute-start(bf16[256,2048]{1,0:T(8,128)(2,1)} %get-tuple-element.444.own), channel_id=1, source_target_pairs={{0,1},{1,0},{2,3},{3,2},{4,5},{5,4},{6,7},{7,6},{8,9},{9,8},{10,11... | collective-permute-start | bytes 3145736 | tf_op jit(solution)/shard_map/ppermute | solution.py:567
  584.5 44.8 %collective-permute-start.36 = (bf16[256,2048]{1,0:T(8,128)(2,1)}, bf16[256,2048]{1,0:T(8,128)(2,1)S(1)}, u32[]{:S(2)}, u32[]{:S(2)}) collective-permute-start(bf16[256,2048]{1,0:T(8,128)(2,1)} %get-tuple-element.444.own), channel_id=1, source_target_pairs={{0,2},{1,3},{2,0},{3,1},{4,6},{5,7},{6,4},{7,5},{8,10},{9,11},{10,... | collective-permute-start | bytes 3145736 | tf_op jit(solution)/shard_map/ppermute | solution.py:567
  585.5 125.7 %collective-permute-start.42 = (bf16[2,1024,256]{2,1,0:T(8,128)(2,1)}, bf16[2,1024,256]{2,1,0:T(8,128)(2,1)}, u32[]{:S(2)}, u32[]{:S(2)}) collective-permute-start(bf16[2,1024,256]{2,1,0:T(8,128)(2,1)} %get-tuple-element.478), channel_id=1, source_target_pairs={{0,4},{4,0},{8,12},{12,8},{16,20},{20,16},{24,28},{28,24},{1,5},{5... | collective-permute-start | bytes 3145736 | tf_op jit(solution)/shard_map/ppermute | solution.py:567
  622.5 88.7 %collective-permute-start.43 = (bf16[2,1024,256]{2,1,0:T(8,128)(2,1)}, bf16[2,1024,256]{2,1,0:T(8,128)(2,1)}, u32[]{:S(2)}, u32[]{:S(2)}) collective-permute-start(bf16[2,1024,256]{2,1,0:T(8,128)(2,1)} %get-tuple-element.479), channel_id=1, source_target_pairs={{0,4},{4,0},{8,12},{12,8},{16,20},{20,16},{24,28},{28,24},{1,5},{5... | collective-permute-start | bytes 3145736 | tf_op jit(solution)/shard_map/ppermute | solution.py:567
  629.3 52.6 %collective-permute-start.40 = (bf16[256,2048]{1,0:T(8,128)(2,1)}, bf16[256,2048]{1,0:T(8,128)(2,1)}, u32[]{:S(2)}, u32[]{:S(2)}) collective-permute-start(bf16[256,2048]{1,0:T(8,128)(2,1)} %get-tuple-element.454), channel_id=1, source_target_pairs={{0,2},{1,3},{2,0},{3,1},{4,6},{5,7},{6,4},{7,5},{8,10},{9,11},{10,... | collective-permute-start | bytes 3145736 | tf_op jit(solution)/shard_map/ppermute | solution.py:567
  711.2 464.7 %collective-permute-start.44 = (bf16[256,2048]{1,0:T(8,128)(2,1)}, bf16[256,2048]{1,0:T(8,128)(2,1)}, u32[]{:S(2)}, u32[]{:S(2)}) collective-permute-start(bf16[256,2048]{1,0:T(8,128)(2,1)} %get-tuple-element.499), channel_id=1, source_target_pairs={{0,2},{1,3},{2,0},{3,1},{4,6},{5,7},{6,4},{7,5},{8,10},{9,11},{10,... | collective-permute-start | bytes 3145736 | tf_op jit(solution)/shard_map/ppermute | solution.py:567
  712.3 463.6 %collective-permute-start.45 = (bf16[256,2048]{1,0:T(8,128)(2,1)}, bf16[256,2048]{1,0:T(8,128)(2,1)}, u32[]{:S(2)}, u32[]{:S(2)}) collective-permute-start(bf16[256,2048]{1,0:T(8,128)(2,1)} %get-tuple-element.501), channel_id=1, source_target_pairs={{0,2},{1,3},{2,0},{3,1},{4,6},{5,7},{6,4},{7,5},{8,10},{9,11},{10,... | collective-permute-start | bytes 3145736 | tf_op jit(solution)/shard_map/ppermute | solution.py:567
  (131 other events, 2485.5 us)

commit v4 on v3

--- a/solution.py
+++ b/solution.py
@@ -72,21 +72,20 @@
 
 def pair_forward(query, keys, values, mask, first):
     scaled = stack_pair(query * jnp.asarray(HEAD**-0.5, bf16), first)
-    probs = pair_probs(scaled, keys, mask)
-    return unstack_pair(dot_nn(probs.astype(bf16), values), first).astype(bf16)
-
-
-def pair_backward(grad, query, keys, values, mask, first):
+    probs = pair_probs(scaled, keys, mask).astype(bf16)
+    return unstack_pair(dot_nn(probs, values), first).astype(bf16), probs
+
+
+def pair_backward(grad, query, keys, values, probs, first):
     scaled = stack_pair(query * jnp.asarray(HEAD**-0.5, bf16), first)
-    probs = pair_probs(scaled, keys, mask)
     grads = stack_pair(grad, first)
     d_probs = dot_nt(grads, values)
-    d_scores = (
-        probs * (d_probs - jnp.sum(probs * d_probs, axis=-1, keepdims=True))
-    ).astype(bf16)
+    wide = probs.astype(f32)
+    weighted = wide * d_probs
+    d_scores = (weighted - wide * jnp.sum(weighted, axis=-1, keepdims=True)).astype(bf16)
     d_query = unstack_pair(dot_nn(d_scores, keys), first) * HEAD**-0.5
     d_keys = dot_tn(d_scores, scaled)
-    d_values = dot_tn(probs.astype(bf16), grads)
+    d_values = dot_tn(probs, grads)
     return d_query.astype(bf16), d_keys.astype(bf16), d_values.astype(bf16)
 
 
@@ -94,13 +93,13 @@
     return slice(part * width + pair * PAIR, part * width + (pair + 1) * PAIR)
 
 
-def self_forward_kernel(length_ref, prefix_ref, qkv_ref, out_ref):
+def self_forward_kernel(length_ref, prefix_ref, qkv_ref, out_ref, probs_ref):
     at = pl.program_id(0)
     width = out_ref.shape[1]
     first = first_head()
     mask = self_mask(length_ref[at], prefix_ref[at])
     for pair in range(width // PAIR):
-        out_ref[:, lanes(0, width, pair)] = pair_forward(
+        out_ref[:, lanes(0, width, pair)], probs_ref[0, pair] = pair_forward(
             qkv_ref[:, lanes(0, width, pair)],
             qkv_ref[:, lanes(1, width, pair)],
             qkv_ref[:, lanes(2, width, pair)],
@@ -109,11 +108,9 @@
         )
 
 
-def self_backward_kernel(length_ref, prefix_ref, qkv_ref, grad_ref, out_ref):
-    at = pl.program_id(0)
+def self_backward_kernel(qkv_ref, probs_ref, grad_ref, out_ref):
     width = grad_ref.shape[1]
     first = first_head()
-    mask = self_mask(length_ref[at], prefix_ref[at])
     for pair in range(width // PAIR):
         for part, value in enumerate(
             pair_backward(
@@ -121,31 +118,36 @@
                 qkv_ref[:, lanes(0, width, pair)],
                 qkv_ref[:, lanes(1, width, pair)],
                 qkv_ref[:, lanes(2, width, pair)],
-                mask,
+                probs_ref[0, pair],
                 first,
             )
         ):
             out_ref[:, lanes(part, width, pair)] = value
 
 
-def cross_forward_kernel(which_ref, query_ref, key_ref, value_ref, out_ref):
+def cross_forward_kernel(which_ref, query_ref, key_ref, value_ref, out_ref, probs_ref):
     width = out_ref.shape[1]
     first = first_head()
     for pair in range(width // PAIR):
         at = lanes(0, width, pair)
-        out_ref[:, at] = pair_forward(
+        out_ref[:, at], probs_ref[0, pair] = pair_forward(
             query_ref[:, at], key_ref[:, at], value_ref[:, at], None, first
         )
 
 
-def cross_backward_kernel(which_ref, query_ref, key_ref, value_ref, grad_ref, *rest):
+def cross_backward_kernel(which_ref, query_ref, key_ref, value_ref, probs_ref, grad_ref, *rest):
     d_query_ref, d_key_ref, d_value_ref = rest[-3:]
     width = query_ref.shape[1]
     first = first_head()
     for pair in range(width // PAIR):
         at = lanes(0, width, pair)
         d_query_ref[:, at], d_key_ref[:, at], d_value_ref[:, at] = pair_backward(
-            grad_ref[:, at], query_ref[:, at], key_ref[:, at], value_ref[:, at], None, first
+            grad_ref[:, at],
+            query_ref[:, at],
+            key_ref[:, at],
+            value_ref[:, at],
+            probs_ref[0, pair],
+            first,
         )
 
 
@@ -163,6 +165,14 @@
         bytes_accessed=moved,
         transcendentals=examples * SEQ * keys * width // HEAD,
     )
+
+
+def probs_spec(width, keys):
+    return pl.BlockSpec((1, width // PAIR, 2 * SEQ, keys), lambda i, *_: (i, 0, 0, 0))
+
+
+def probs_shape(rows, width, keys):
+    return pltpu.HBM((rows // SEQ, width // PAIR, 2 * SEQ, keys), bf16)
 
 
 def self_forward(qkv, length, prefix):
@@ -174,29 +184,29 @@
             num_scalar_prefetch=2,
             grid=(rows // SEQ,),
             in_specs=[by_row(triple)],
-            out_specs=by_row(width),
+            out_specs=[by_row(width), probs_spec(width, SEQ)],
         ),
-        out_shape=jax.ShapeDtypeStruct((rows, width), bf16),
+        out_shape=[
+            jax.ShapeDtypeStruct((rows, width), bf16),
+            probs_shape(rows, width, SEQ),
+        ],
         compiler_params=params(),
-        cost_estimate=attention_cost(rows // SEQ, width, SEQ, 2, rows * width * 8),
+        cost_estimate=attention_cost(rows // SEQ, width, SEQ, 2, rows * width * 12),
     )(length, prefix, qkv)
 
 
-def self_backward(qkv, grad, length, prefix):
+def self_backward(qkv, probs, grad):
     rows, triple = qkv.shape
     width = triple // 3
     return pl.pallas_call(
         self_backward_kernel,
-        grid_spec=pltpu.PrefetchScalarGridSpec(
-            num_scalar_prefetch=2,
-            grid=(rows // SEQ,),
-            in_specs=[by_row(triple), by_row(width)],
-            out_specs=by_row(triple),
-        ),
+        grid=(rows // SEQ,),
+        in_specs=[by_row(triple), probs_spec(width, SEQ), by_row(width)],
+        out_specs=by_row(triple),
         out_shape=jax.ShapeDtypeStruct((rows, triple), bf16),
         compiler_params=params(),
-        cost_estimate=attention_cost(rows // SEQ, width, SEQ, 5, rows * width * 14),
-    )(length, prefix, qkv, grad)
+        cost_estimate=attention_cost(rows // SEQ, width, SEQ, 4, rows * width * 18),
+    )(qkv, probs, grad)
 
 
 def cross_forward(query, keys, values, which, patch):
@@ -208,25 +218,28 @@
             num_scalar_prefetch=1,
             grid=(rows // SEQ,),
             in_specs=[by_row(width), by_patch, by_patch],
-            out_specs=by_row(width),
+            out_specs=[by_row(width), probs_spec(width, patch)],
         ),
-        out_shape=jax.ShapeDtypeStruct((rows, width), bf16),
+        out_shape=[
+            jax.ShapeDtypeStruct((rows, width), bf16),
+            probs_shape(rows, width, patch),
+        ],
         compiler_params=params(),
-        cost_estimate=attention_cost(rows // SEQ, width, patch, 2, rows * width * 12),
+        cost_estimate=attention_cost(rows // SEQ, width, patch, 2, rows * width * 20),
     )(which, query, keys, values)
 
 
-def cross_backward(query, keys, values, grad, which, patch, earlier):
+def cross_backward(query, keys, values, probs, grad, which, patch, earlier):
     rows, width = query.shape
     by_patch = pl.BlockSpec((patch, width), lambda i, which: (which[i], 0))
-    in_specs = [by_row(width), by_patch, by_patch, by_row(width)]
-    operands = [which, query, keys, values, grad]
+    in_specs = [by_row(width), by_patch, by_patch, probs_spec(width, patch), by_row(width)]
+    operands = [which, query, keys, values, probs, grad]
     aliases = {}
     for at, item in enumerate(earlier):
         in_specs.append(pl.BlockSpec(memory_space=pl.ANY))
         aliases[len(operands)] = 1 + at
         operands.append(item)
-    whole = jax.ShapeDtypeStruct(keys.shape, bf16)
+    whole = pltpu.HBM(keys.shape, bf16)
     return pl.pallas_call(
         cross_backward_kernel,
         grid_spec=pltpu.PrefetchScalarGridSpec(
@@ -238,7 +251,7 @@
         out_shape=[jax.ShapeDtypeStruct((rows, width), bf16), whole, whole],
         input_output_aliases=aliases,
         compiler_params=params(),
-        cost_estimate=attention_cost(rows // SEQ, width, patch, 5, rows * width * 24),
+        cost_estimate=attention_cost(rows // SEQ, width, patch, 4, rows * width * 32),
     )(*operands)
 
 
@@ -314,9 +327,9 @@
     return pl.pallas_call(
         partial(gathered_kernel, transposed, 512),
         in_specs=[IN_VMEM] * 4,
-        out_specs=[pl.BlockSpec(memory_space=pl.ANY), IN_VMEM],
+        out_specs=[pl.BlockSpec(memory_space=pltpu.HBM), IN_VMEM],
         out_shape=[
-            jax.ShapeDtypeStruct((4 * rows, model), bf16),
+            pltpu.HBM((4 * rows, model), bf16),
             jax.ShapeDtypeStruct((4 * rows, units), bf16),
         ],
         scratch_shapes=[
@@ -503,9 +516,9 @@
     whole = pl.BlockSpec((rows, model), lambda i: (0, 0))
     columns = pl.BlockSpec((model, tile), lambda i: (0, i))
     out = pl.BlockSpec((4 * rows, tile), lambda i: (0, i))
-    full = pl.BlockSpec(memory_space=pl.ANY)
+    full = pl.BlockSpec(memory_space=pltpu.HBM)
     shape = jax.ShapeDtypeStruct((4 * rows, units), bf16)
-    full_shape = jax.ShapeDtypeStruct((4 * rows, model), bf16)
+    full_shape = pltpu.HBM((4 * rows, model), bf16)
     return pl.pallas_call(
         partial(gathered_mlp_kernel, units // tile),
         grid=(units // tile,),
@@ -630,12 +643,14 @@
         self.make().wait_recv()
 
 
-def sum_kernel(cycles, open_count, paired_count, *refs):
-    inputs, refs = refs[: open_count + 2 * paired_count], refs[open_count + 2 * paired_count :]
-    open_in = inputs[:open_count]
-    paired_in = inputs[open_count : open_count + paired_count]
-    arrived_in = inputs[open_count + paired_count :]
-    open_out, paired_out = refs[:2]
+def sum_kernel(cycles, paired_count, late, *refs):
+    inputs, refs = refs[: 8 + 2 * paired_count], refs[8 + 2 * paired_count :]
+    factors = (inputs[0:4], inputs[4:8])
+    paired_in = inputs[8 : 8 + paired_count]
+    arrived_in = list(inputs[8 + paired_count :])
+    late_other = arrived_in[late]
+    open_out, paired_out, late_arrived = refs[:3]
+    arrived_in[late] = late_arrived
     (
         opened,
         paired,
@@ -650,7 +665,11 @@
         fill_sem,
         ring,
         ring_sem,
-    ) = refs[2:]
+        factor,
+        factor_sem,
+        late_send,
+        late_recv,
+    ) = refs[3:]
     at = lax.axis_index("dp")
     y = lax.rem(at, 2)
     z = lax.div(at, 2)
@@ -662,6 +681,9 @@
     side = z - 1
     paired_chunks = paired.shape[0] // CHUNK
 
+    def rows_of(index):
+        return pl.ds(pl.multiple_of(index * CHUNK, CHUNK), CHUNK)
+
     barrier = pltpu.get_barrier_semaphore()
 
     def greet(target):
@@ -671,14 +693,68 @@
     greet(along)
 
     fills = []
-    for sources, target in ((open_in, opened), (paired_in, paired)):
-        start = 0
-        for source in sources:
-            place = target.at[pl.ds(start, source.shape[0])]
-            fills.append(pltpu.make_async_copy(source, place, fill_sem.at[len(fills)]))
-            start += source.shape[0]
+    start = 0
+    for source in paired_in:
+        place = paired.at[pl.ds(start, source.shape[0])]
+        fills.append(pltpu.make_async_copy(source, place, fill_sem.at[len(fills)]))
+        start += source.shape[0]
     for fill in fills:
         fill.start()
+
+    first_height, first_width = factors[0][0].shape[1], factors[0][2].shape[1]
+    first_pieces = first_width // WIDE
+    first_groups = first_height * first_width // (CHUNK * WIDE * 4)
+    second_pieces = factors[1][2].shape[1] // WIDE
+    chunk_count = cycles * 8
+
+    def place_of(number):
+        group = (number // 4 % 2) * cycles + number // 8
+        return group, number % 4
+
+    def factor_copies(which, left_at, right_at, slot):
+        copies = []
+        for at in range(4):
+            column = left_at if at < 2 else right_at
+            columns = pl.ds(pl.multiple_of(column * WIDE, WIDE), WIDE)
+            copies.append(
+                pltpu.make_async_copy(
+                    factors[which][at].at[:, columns], factor.at[slot, at], factor_sem.at[slot, at]
+                )
+            )
+        return copies
+
+    def load(number):
+        group, member = place_of(number)
+        slot = lax.rem(number, 2)
+
+        @pl.when((number < chunk_count) & (group < first_groups))
+        def _():
+            left = (group // first_pieces) * (first_height // 2 // WIDE) + member
+            for copy in factor_copies(0, left, group % first_pieces, slot):
+                copy.start()
+
+        @pl.when((number < chunk_count) & (group >= first_groups))
+        def _():
+            chunk = (group - first_groups) * 4 + member
+            for copy in factor_copies(1, chunk // second_pieces, chunk % second_pieces, slot):
+                copy.start()
+
+    def multiply(number):
+        group, member = place_of(number)
+        slot = lax.rem(number, 2)
+        load(number + 1)
+        for copy in factor_copies(0, 0, 0, slot):
+            copy.wait()
+        product = dot_tn(factor[slot, 0], factor[slot, 2]) + dot_tn(
+            factor[slot, 1], factor[slot, 3]
+        )
+        opened[rows_of(group * 4 + member), :] = product.astype(bf16)
+
+    load(0)
+
+    @pl.loop(0, 8)
+    def _(number):
+        multiply(number)
 
     @pl.when(inner)
     def _():
@@ -772,9 +848,6 @@
 
     def nothing():
         return None
-
-    def rows_of(index):
-        return pl.ds(pl.multiple_of(index * CHUNK, CHUNK), CHUNK)
 
     def open_stages(stream, cycle):
         first = (stream * cycles + cycle) * 4
@@ -874,11 +947,38 @@
                 if offset in (2 + index, 3 + index, 5 + index, 7 + index, LAST_HOP[index]):
                     pl.when(chunk < paired_chunks)(each)
 
+    def late_copy(piece):
+        rows = rows_of(piece)
+        return pltpu.make_async_remote_copy(
+            src_ref=late_other.at[rows],
+            dst_ref=late_arrived.at[rows],
+            send_sem=late_send.at[piece],
+            recv_sem=late_recv.at[piece],
+            device_id={"dp": beside},
+            device_id_type=MESH,
+        )
+
+    late_count = late_other.shape[0] // CHUNK
+
     def body(step, carry):
         for phase in range(PERIOD):
+            if phase == 0:
+
+                @pl.when(step == 1)
+                def _():
+                    @pl.loop(0, late_count)
+                    def _(piece):
+                        late_copy(piece).wait()
 
             @pl.loop(0, 2)
             def _(stream):
+                if phase in (0, 2, 4, 6):
+                    piece = phase + stream
+
+                    @pl.when((step == 0) & (piece < late_count))
+                    def _():
+                        late_copy(piece).start()
+
                 for offset in offsets:
                     if (offset + 1) % PERIOD == phase:
                         run(step, stream, offset, (offset + 1) // PERIOD, 1)
@@ -886,24 +986,33 @@
                     if offset % PERIOD == phase:
                         run(step, stream, offset, offset // PERIOD, 0)
 
+            if phase < 8:
+                number = (step + 1) * 8 + phase
+                pl.when(number < chunk_count)(partial(multiply, number))
+
         return carry
 
     lax.fori_loop(0, cycles + 2, body, 0)
 
 
-def sum_chunks(opened, paired, arrived):
-    open_rows = sum(item.shape[0] for item in opened)
+def sum_chunks(factors, paired, arrived, late):
+    open_rows = sum(item[0].shape[1] * item[2].shape[1] // WIDE for item in factors)
     paired_rows = sum(item.shape[0] for item in paired)
+    depth = factors[0][0].shape[0]
     cycles = open_rows // (CHUNK * 8)
     chunks = paired_rows // CHUNK
+    late_chunks = paired[late].shape[0] // CHUNK
+    late_first = sum(item.shape[0] for item in paired[:late]) // CHUNK % (cycles * PAIRED)
     assert cycles * CHUNK * 8 == open_rows and chunks <= 2 * cycles * PAIRED
+    assert late_chunks <= 8 and 3 * PAIRED <= late_first <= cycles * PAIRED - late_chunks
     return pl.pallas_call(
-        partial(sum_kernel, cycles, len(opened), len(paired)),
-        in_specs=[pl.BlockSpec(memory_space=pl.ANY)] * (len(opened) + 2 * len(paired)),
-        out_specs=[pl.BlockSpec(memory_space=pl.ANY)] * 2,
+        partial(sum_kernel, cycles, len(paired), late),
+        in_specs=[pl.BlockSpec(memory_space=pl.ANY)] * (8 + 2 * len(paired)),
+        out_specs=[pl.BlockSpec(memory_space=pl.ANY)] * 3,
         out_shape=[
             jax.ShapeDtypeStruct((open_rows, WIDE), bf16),
             jax.ShapeDtypeStruct((2, paired_rows, WIDE), bf16),
+            jax.ShapeDtypeStruct(paired[late].shape, bf16),
         ],
         scratch_shapes=[
             pltpu.VMEM((open_rows, WIDE), bf16),
@@ -916,49 +1025,23 @@
             pltpu.SemaphoreType.DMA((chunks, 4)),
             pltpu.SemaphoreType.DMA((chunks, 4)),
             pltpu.SemaphoreType.DMA((chunks,)),
-            pltpu.SemaphoreType.DMA((len(opened) + len(paired),)),
+            pltpu.SemaphoreType.DMA((len(paired),)),
             pltpu.VMEM((2, PAIRED, CHUNK, WIDE), bf16),
             pltpu.SemaphoreType.DMA((2, PAIRED)),
+            pltpu.VMEM((2, 4, depth, WIDE), bf16),
+            pltpu.SemaphoreType.DMA((2, 4)),
+            pltpu.SemaphoreType.DMA((8,)),
+            pltpu.SemaphoreType.DMA((8,)),
         ],
         compiler_params=pltpu.CompilerParams(
             collective_id=0, has_side_effects=True, vmem_limit_bytes=63 * 1024 * 1024
         ),
         cost_estimate=pl.CostEstimate(
-            flops=open_rows * WIDE * 4,
+            flops=open_rows * WIDE * 4 * depth,
             bytes_accessed=(open_rows + 2 * paired_rows) * WIDE * 8,
             transcendentals=0,
         ),
-    )(*opened, *paired, *arrived)
-
-
-def weight_grad_kernel(count, *refs):
-    lefts, rights, out = refs[:count], refs[count : 2 * count], refs[-1]
-    total = sum(dot_tn(left[...], right[...]) for left, right in zip(lefts, rights))
-    for piece in range(out.shape[1]):
-        out[0, piece] = total[:, piece * WIDE : (piece + 1) * WIDE].astype(bf16)
-
-
-def weight_grad(lefts, rights):
-    depth, height = lefts[0].shape
-    width = rights[0].shape[1]
-    half, pieces = height // 2, width // WIDE
-    tile = half if half <= 640 else 512
-    steps = half // tile
-    count = len(lefts)
-    return pl.pallas_call(
-        partial(weight_grad_kernel, count),
-        grid=(2 * steps,),
-        in_specs=[pl.BlockSpec((depth, tile), lambda i: (0, i))] * count
-        + [pl.BlockSpec((depth, width), lambda i: (0, 0))] * count,
-        out_specs=pl.BlockSpec((1, pieces, tile, WIDE), lambda i: (i // steps, 0, i % steps, 0)),
-        out_shape=jax.ShapeDtypeStruct((2, pieces, half, WIDE), bf16),
-        compiler_params=pltpu.CompilerParams(vmem_limit_bytes=VMEM_LIMIT),
-        cost_estimate=pl.CostEstimate(
-            flops=2 * count * depth * height * width,
-            bytes_accessed=2 * (count * depth * (height + width) + height * width),
-            transcendentals=0,
-        ),
-    )(*lefts, *rights)
+    )(*factors[0], *factors[1], *paired, *arrived)
 
 
 def side_grads_kernel(steps, count, y_ref, *refs):
@@ -1134,6 +1217,7 @@
     norm_one = [item[0] for item in norm_one]
 
     none = [None] * batches
+    self_probs, cross_probs = list(none), list(none)
     full_one, qkv, mixed_self, x_one, norm_two, scale_two = ([None] * batches for _ in range(6))
     full_two, query, mixed_cross, x_two, norm_three, scale_three = (
         [None] * batches for _ in range(6)
@@ -1148,7 +1232,7 @@
 
     def self_block(b, arrived):
         full_one[b], qkv[b] = gathered_dot(norm_one[b], arrived, w_qkv, False, 1)
-        mixed_self[b] = self_forward(qkv[b], lengths[b], prefixes[b])
+        mixed_self[b], self_probs[b] = self_forward(qkv[b], lengths[b], prefixes[b])
         return scattered_dot([mixed_self[b]], [o_self], False, True, 2)
 
     def self_norm(b, arrived):
@@ -1157,7 +1241,7 @@
 
     def cross_block(b, arrived, keys, values):
         full_two[b], query[b] = gathered_dot(norm_two[b], arrived, q_cross, False, 3)
-        mixed_cross[b] = cross_forward(query[b], keys, values, which[b], patch)
+        mixed_cross[b], cross_probs[b] = cross_forward(query[b], keys, values, which[b], patch)
         return scattered_dot([mixed_cross[b]], [o_cross], False, True, 4)
 
     def cross_norm(b, arrived):
@@ -1182,7 +1266,7 @@
     def cross_back(b, own, arrived, keys, values, earlier):
         grad_two[b], d_mixed = gathered_dot(own, arrived, o_cross, True, 7)
         d_query[b], *d_kv = cross_backward(
-            query[b], keys, values, d_mixed, which[b], patch, earlier
+            query[b], keys, values, cross_probs[b], d_mixed, which[b], patch, earlier
         )
         return scattered_dot([d_query[b]], [q_cross], True, False, 8), d_kv
 
@@ -1195,7 +1279,7 @@
 
     def self_back(b, own, arrived):
         grad_one[b], d_mixed = gathered_dot(own, arrived, o_self, True, 9)
-        d_qkv[b] = self_backward(qkv[b], d_mixed, lengths[b], prefixes[b])
+        d_qkv[b] = self_backward(qkv[b], self_probs[b], d_mixed)
         return scattered_dot([d_qkv[b]], [w_qkv], True, False, 10)
 
     def self_norm_back(b, arrived):
@@ -1256,16 +1340,16 @@
         grads[1], got[1], sent[0] = fence(grads[1], got[1], sent[0])
         back[0] = scatter_move(sent[0])
         mlp_block(1, got[1], grads[1])
-        back[0], d_gate[1], d_up[1], hidden = fence(back[0], d_gate[1], d_up[1], hidden)
+        down_other, down_mine = side_grads(hidden, grad_three)
+        back[0], d_gate[1], d_up[1], down_other = fence(
+            back[0], d_gate[1], d_up[1], down_other
+        )
         own[0] = mlp_norm_back(0, back[0])
         got[0] = gather_start(own[0])
+        down_sent = flip(down_other, "dp", 1)
         sent[1] = mlp_back(1)
-        down_other, down_mine = side_grads(hidden, grad_three)
-        own[0], got[0], sent[1], d_gate, d_up, down_other = fence(
-            own[0], got[0], sent[1], d_gate, d_up, down_other
-        )
+        own[0], got[0], sent[1], d_gate, d_up = fence(own[0], got[0], sent[1], d_gate, d_up)
         back[1] = scatter_move(sent[1])
-        down_sent = flip(down_other, "dp", 1)
         gate_other, gate_mine = side_grads(full_three, d_gate)
         up_other, up_mine = side_grads(full_three, d_up)
         back[1], gate_other, up_other = fence(back[1], gate_other, up_other)
@@ -1291,37 +1375,36 @@
             own[0], back[1], d_kv, o_other, q_other, shown[0], gate_sent, down_mine
         )
         got[0] = gather_start(own[0])
-        o_sent, q_sent = flip(o_other, "dp", 1), flip(q_other, "dp", 1)
         own[1] = cross_norm_back(1, back[1])
         k_other, k_mine = side_grads([patches], [d_kv[0]])
         v_other, v_mine = side_grads([patches], [d_kv[1]])
-        got[0], own[1], k_other, v_other, hidden, up_sent, gate_mine = fence(
-            got[0], own[1], k_other, v_other, hidden, up_sent, gate_mine
+        got[0], own[1], k_other, v_other, hidden, gate_mine = fence(
+            got[0], own[1], k_other, v_other, hidden, gate_mine
         )
         got[1] = gather_start(own[1])
-        k_sent, v_sent = flip(k_other, "dp", 1), flip(v_other, "dp", 1)
+        o_sent = flip(o_other, "dp", 1)
         sent[0] = self_back(0, own[0], got[0])
-        got[1], sent[0], o_sent, q_sent, up_mine = fence(got[1], sent[0], o_sent, q_sent, up_mine)
+        got[1], sent[0], up_sent, o_sent, q_other = fence(
+            got[1], sent[0], up_sent, o_sent, q_other
+        )
+        q_sent = flip(q_other, "dp", 1)
         back[0] = scatter_move(sent[0])
         sent[1] = self_back(1, own[1], got[1])
-        back[0], sent[1], mixed_self, hidden, o_mine, q_mine = fence(
-            back[0], sent[1], mixed_self, hidden, o_mine, q_mine
-        )
+        back[0], sent[1], mixed_self, hidden, q_sent, k_other = fence(
+            back[0], sent[1], mixed_self, hidden, q_sent, k_other
+        )
+        k_sent = flip(k_other, "dp", 1)
         back[1] = scatter_move(sent[1])
         self_norm_back(0, back[0])
-        d_oself = weight_grad(mixed_self, grad_one)
-        d_wqkv = weight_grad(full_one, d_qkv)
         shown[1] = project_out(1)
-        back[1], grad_input[0], d_wqkv, d_oself, shown, k_sent, v_sent = fence(
-            back[1], grad_input[0], d_wqkv, d_oself, shown, k_sent, v_sent
-        )
+        back[1], grad_input[0], shown, k_sent = fence(back[1], grad_input[0], shown, k_sent)
         self_norm_back(1, back[1])
         back = [scatter_move(shown[b]) for b in each_batch]
-        opened = [d_wqkv, d_oself]
+        factors = [[*full_one, *d_qkv], [*mixed_self, *grad_one]]
         paired = [down_mine, gate_mine, up_mine, q_mine, k_mine, v_mine, o_mine]
-        arrived = [down_sent, gate_sent, up_sent, q_sent, k_sent, v_sent, o_sent]
-        open_sum, paired_sum = sum_chunks(
-            *([stacked(item) for item in items] for items in (opened, paired, arrived))
+        arrived = [down_sent, gate_sent, up_sent, q_sent, k_sent, v_other, o_sent]
+        open_sum, paired_sum, _ = sum_chunks(
+            factors, *([stacked(item) for item in items] for items in (paired, arrived)), 5
         )
     else:
         sent[0] = self_block(0, gather_start(norm_one[0]))

time: 1240 us -> 1200 us (0.968)
  Pallas kernels: 941 us -> 899 us
  waiting for transfers between devices: 122 us -> 144 us
  local copies, waits for them, and re-layouts: 31.7 us -> 14.8 us
    pallas_call x5 -> x3, Pallas kernels: 523 us -> 490 us  [the longest x1 468 us: sum_chunks(): pl.pallas_call(partial(sum_kernel, cycles, len(paired), late), in_specs=[...]
    ppermute x51 -> x50, waiting for transfers between devices: 122 us -> 144 us  [flip(): return lax.ppermute(tensor, axis, [(i, i ^ bit) for i in range(count)])]
    unnamed x208 -> x192, local copies, waits for them, and re-layouts: 27.6 us -> 10.7 us
    ppermute x51 -> x50, starting transfers between devices: 40.3 us -> 38.5 us  [flip(): return lax.ppermute(tensor, axis, [(i, i ^ bit) for i in range(count)])]
  transfers between devices with their start and end apart: 51 -> 50, of which waited for: 16 -> 19; matrix products, arithmetic and copies ran while one was open for 7% -> 7% of each run, Pallas kernels for 76% -> 76%
where the time goes in v4:
time: 1200 us; the launch traced here: 1190 us
  Pallas kernels  899 us (75%)
  waiting for transfers between devices  144 us (12%)
  other arithmetic  64.3 us (5%)
  starting transfers between devices  38.5 us (3%)
  matrix products  25.6 us (2%)
  local copies, waits for them, and re-layouts  14.8 us (1%)
    pallas_call x1, Pallas kernels, sum_chunks(): pl.pallas_call(partial(sum_kernel, cycles, len(paired), late), in_specs=[...  468 us
    ppermute x50, waiting for transfers between devices, flip(): return lax.ppermute(tensor, axis, [(i, i ^ bit) for i in range(count)])  144 us
    pallas_call x12, Pallas kernels, scattered_dot(): pl.pallas_call(partial(scattered_kernel, transposed, len(lefts), size), i...  103 us
    pallas_call x7, Pallas kernels, side_grads(): pl.pallas_call(partial(side_grads_kernel, steps, count), grid_spec=pltpu....  101 us
    pallas_call x2, Pallas kernels, gathered_mlp(): pl.pallas_call(partial(gathered_mlp_kernel, units // tile), grid=(units /...  57.2 us
    pallas_call x8, Pallas kernels, gathered_dot(): pl.pallas_call(partial(gathered_kernel, transposed, 512), in_specs=[IN_VM...  41 us
    pallas_call x4, Pallas kernels, unpack(): pl.pallas_call(partial(unpack_kernel, pieces), grid=(2, steps), in_specs=...  39.5 us
    ppermute x50, starting transfers between devices, flip(): return lax.ppermute(tensor, axis, [(i, i ^ bit) for i in range(count)])  38.5 us
  transfers between devices with their start and end apart: 50, of which 19 were waited for; matrix products, arithmetic and copies ran while one was open for 7% of the time, Pallas kernels for 76%

profile of v4, /device:TPU:0, one launch (start us, length us, event | category | flops | bytes accessed | tf_op | source)
XLA Modules:
  0.0 1188.8 jit_solution(10097301060227429844)
XLA Ops:
  89.7 12.9 %fusion.key_ref = bf16[4096,512]{1,0:T(8,128)(2,1)S(1)} fusion(bf16[4096,2048]{1,0:T(8,128)(2,1)} %refs_0_.3, bf16[2048,512]{1,0:T(8,128)(2,1)S(1)} %copy-done.79), kind=kOutput, calls=%fused_computation.7 | convolution fusion | flops 8592031744 | bytes 23068672 | tf_op jit(solution)/shard_map/dot_general | solution.py:21
  102.7 11.3 collective-permute-done.9
  114.5 12.7 %fusion.1.value_ref = bf16[4096,512]{1,0:T(8,128)(2,1)S(1)} fusion(bf16[4096,2048]{1,0:T(8,128)(2,1)} %refs_0_.3, bf16[2048,512]{1,0:T(8,128)(2,1)S(1)} %copy-done.80), kind=kOutput, calls=%fused_computation.8 | convolution fusion | flops 8592031744 | bytes 23068672 | tf_op jit(solution)/shard_map/dot_general | solution.py:21
  140.6 22.9 %collective-permute-done.11.across = bf16[256,2048]{1,0:T(8,128)(2,1)S(1)} collective-permute-done((bf16[256,2048]{1,0:T(8,128)(2,1)S(1)}, bf16[256,2048]{1,0:T(8,128)(2,1)S(1)}, u32[]{:S(2)}, u32[]{:S(2)}) %collective-permute-start.11) | collective-permute-done | bytes 1048608 | tf_op jit(solution)/shard_map/ppermute | solution.py:580
  193.3 10.3 shard_map.334
  215.2 22.5 %collective-permute-done.16 = bf16[256,2048]{1,0:T(8,128)(2,1)S(1)} collective-permute-done((bf16[256,2048]{1,0:T(8,128)(2,1)S(1)}, bf16[256,2048]{1,0:T(8,128)(2,1)S(1)}, u32[]{:S(2)}, u32[]{:S(2)}) %collective-permute-start.16) | collective-permute-done | bytes 1048608 | tf_op jit(solution)/shard_map/ppermute | solution.py:580
  240.4 22.9 %collective-permute-done.17.refs_2_ = bf16[256,2048]{1,0:T(8,128)(2,1)S(1)} collective-permute-done((bf16[256,2048]{1,0:T(8,128)(2,1)S(1)}, bf16[256,2048]{1,0:T(8,128)(2,1)S(1)}, u32[]{:S(2)}, u32[]{:S(2)}) %collective-permute-start.17) | collective-permute-done | bytes 1048608 | tf_op jit(solution)/shard_map/ppermute | solution.py:580
  264.3 28.6 %shard_map.336 = (bf16[1024,2048]{1,0:T(8,128)(2,1)}, bf16[1024,2048]{1,0:T(8,128)(2,1)}, bf16[1024,1280]{1,0:T(8,128)(2,1)}, bf16[1024,1280]{1,0:T(8,128)(2,1)}, bf16[1024,1280]{1,0:T(8,128)(2,1)}) custom-call(bf16[256,2048]{1,0:T(8,128)(2,1)} %copy-done.62, bf16[256,2048]{1,0:T(8,128)(2,1)} %copy-done.90, bf16[256,2048]{1,0:T(8,128)(2,1)} %copy-done.91, ...), custom_call_target="tpu_custom_call" | custom-call | flops 16106127360 | bytes 38273024 | tf_op jit(solution)/shard_map/pallas_call | solution.py:522
  297.9 17.7 %shard_map.337 = (f32[256,2048]{1,0:T(8,128)S(1)}, bf16[256,2048]{1,0:T(8,128)(2,1)S(1)}) custom-call(bf16[1024,1280]{1,0:T(8,128)(2,1)S(1)} %copy-done.37, bf16[1024,1280]{1,0:T(8,128)(2,1)} %get-tuple-element.394.refs_1_.refs_2_, bf16[2048,1280]{1,0:T(8,128)(2,1)} %refs_2_.3, bf16[2048,1280]{1,0:T(8,128)(2,1)} %refs_3_.3), custom_call_target="tpu_custom_call" | custom-call | flops 10737418240 | bytes 33554432 | tf_op jit(solution)/shard_map/pallas_call | solution.py:401
  321.8 28.6 %shard_map.338 = (bf16[1024,2048]{1,0:T(8,128)(2,1)}, bf16[1024,2048]{1,0:T(8,128)(2,1)}, bf16[1024,1280]{1,0:T(8,128)(2,1)}, bf16[1024,1280]{1,0:T(8,128)(2,1)}, bf16[1024,1280]{1,0:T(8,128)(2,1)}) custom-call(bf16[256,2048]{1,0:T(8,128)(2,1)} %copy-done.61, bf16[256,2048]{1,0:T(8,128)(2,1)} %copy-done.86, bf16[256,2048]{1,0:T(8,128)(2,1)} %copy-done.87, ...), custom_call_target="tpu_custom_call" | custom-call | flops 16106127360 | bytes 38273024 | tf_op jit(solution)/shard_map/pallas_call | solution.py:522
  350.5 18.6 %shard_map.339 = (bf16[8,640,256]{2,1,0:T(8,128)(2,1)}, bf16[8,640,256]{2,1,0:T(8,128)(2,1)}) custom-call(s32[1]{0:T(128)} %bitcast.9.y_ref, bf16[1024,1280]{1,0:T(8,128)(2,1)} %get-tuple-element.438.refs_0_, bf16[1024,1280]{1,0:T(8,128)(2,1)} %get-tuple-element.493.refs_1_.refs_0_, bf16[1024,2048]{1,0:T(8,128)(2,1)} %get-tuple-element.376.refs_2_, ...), custom_call_target="tpu_custom_call" | custom-call | flops 10737418240 | bytes 18874368 | tf_op jit(solution)/shard_map/pallas_call | solution.py:1072
  375.7 18.7 %shard_map.340 = (f32[256,2048]{1,0:T(8,128)S(1)}, bf16[256,2048]{1,0:T(8,128)(2,1)}) custom-call(bf16[1024,1280]{1,0:T(8,128)(2,1)S(1)} %copy-done.38, bf16[1024,1280]{1,0:T(8,128)(2,1)} %get-tuple-element.395.refs_1_.refs_3_, bf16[2048,1280]{1,0:T(8,128)(2,1)} %refs_2_.3, bf16[2048,1280]{1,0:T(8,128)(2,1)} %refs_3_.3), custom_call_target="tpu_custom_call" | custom-call | flops 10737418240 | bytes 33554432 | tf_op jit(solution)/shard_map/pallas_call | solution.py:401
  400.6 17.1 %shard_map.341 = (bf16[5,1024,256]{2,1,0:T(8,128)(2,1)}, bf16[5,1024,256]{2,1,0:T(8,128)(2,1)}) custom-call(s32[1]{0:T(128)} %bitcast.9.y_ref, bf16[1024,2048]{1,0:T(8,128)(2,1)} %get-tuple-element.389.refs_0_, bf16[1024,2048]{1,0:T(8,128)(2,1)} %get-tuple-element.390.refs_1_, bf16[1024,1280]{1,0:T(8,128)(2,1)} %get-tuple-element.391.refs_0_.refs_2_, ...), custom_call_target="tpu_custom_call" | custom-call | flops 10737418240 | bytes 18874368 | tf_op jit(solution)/shard_map/pallas_call | solution.py:1072
  417.7 17.4 %shard_map.342 = (bf16[5,1024,256]{2,1,0:T(8,128)(2,1)}, bf16[5,1024,256]{2,1,0:T(8,128)(2,1)}) custom-call(s32[1]{0:T(128)} %bitcast.9.y_ref, bf16[1024,2048]{1,0:T(8,128)(2,1)} %get-tuple-element.389.refs_0_, bf16[1024,2048]{1,0:T(8,128)(2,1)} %get-tuple-element.390.refs_1_, bf16[1024,1280]{1,0:T(8,128)(2,1)} %get-tuple-element.394.refs_1_.refs_2_, ...), custom_call_target="tpu_custom_call" | custom-call | flops 10737418240 | bytes 18874368 | tf_op jit(solution)/shard_map/pallas_call | solution.py:1072
  447.0 14.9 %shard_map.344 = (bf16[1024,512]{1,0:T(8,128)(2,1)S(1)}, bf16[4096,512]{1,0:T(8,128)(2,1)}, bf16[4096,512]{1,0:T(8,128)(2,1)}) custom-call(s32[8]{0:T(128)S(1)} %add.273.which_ref, bf16[1024,512]{1,0:T(8,128)(2,1)S(1)} %get-tuple-element.321.query_ref, bf16[4096,512]{1,0:T(8,128)(2,1)S(1)} %copy-done.3, bf16[4096,512]{1,0:T(8,128)(2,1)S(1)} %copy-done.5, ...), custom_call_target="tpu_custom_call" | custom-call | flops 2147483648 | bytes 16777216 | tf_op jit(solution)/shard_map/pallas_call | solution.py:243
  474.1 14.9 %shard_map.347 = (bf16[1024,512]{1,0:T(8,128)(2,1)S(1)}, bf16[4096,512]{1,0:T(8,128)(2,1)}, bf16[4096,512]{1,0:T(8,128)(2,1)}) custom-call(s32[8]{0:T(128)S(1)} %add.278.which_ref, bf16[1024,512]{1,0:T(8,128)(2,1)S(1)} %get-tuple-element.329.query_ref, bf16[4096,512]{1,0:T(8,128)(2,1)S(1)} %copy-done.3, ...), custom_call_target="tpu_custom_call", output_to_operand_aliasing={{1}: (6, {}), {2}: (7, {})} | custom-call | flops 2147483648 | bytes 16777216 | tf_op jit(solution)/shard_map/pallas_call | solution.py:243
  536.6 14.3 %shard_map.352 = (bf16[2,1024,256]{2,1,0:T(8,128)(2,1)}, bf16[2,1024,256]{2,1,0:T(8,128)(2,1)}) custom-call(s32[1]{0:T(128)} %bitcast.9.y_ref, bf16[4096,2048]{1,0:T(8,128)(2,1)} %refs_0_.3, bf16[4096,512]{1,0:T(8,128)(2,1)} %get-tuple-element.446.refs_1_), custom_call_target="tpu_custom_call" | custom-call | flops 8589934592 | bytes 23068672 | tf_op jit(solution)/shard_map/pallas_call | solution.py:1072
  555.8 14.6 %shard_map.353 = (bf16[2,1024,256]{2,1,0:T(8,128)(2,1)}, bf16[2,1024,256]{2,1,0:T(8,128)(2,1)}) custom-call(s32[1]{0:T(128)} %bitcast.9.y_ref, bf16[4096,2048]{1,0:T(8,128)(2,1)} %refs_0_.3, bf16[4096,512]{1,0:T(8,128)(2,1)} %get-tuple-element.448.refs_1_), custom_call_target="tpu_custom_call" | custom-call | flops 8589934592 | bytes 23068672 | tf_op jit(solution)/shard_map/pallas_call | solution.py:1072
  575.8 11.2 shard_map.355.refs_0_.refs_2_
  611.2 11.2 shard_map.358.refs_0_.refs_3_
  646.2 12.1 %collective-permute-done.41 = bf16[256,2048]{1,0:T(8,128)(2,1)S(1)} collective-permute-done((bf16[256,2048]{1,0:T(8,128)(2,1)S(1)}, bf16[256,2048]{1,0:T(8,128)(2,1)S(1)}, u32[]{:S(2)}, u32[]{:S(2)}) %collective-permute-start.41) | collective-permute-done | bytes 1048608 | tf_op jit(solution)/shard_map/ppermute | solution.py:580
  662.1 467.8 %shard_map.361 = (bf16[16384,256]{1,0:T(8,128)(2,1)}, bf16[2,23552,256]{2,1,0:T(8,128)(2,1)}, bf16[2048,256]{1,0:T(8,128)(2,1)}) custom-call(bf16[1024,2048]{1,0:T(8,128)(2,1)} %get-tuple-element.337.refs_0_, bf16[1024,2048]{1,0:T(8,128)(2,1)} %get-tuple-element.338.refs_1_, bf16[1024,1536]{1,0:T(8,128)(2,1)} %copy-done.14, bf16[1024,1536]{1,0:T(8,128)(2,1)} %copy-done.15, ...), custom_call_target="tpu_custom_call" | custom-call | flops 17179869184 | bytes 130023424 | tf_op jit(solution)/shard_map/pallas_call | solution.py:1008
  1148.9 12.3 %shard_map.363 = (f32[2048,1280]{1,0:T(8,128)}, f32[2048,1280]{1,0:T(8,128)}) custom-call(bf16[2,23552,256]{2,1,0:T(8,128)(2,1)} %get-tuple-element.514.refs_0_.refs_1_.refs_2_.refs_3_.refs_4_.refs_5_.refs_6_.refs_7_.refs_8_.refs_9_, bf16[2,23552,256]{2,1,0:T(8,128)(2,1)} %get-tuple-element.514.refs_0_.refs_1_.refs_2_.refs_3_.refs_4_.refs_5_.refs_6_.refs_7_.refs_8_.refs_9_, ...), custom_call_target="tpu_custom_call" | custom-call | flops 5242880 | bytes 31457280 | tf_op jit(solution)/shard_map/pallas_call | solution.py:1123
  1164.7 14.0 %shard_map.364 = (f32[2048,512]{1,0:T(8,128)}, f32[2048,512]{1,0:T(8,128)}, f32[2048,512]{1,0:T(8,128)}, f32[2048,512]{1,0:T(8,128)}, f32[2048,512]{1,0:T(8,128)}, /*index=5*/f32[2048,512]{1,0:T(8,128)}) custom-call(bf16[2,23552,256]{2,1,0:T(8,128)(2,1)} %get-tuple-element.514.refs_0_.refs_1_.refs_2_.refs_3_.refs_4_.refs_5_.refs_6_.refs_7_.refs_8_.refs_9_, ...), custom_call_target="tpu_custom_call" | custom-call | flops 6291456 | bytes 37748736 | tf_op jit(solution)/shard_map/pallas_call | solution.py:1123
  (392 shorter events, 336.7 us)
Async XLA Ops:
  4.1 33.9 %collective-permute-start.1 = (bf16[256,2048]{1,0:T(8,128)(2,1)S(1)}, bf16[256,2048]{1,0:T(8,128)(2,1)S(1)}, u32[]{:S(2)}, u32[]{:S(2)}) collective-permute-start(bf16[256,2048]{1,0:T(8,128)(2,1)S(1)} %get-tuple-element.574.own), channel_id=1, source_target_pairs={{0,1},{1,0},{2,3},{3,2},{4,5},{5,4},{6,7},{7,6},{8,9},{9,8},{10,11... | collective-permute-start | bytes 3145736 | tf_op jit(solution)/shard_map/ppermute | solution.py:580
  4.6 33.4 %collective-permute-start = (bf16[256,2048]{1,0:T(8,128)(2,1)S(1)}, bf16[256,2048]{1,0:T(8,128)(2,1)}, u32[]{:S(2)}, u32[]{:S(2)}) collective-permute-start(bf16[256,2048]{1,0:T(8,128)(2,1)S(1)} %get-tuple-element.574.own), channel_id=1, source_target_pairs={{0,2},{1,3},{2,0},{3,1},{4,6},{5,7},{6,4},{7,5},{8,10},{9,11},{10,... | collective-permute-start | bytes 3145736 | tf_op jit(solution)/shard_map/ppermute | solution.py:580
  38.0 25.6 %collective-permute-start.5 = (bf16[256,2048]{1,0:T(8,128)(2,1)S(1)}, bf16[256,2048]{1,0:T(8,128)(2,1)S(1)}, u32[]{:S(2)}, u32[]{:S(2)}) collective-permute-start(bf16[256,2048]{1,0:T(8,128)(2,1)S(1)} %get-tuple-element.288.own), channel_id=1, source_target_pairs={{0,2},{1,3},{2,0},{3,1},{4,6},{5,7},{6,4},{7,5},{8,10},{9,11},{10,... | collective-permute-start | bytes 3145736 | tf_op jit(solution)/shard_map/ppermute | solution.py:580
  63.6 25.6 %collective-permute-start.7 = (bf16[256,2048]{1,0:T(8,128)(2,1)S(1)}, bf16[256,2048]{1,0:T(8,128)(2,1)S(1)}, u32[]{:S(2)}, u32[]{:S(2)}) collective-permute-start(bf16[256,2048]{1,0:T(8,128)(2,1)S(1)} %get-tuple-element.353.refs_3_), channel_id=1, source_target_pairs={{0,2},{1,3},{2,0},{3,1},{4,6},{5,7},{6,4},{7,5},{8,10},{9,11},{10,... | collective-permute-start | bytes 3145736 | tf_op jit(solution)/shard_map/ppermute | solution.py:580
  137.9 25.6 %collective-permute-start.11 = (bf16[256,2048]{1,0:T(8,128)(2,1)S(1)}, bf16[256,2048]{1,0:T(8,128)(2,1)S(1)}, u32[]{:S(2)}, u32[]{:S(2)}) collective-permute-start(bf16[256,2048]{1,0:T(8,128)(2,1)S(1)} %multiply_convert_fusion.3.own), channel_id=1, source_target_pairs={{0,2},{1,3},{2,0},{3,1},{4,6},{5,7},{6,4},{7,5},{8,10},{9,11},{10,... | collective-permute-start | bytes 3145736 | tf_op jit(solution)/shard_map/ppermute | solution.py:580
  163.5 25.6 %collective-permute-start.13 = (bf16[256,2048]{1,0:T(8,128)(2,1)S(1)}, bf16[256,2048]{1,0:T(8,128)(2,1)S(1)}, u32[]{:S(2)}, u32[]{:S(2)}) collective-permute-start(bf16[256,2048]{1,0:T(8,128)(2,1)S(1)} %multiply_convert_fusion.2.own), channel_id=1, source_target_pairs={{0,2},{1,3},{2,0},{3,1},{4,6},{5,7},{6,4},{7,5},{8,10},{9,11},{10,... | collective-permute-start | bytes 3145736 | tf_op jit(solution)/shard_map/ppermute | solution.py:580
  263.3 29.6 %collective-permute-start.20 = (bf16[256,2048]{1,0:T(8,128)(2,1)S(1)}, bf16[256,2048]{1,0:T(8,128)(2,1)S(1)}, u32[]{:S(2)}, u32[]{:S(2)}) collective-permute-start(bf16[256,2048]{1,0:T(8,128)(2,1)S(1)} %multiply_convert_fusion.refs_0_), channel_id=1, source_target_pairs={{0,1},{1,0},{2,3},{3,2},{4,5},{5,4},{6,7},{7,6},{8,9},{9,8},{10,11... | collective-permute-start | bytes 3145736 | tf_op jit(solution)/shard_map/ppermute | solution.py:580
  263.3 29.6 %collective-permute-start.19 = (bf16[256,2048]{1,0:T(8,128)(2,1)S(1)}, bf16[256,2048]{1,0:T(8,128)(2,1)S(1)}, u32[]{:S(2)}, u32[]{:S(2)}) collective-permute-start(bf16[256,2048]{1,0:T(8,128)(2,1)S(1)} %multiply_convert_fusion.refs_0_), channel_id=1, source_target_pairs={{0,2},{1,3},{2,0},{3,1},{4,6},{5,7},{6,4},{7,5},{8,10},{9,11},{10,... | collective-permute-start | bytes 3145736 | tf_op jit(solution)/shard_map/ppermute | solution.py:580
  295.0 25.8 %collective-permute-start.21 = (bf16[256,2048]{1,0:T(8,128)(2,1)}, bf16[256,2048]{1,0:T(8,128)(2,1)}, u32[]{:S(2)}, u32[]{:S(2)}) collective-permute-start(bf16[256,2048]{1,0:T(8,128)(2,1)} %get-tuple-element.359.refs_3_), channel_id=1, source_target_pairs={{0,2},{1,3},{2,0},{3,1},{4,6},{5,7},{6,4},{7,5},{8,10},{9,11},{10,... | collective-permute-start | bytes 3145736 | tf_op jit(solution)/shard_map/ppermute | solution.py:580
  320.7 48.4 %collective-permute-start.23 = (bf16[256,2048]{1,0:T(8,128)(2,1)S(1)}, bf16[256,2048]{1,0:T(8,128)(2,1)S(1)}, u32[]{:S(2)}, u32[]{:S(2)}) collective-permute-start(bf16[256,2048]{1,0:T(8,128)(2,1)S(1)} %get-tuple-element.367), channel_id=1, source_target_pairs={{0,2},{1,3},{2,0},{3,1},{4,6},{5,7},{6,4},{7,5},{8,10},{9,11},{10,... | collective-permute-start | bytes 3145736 | tf_op jit(solution)/shard_map/ppermute | solution.py:580
  375.2 92.0 %collective-permute-start.29 = (bf16[8,640,256]{2,1,0:T(8,128)(2,1)}, bf16[8,640,256]{2,1,0:T(8,128)(2,1)}, u32[]{:S(2)}, u32[]{:S(2)}) collective-permute-start(bf16[8,640,256]{2,1,0:T(8,128)(2,1)} %get-tuple-element.409), channel_id=1, source_target_pairs={{0,4},{4,0},{8,12},{12,8},{16,20},{20,16},{24,28},{28,24},{1,5},{5... | collective-permute-start | bytes 7864328 | tf_op jit(solution)/shard_map/ppermute | solution.py:580
  399.6 35.4 %collective-permute-start.26 = (bf16[256,2048]{1,0:T(8,128)(2,1)}, bf16[256,2048]{1,0:T(8,128)(2,1)}, u32[]{:S(2)}, u32[]{:S(2)}) collective-permute-start(bf16[256,2048]{1,0:T(8,128)(2,1)} %get-tuple-element.388), channel_id=1, source_target_pairs={{0,2},{1,3},{2,0},{3,1},{4,6},{5,7},{6,4},{7,5},{8,10},{9,11},{10,... | collective-permute-start | bytes 3145736 | tf_op jit(solution)/shard_map/ppermute | solution.py:580
  467.3 36.0 %collective-permute-start.30 = (bf16[256,2048]{1,0:T(8,128)(2,1)S(1)}, bf16[256,2048]{1,0:T(8,128)(2,1)}, u32[]{:S(2)}, u32[]{:S(2)}) collective-permute-start(bf16[256,2048]{1,0:T(8,128)(2,1)S(1)} %get-tuple-element.421), channel_id=1, source_target_pairs={{0,2},{1,3},{2,0},{3,1},{4,6},{5,7},{6,4},{7,5},{8,10},{9,11},{10,... | collective-permute-start | bytes 3145736 | tf_op jit(solution)/shard_map/ppermute | solution.py:580
  468.4 65.7 %collective-permute-start.32 = (bf16[5,1024,256]{2,1,0:T(8,128)(2,1)}, bf16[5,1024,256]{2,1,0:T(8,128)(2,1)}, u32[]{:S(2)}, u32[]{:S(2)}) collective-permute-start(bf16[5,1024,256]{2,1,0:T(8,128)(2,1)} %get-tuple-element.441), channel_id=1, source_target_pairs={{0,4},{4,0},{8,12},{12,8},{16,20},{20,16},{24,28},{28,24},{1,5},{5... | collective-permute-start | bytes 7864328 | tf_op jit(solution)/shard_map/ppermute | solution.py:580
  468.9 127.2 %collective-permute-start.37 = (bf16[5,1024,256]{2,1,0:T(8,128)(2,1)}, bf16[5,1024,256]{2,1,0:T(8,128)(2,1)}, u32[]{:S(2)}, u32[]{:S(2)}) collective-permute-start(bf16[5,1024,256]{2,1,0:T(8,128)(2,1)} %get-tuple-element.459), channel_id=1, source_target_pairs={{0,4},{4,0},{8,12},{12,8},{16,20},{20,16},{24,28},{28,24},{1,5},{5... | collective-permute-start | bytes 7864328 | tf_op jit(solution)/shard_map/ppermute | solution.py:580
  503.3 30.7 %collective-permute-start.31 = (bf16[256,2048]{1,0:T(8,128)(2,1)S(1)}, bf16[256,2048]{1,0:T(8,128)(2,1)S(1)}, u32[]{:S(2)}, u32[]{:S(2)}) collective-permute-start(bf16[256,2048]{1,0:T(8,128)(2,1)S(1)} %get-tuple-element.427), channel_id=1, source_target_pairs={{0,2},{1,3},{2,0},{3,1},{4,6},{5,7},{6,4},{7,5},{8,10},{9,11},{10,... | collective-permute-start | bytes 3145736 | tf_op jit(solution)/shard_map/ppermute | solution.py:580
  535.1 35.3 %collective-permute-start.34 = (bf16[256,2048]{1,0:T(8,128)(2,1)S(1)}, bf16[256,2048]{1,0:T(8,128)(2,1)S(1)}, u32[]{:S(2)}, u32[]{:S(2)}) collective-permute-start(bf16[256,2048]{1,0:T(8,128)(2,1)S(1)} %get-tuple-element.443.own), channel_id=1, source_target_pairs={{0,1},{1,0},{2,3},{3,2},{4,5},{5,4},{6,7},{7,6},{8,9},{9,8},{10,11... | collective-permute-start | bytes 3145736 | tf_op jit(solution)/shard_map/ppermute | solution.py:580
  535.6 34.8 %collective-permute-start.33 = (bf16[256,2048]{1,0:T(8,128)(2,1)S(1)}, bf16[256,2048]{1,0:T(8,128)(2,1)S(1)}, u32[]{:S(2)}, u32[]{:S(2)}) collective-permute-start(bf16[256,2048]{1,0:T(8,128)(2,1)S(1)} %get-tuple-element.443.own), channel_id=1, source_target_pairs={{0,2},{1,3},{2,0},{3,1},{4,6},{5,7},{6,4},{7,5},{8,10},{9,11},{10,... | collective-permute-start | bytes 3145736 | tf_op jit(solution)/shard_map/ppermute | solution.py:580
  553.1 52.8 %collective-permute-start.38 = (bf16[8,256,256]{2,1,0:T(8,128)(2,1)}, bf16[8,256,256]{2,1,0:T(8,128)(2,1)}, u32[]{:S(2)}, u32[]{:S(2)}) collective-permute-start(bf16[8,256,256]{2,1,0:T(8,128)(2,1)} %get-tuple-element.460), channel_id=1, source_target_pairs={{0,4},{4,0},{8,12},{12,8},{16,20},{20,16},{24,28},{28,24},{1,5},{5... | collective-permute-start | bytes 3145736 | tf_op jit(solution)/shard_map/ppermute | solution.py:580
  570.4 35.5 %collective-permute-start.36 = (bf16[256,2048]{1,0:T(8,128)(2,1)S(1)}, bf16[256,2048]{1,0:T(8,128)(2,1)S(1)}, u32[]{:S(2)}, u32[]{:S(2)}) collective-permute-start(bf16[256,2048]{1,0:T(8,128)(2,1)S(1)} %get-tuple-element.456.own), channel_id=1, source_target_pairs={{0,1},{1,0},{2,3},{3,2},{4,5},{5,4},{6,7},{7,6},{8,9},{9,8},{10,11... | collective-permute-start | bytes 3145736 | tf_op jit(solution)/shard_map/ppermute | solution.py:580
  570.5 35.4 %collective-permute-start.35 = (bf16[256,2048]{1,0:T(8,128)(2,1)S(1)}, bf16[256,2048]{1,0:T(8,128)(2,1)S(1)}, u32[]{:S(2)}, u32[]{:S(2)}) collective-permute-start(bf16[256,2048]{1,0:T(8,128)(2,1)S(1)} %get-tuple-element.456.own), channel_id=1, source_target_pairs={{0,2},{1,3},{2,0},{3,1},{4,6},{5,7},{6,4},{7,5},{8,10},{9,11},{10,... | collective-permute-start | bytes 3145736 | tf_op jit(solution)/shard_map/ppermute | solution.py:580
  605.9 25.7 %collective-permute-start.39 = (bf16[256,2048]{1,0:T(8,128)(2,1)S(1)}, bf16[256,2048]{1,0:T(8,128)(2,1)S(1)}, u32[]{:S(2)}, u32[]{:S(2)}) collective-permute-start(bf16[256,2048]{1,0:T(8,128)(2,1)S(1)} %get-tuple-element.466), channel_id=1, source_target_pairs={{0,2},{1,3},{2,0},{3,1},{4,6},{5,7},{6,4},{7,5},{8,10},{9,11},{10,... | collective-permute-start | bytes 3145736 | tf_op jit(solution)/shard_map/ppermute | solution.py:580
  660.1 469.9 %collective-permute-start.43 = (bf16[256,2048]{1,0:T(8,128)(2,1)}, bf16[256,2048]{1,0:T(8,128)(2,1)}, u32[]{:S(2)}, u32[]{:S(2)}) collective-permute-start(bf16[256,2048]{1,0:T(8,128)(2,1)} %get-tuple-element.503), channel_id=1, source_target_pairs={{0,2},{1,3},{2,0},{3,1},{4,6},{5,7},{6,4},{7,5},{8,10},{9,11},{10,... | collective-permute-start | bytes 3145736 | tf_op jit(solution)/shard_map/ppermute | solution.py:580
  661.1 468.9 %collective-permute-start.44 = (bf16[256,2048]{1,0:T(8,128)(2,1)}, bf16[256,2048]{1,0:T(8,128)(2,1)}, u32[]{:S(2)}, u32[]{:S(2)}) collective-permute-start(bf16[256,2048]{1,0:T(8,128)(2,1)} %get-tuple-element.505), channel_id=1, source_target_pairs={{0,2},{1,3},{2,0},{3,1},{4,6},{5,7},{6,4},{7,5},{8,10},{9,11},{10,... | collective-permute-start | bytes 3145736 | tf_op jit(solution)/shard_map/ppermute | solution.py:580
  (122 other events, 2121.6 us)

commit v5 on v4

--- a/solution.py
+++ b/solution.py
@@ -452,104 +452,97 @@
         )
 
 
-def gathered_mlp_kernel(tiles, *refs):
-    norms, grads = refs[:3], refs[3:6]
-    gate_ref, up_ref, down_ref = refs[6:9]
-    full_norm, full_grad, hidden_ref, d_gate_ref, d_up_ref = refs[9:14]
-    corner_norm, corner_grad, sems, local = refs[14:]
+def gathered_tiles_kernel(tiles, extra, body, *refs):
+    blocks, ins, full, outs = refs[:3], refs[3 : 3 + extra], refs[3 + extra], refs[4 + extra : -3]
+    corner, sems, local = refs[-3:]
     tile = pl.program_id(0)
-    rows = norms[0].shape[0]
+    rows = blocks[0].shape[0]
     partner = other_core()
-    norms = (*norms, corner_norm)
-    grads = (*grads, corner_grad)
-
-    def given(at):
-        source, target = ((norms[2], corner_norm), (grads[2], corner_grad))[at]
-        return to_partner(source, target, sems.at[2 * at], sems.at[2 * at + 1], partner)
-
-    def keep(which, at):
-        source, target = ((norms, full_norm), (grads, full_grad))[which]
-        return pltpu.make_async_copy(
-            source[at], target.at[pl.ds(at * rows, rows)], local.at[which, at]
-        )
+    blocks = (*blocks, corner)
+
+    def given():
+        return to_partner(blocks[2], corner, sems.at[0], sems.at[1], partner)
+
+    def keep(at):
+        return pltpu.make_async_copy(blocks[at], full.at[pl.ds(at * rows, rows)], local.at[at])
 
     @pl.when(tile == 0)
     def _():
         meet(partner)
-        for which in range(2):
-            given(which).start()
-        for which in range(2):
-            for at in range(3):
-                keep(which, at).start()
+        given().start()
+        for at in range(3):
+            keep(at).start()
 
     for at in range(4):
         if at == 3:
 
             @pl.when(tile == 0)
             def _():
-                for which in range(2):
-                    given(which).wait()
-                    keep(which, 3).start()
-
-        place = slice(at * rows, (at + 1) * rows)
-        hidden_ref[place, :], d_gate_ref[place, :], d_up_ref[place, :] = mlp_rows(
-            norms[at][...], grads[at][...], gate_ref, up_ref, down_ref
-        )
+                given().wait()
+                keep(3).start()
+
+        body(slice(at * rows, (at + 1) * rows), blocks[at][...], ins, outs)
 
     @pl.when(tile == tiles - 1)
     def _():
-        for which in range(2):
-            for at in range(4):
-                keep(which, at).wait()
-
-
-def gathered_mlp(own_norm, arrived_norm, own_grad, arrived_grad, w_gate, w_up, w_down, ident):
-    model, units = w_gate.shape
-    if lax.axis_size("mp") != 4:
-        return (
-            arrived_norm,
-            arrived_grad,
-            *mlp(arrived_norm, arrived_grad, w_gate, w_up, w_down),
-        )
-    rows = own_norm.shape[0]
+        for at in range(4):
+            keep(at).wait()
+
+
+def up_body(place, norm, ins, outs):
+    gate = dot_nn(norm, ins[0][...])
+    up = dot_nn(norm, ins[1][...])
+    curve = 0.7978845608028654
+    square = gate * gate
+    bend = jnp.tanh(curve * gate * (1.0 + 0.044715 * square))
+    half = 0.5 * (1.0 + bend)
+    value = gate * half
+    slope = half + 0.5 * curve * gate * (1.0 - bend * bend) * (1.0 + 0.134145 * square)
+    outs[0][place, :] = (value * up).astype(bf16)
+    outs[1][place, :] = (up * slope).astype(bf16)
+    outs[2][place, :] = value.astype(bf16)
+
+
+def down_body(place, grad, ins, outs):
+    d_hidden = dot_nt(grad, ins[0][...])
+    outs[0][place, :] = (d_hidden * ins[1][place, :].astype(f32)).astype(bf16)
+    outs[1][place, :] = (d_hidden * ins[2][place, :].astype(f32)).astype(bf16)
+
+
+def gathered_tiles(own, arrived, weights, tiled, body, out_count, ident):
+    across, beside = arrived
+    rows, model = own.shape
+    units = weights[0].shape[1 if body is up_body else 0]
     tile = 256
     whole = pl.BlockSpec((rows, model), lambda i: (0, 0))
-    columns = pl.BlockSpec((model, tile), lambda i: (0, i))
-    out = pl.BlockSpec((4 * rows, tile), lambda i: (0, i))
-    full = pl.BlockSpec(memory_space=pltpu.HBM)
-    shape = jax.ShapeDtypeStruct((4 * rows, units), bf16)
-    full_shape = pltpu.HBM((4 * rows, model), bf16)
+    by_tile = pl.BlockSpec((4 * rows, tile), lambda i: (0, i))
+    weight_specs = [
+        pl.BlockSpec((model, tile), lambda i: (0, i))
+        if body is up_body
+        else pl.BlockSpec((tile, model), lambda i: (i, 0))
+        for _ in weights
+    ]
     return pl.pallas_call(
-        partial(gathered_mlp_kernel, units // tile),
+        partial(gathered_tiles_kernel, units // tile, len(weights) + len(tiled), body),
         grid=(units // tile,),
-        in_specs=[whole] * 6 + [columns, columns, pl.BlockSpec((tile, model), lambda i: (i, 0))],
-        out_specs=[full, full, out, out, out],
-        out_shape=[full_shape, full_shape, shape, shape, shape],
+        in_specs=[whole] * 3 + weight_specs + [by_tile] * len(tiled),
+        out_specs=[pl.BlockSpec(memory_space=pltpu.HBM)] + [by_tile] * out_count,
+        out_shape=[pltpu.HBM((4 * rows, model), bf16)]
+        + [jax.ShapeDtypeStruct((4 * rows, units), bf16)] * out_count,
         scratch_shapes=[
             pltpu.VMEM((rows, model), bf16),
-            pltpu.VMEM((rows, model), bf16),
+            pltpu.SemaphoreType.DMA((2,)),
             pltpu.SemaphoreType.DMA((4,)),
-            pltpu.SemaphoreType.DMA((2, 4)),
         ],
         compiler_params=pltpu.CompilerParams(
             collective_id=ident, has_side_effects=True, vmem_limit_bytes=VMEM_LIMIT
         ),
         cost_estimate=pl.CostEstimate(
-            flops=24 * rows * model * units,
-            bytes_accessed=28 * rows * model + 6 * model * units + 24 * rows * units,
+            flops=8 * rows * model * units * len(weights),
+            bytes_accessed=14 * rows * model + 2 * len(weights) * model * units + 24 * rows * units,
             transcendentals=4 * rows * units,
         ),
-    )(
-        own_norm,
-        arrived_norm[1],
-        arrived_norm[0],
-        own_grad,
-        arrived_grad[1],
-        arrived_grad[0],
-        w_gate,
-        w_up,
-        w_down,
-    )
+    )(own, beside, across, *weights, *tiled)
 
 
 def mlp(norm, grad, w_gate, w_up, w_down):
@@ -1217,7 +1210,7 @@
     norm_one = [item[0] for item in norm_one]
 
     none = [None] * batches
-    self_probs, cross_probs = list(none), list(none)
+    self_probs, cross_probs, slope, value = (list(none) for _ in range(4))
     full_one, qkv, mixed_self, x_one, norm_two, scale_two = ([None] * batches for _ in range(6))
     full_two, query, mixed_cross, x_two, norm_three, scale_three = (
         [None] * batches for _ in range(6)
@@ -1248,9 +1241,14 @@
         x_two[b] = x_one[b] + scatter_end(arrived)
         norm_three[b], scale_three[b] = normalize(x_two[b], gain_mlp)
 
-    def mlp_block(b, arrived_norm, arrived_grad):
-        full_three[b], grad_three[b], hidden[b], d_gate[b], d_up[b] = gathered_mlp(
-            norm_three[b], arrived_norm, outer_low[b], arrived_grad, w_gate, w_up, w_down, 5
+    def mlp_up(b, arrived):
+        full_three[b], hidden[b], slope[b], value[b] = gathered_tiles(
+            norm_three[b], arrived, [w_gate, w_up], [], up_body, 3, 5
+        )
+
+    def mlp_down(b, arrived):
+        grad_three[b], d_gate[b], d_up[b] = gathered_tiles(
+            outer_low[b], arrived, [w_down], [slope[b], value[b]], down_body, 2, 12
         )
 
     def mlp_back(b):
@@ -1304,20 +1302,18 @@
         )
         got[1] = gather_start(norm_one[1])
         sent[0] = self_block(0, got[0])
-        sent[0], got[1], outer_low = fence(sent[0], got[1], outer_low)
-        grads[0] = gather_start(outer_low[0])
+        sent[0], got[1] = fence(sent[0], got[1])
+        back[0] = scatter_move(sent[0])
         sent[1] = self_block(1, got[1])
-        sent, grads[0], k_cross = fence(sent, grads[0], k_cross)
-        back[0] = scatter_move(sent[0])
-        keys = dot_nn(patches, k_cross).astype(bf16)
-        back[0], sent[1], keys, v_cross = fence(back[0], sent[1], keys, v_cross)
+        back[0], sent[1], k_cross = fence(back[0], sent[1], k_cross)
         back[1] = scatter_move(sent[1])
         self_norm(0, back[0])
-        values = dot_nn(patches, v_cross).astype(bf16)
-        norm_two[0], back[1], values = fence(norm_two[0], back[1], values)
+        keys = dot_nn(patches, k_cross).astype(bf16)
+        norm_two[0], back[1], keys, v_cross = fence(norm_two[0], back[1], keys, v_cross)
         got[0] = gather_start(norm_two[0])
         self_norm(1, back[1])
-        norm_two[1], got[0], outer_low = fence(norm_two[1], got[0], outer_low)
+        values = dot_nn(patches, v_cross).astype(bf16)
+        norm_two[1], got[0], values = fence(norm_two[1], got[0], values)
         got[1] = gather_start(norm_two[1])
         sent[0] = cross_block(0, got[0], keys, values)
         sent[0], got[1] = fence(sent[0], got[1])
@@ -1331,15 +1327,17 @@
         cross_norm(1, back[1])
         got[0], outer_low, norm_three[1] = fence(got[0], outer_low, norm_three[1])
         got[1] = gather_start(norm_three[1])
-        mlp_block(0, got[0], grads[0])
-        got[1], d_gate[0], d_up[0], outer_low[1] = fence(
-            got[1], d_gate[0], d_up[0], outer_low[1]
-        )
+        mlp_up(0, got[0])
+        got[1], slope[0], outer_low = fence(got[1], slope[0], outer_low)
+        grads[0] = gather_start(outer_low[0])
+        mlp_up(1, got[1])
+        grads[0], slope[1], outer_low[1] = fence(grads[0], slope[1], outer_low[1])
         grads[1] = gather_start(outer_low[1])
+        mlp_down(0, grads[0])
         sent[0] = mlp_back(0)
-        grads[1], got[1], sent[0] = fence(grads[1], got[1], sent[0])
+        grads[1], sent[0] = fence(grads[1], sent[0])
         back[0] = scatter_move(sent[0])
-        mlp_block(1, got[1], grads[1])
+        mlp_down(1, grads[1])
         down_other, down_mine = side_grads(hidden, grad_three)
         back[0], d_gate[1], d_up[1], down_other = fence(
             back[0], d_gate[1], d_up[1], down_other
@@ -1370,9 +1368,8 @@
         own[0] = cross_norm_back(0, back[0])
         o_other, o_mine = side_grads(mixed_cross, grad_two)
         q_other, q_mine = side_grads(full_two, d_query)
-        shown[0] = project_out(0)
-        own[0], back[1], d_kv, o_other, q_other, shown[0], gate_sent, down_mine = fence(
-            own[0], back[1], d_kv, o_other, q_other, shown[0], gate_sent, down_mine
+        own[0], back[1], d_kv, o_other, q_other, gate_sent, down_mine = fence(
+            own[0], back[1], d_kv, o_other, q_other, gate_sent, down_mine
         )
         got[0] = gather_start(own[0])
         own[1] = cross_norm_back(1, back[1])
@@ -1396,7 +1393,7 @@
         k_sent = flip(k_other, "dp", 1)
         back[1] = scatter_move(sent[1])
         self_norm_back(0, back[0])
-        shown[1] = project_out(1)
+        shown = [project_out(b) for b in each_batch]
         back[1], grad_input[0], shown, k_sent = fence(back[1], grad_input[0], shown, k_sent)
         self_norm_back(1, back[1])
         back = [scatter_move(shown[b]) for b in each_batch]
@@ -1413,7 +1410,9 @@
         values = dot_nn(patches, v_cross).astype(bf16)
         sent[0] = cross_block(0, gather_start(norm_two[0]), keys, values)
         cross_norm(0, scatter_move(sent[0]))
-        mlp_block(0, gather_start(norm_three[0]), gather_start(outer_low[0]))
+        full_three[0] = gather_start(norm_three[0])
+        grad_three[0] = gather_start(outer_low[0])
+        hidden[0], d_gate[0], d_up[0] = mlp(full_three[0], grad_three[0], w_gate, w_up, w_down)
         own[0] = mlp_norm_back(0, scatter_move(mlp_back(0)))
         sent[0], d_kv = cross_back(0, own[0], gather_start(own[0]), keys, values, ())
         own[0] = cross_norm_back(0, scatter_move(sent[0]))

time: 1200 us -> 1190 us (level)
  waiting for transfers between devices: 144 us -> 129 us
    ppermute x50, waiting for transfers between devices: 144 us -> 129 us  [flip(): return lax.ppermute(tensor, axis, [(i, i ^ bit) for i in range(count)])]
    pallas_call x2 -> x4, Pallas kernels: 57.2 us -> 70.6 us  [gathered_tiles(): pl.pallas_call(partial(gathered_tiles_kernel, units // tile, len(weights)...]
  transfers between devices with their start and end apart: 50 -> 50, of which waited for: 19 -> 20; matrix products, arithmetic and copies ran while one was open for 7% -> 7% of each run, Pallas kernels for 76% -> 77%
where the time goes in v5:
time: 1190 us; the launch traced here: 1180 us
  Pallas kernels  910 us (76%)
  waiting for transfers between devices  129 us (11%)
  other arithmetic  64.1 us (5%)
  starting transfers between devices  38.1 us (3%)
  matrix products  25.2 us (2%)
  local copies, waits for them, and re-layouts  12.4 us (1%)
    pallas_call x1, Pallas kernels, sum_chunks(): pl.pallas_call(partial(sum_kernel, cycles, len(paired), late), in_specs=[...  465 us
    ppermute x50, waiting for transfers between devices, flip(): return lax.ppermute(tensor, axis, [(i, i ^ bit) for i in range(count)])  129 us
    pallas_call x12, Pallas kernels, scattered_dot(): pl.pallas_call(partial(scattered_kernel, transposed, len(lefts), size), i...  104 us
    pallas_call x7, Pallas kernels, side_grads(): pl.pallas_call(partial(side_grads_kernel, steps, count), grid_spec=pltpu....  101 us
    pallas_call x4, Pallas kernels, gathered_tiles(): pl.pallas_call(partial(gathered_tiles_kernel, units // tile, len(weights)...  70.6 us
    pallas_call x8, Pallas kernels, gathered_dot(): pl.pallas_call(partial(gathered_kernel, transposed, 512), in_specs=[IN_VM...  39.9 us
    pallas_call x4, Pallas kernels, unpack(): pl.pallas_call(partial(unpack_kernel, pieces), grid=(2, steps), in_specs=...  39.5 us
    ppermute x50, starting transfers between devices, flip(): return lax.ppermute(tensor, axis, [(i, i ^ bit) for i in range(count)])  38.1 us
  transfers between devices with their start and end apart: 50, of which 20 were waited for; matrix products, arithmetic and copies ran while one was open for 7% of the time, Pallas kernels for 77%

profile of v5, /device:TPU:0, one launch (start us, length us, event | category | flops | bytes accessed | tf_op | source)
XLA Modules:
  0.0 1180.8 jit_solution(1565162997893948517)
XLA Ops:
  89.2 12.6 %fusion.key_ref = bf16[4096,512]{1,0:T(8,128)(2,1)S(1)} fusion(bf16[4096,2048]{1,0:T(8,128)(2,1)} %refs_0_.3, bf16[2048,512]{1,0:T(8,128)(2,1)S(1)} %copy-done.82), kind=kOutput, calls=%fused_computation.7 | convolution fusion | flops 8592031744 | bytes 23068672 | tf_op jit(solution)/shard_map/dot_general | solution.py:21
  113.0 12.7 %fusion.1.value_ref = bf16[4096,512]{1,0:T(8,128)(2,1)S(1)} fusion(bf16[4096,2048]{1,0:T(8,128)(2,1)} %refs_0_.3, bf16[2048,512]{1,0:T(8,128)(2,1)S(1)} %copy-done.83), kind=kOutput, calls=%fused_computation.8 | convolution fusion | flops 8592031744 | bytes 23068672 | tf_op jit(solution)/shard_map/dot_general | solution.py:21
  127.2 10.9 collective-permute-done.9.across
  189.8 22.5 %collective-permute-done.14 = bf16[256,2048]{1,0:T(8,128)(2,1)S(1)} collective-permute-done((bf16[256,2048]{1,0:T(8,128)(2,1)S(1)}, bf16[256,2048]{1,0:T(8,128)(2,1)S(1)}, u32[]{:S(2)}, u32[]{:S(2)}) %collective-permute-start.14) | collective-permute-done | bytes 1048608 | tf_op jit(solution)/shard_map/ppermute | solution.py:573
  215.0 22.9 %collective-permute-done.15.refs_2_ = bf16[256,2048]{1,0:T(8,128)(2,1)S(1)} collective-permute-done((bf16[256,2048]{1,0:T(8,128)(2,1)S(1)}, bf16[256,2048]{1,0:T(8,128)(2,1)S(1)}, u32[]{:S(2)}, u32[]{:S(2)}) %collective-permute-start.15) | collective-permute-done | bytes 1048608 | tf_op jit(solution)/shard_map/ppermute | solution.py:573
  238.9 19.5 %shard_map.336 = (bf16[1024,2048]{1,0:T(8,128)(2,1)}, bf16[1024,1280]{1,0:T(8,128)(2,1)}, bf16[1024,1280]{1,0:T(8,128)(2,1)}, bf16[1024,1280]{1,0:T(8,128)(2,1)}) custom-call(bf16[256,2048]{1,0:T(8,128)(2,1)} %copy-done.63, bf16[256,2048]{1,0:T(8,128)(2,1)} %copy-done.90, bf16[256,2048]{1,0:T(8,128)(2,1)} %copy-done.92, bf16[2048,1280]{1,0:T(8,128)(2,1)} %refs_2_.3, ...), custom_call_target="tpu_custom_call" | custom-call | flops 10737418240 | bytes 25690112 | tf_op jit(solution)/shard_map/pallas_call | solution.py:525
  265.0 19.7 %shard_map.337 = (bf16[1024,2048]{1,0:T(8,128)(2,1)}, bf16[1024,1280]{1,0:T(8,128)(2,1)}, bf16[1024,1280]{1,0:T(8,128)(2,1)}, bf16[1024,1280]{1,0:T(8,128)(2,1)}) custom-call(bf16[256,2048]{1,0:T(8,128)(2,1)} %copy-done.62, bf16[256,2048]{1,0:T(8,128)(2,1)} %copy-done.88, bf16[256,2048]{1,0:T(8,128)(2,1)} %copy-done.89, bf16[2048,1280]{1,0:T(8,128)(2,1)} %refs_2_.3, ...), custom_call_target="tpu_custom_call" | custom-call | flops 10737418240 | bytes 25690112 | tf_op jit(solution)/shard_map/pallas_call | solution.py:525
  290.9 15.7 %shard_map.338 = (bf16[1024,2048]{1,0:T(8,128)(2,1)}, bf16[1024,1280]{1,0:T(8,128)(2,1)}, bf16[1024,1280]{1,0:T(8,128)(2,1)}) custom-call(bf16[256,2048]{1,0:T(8,128)(2,1)} %get-tuple-element.344.refs_0_, bf16[256,2048]{1,0:T(8,128)(2,1)} %collective-permute-done.20.refs_1_, bf16[256,2048]{1,0:T(8,128)(2,1)} %collective-permute-done.19.refs_2_, ...), custom_call_target="tpu_custom_call" | custom-call | flops 5368709120 | bytes 20447232 | tf_op jit(solution)/shard_map/pallas_call | solution.py:525
  308.3 17.9 %shard_map.339 = (f32[256,2048]{1,0:T(8,128)S(1)}, bf16[256,2048]{1,0:T(8,128)(2,1)S(1)}) custom-call(bf16[1024,1280]{1,0:T(8,128)(2,1)S(1)} %copy-done.36, bf16[1024,1280]{1,0:T(8,128)(2,1)} %get-tuple-element.386.refs_1_.refs_2_, bf16[2048,1280]{1,0:T(8,128)(2,1)} %refs_2_.3, bf16[2048,1280]{1,0:T(8,128)(2,1)} %refs_3_.11), custom_call_target="tpu_custom_call" | custom-call | flops 10737418240 | bytes 33554432 | tf_op jit(solution)/shard_map/pallas_call | solution.py:401
  328.7 15.7 %shard_map.340 = (bf16[1024,2048]{1,0:T(8,128)(2,1)}, bf16[1024,1280]{1,0:T(8,128)(2,1)}, bf16[1024,1280]{1,0:T(8,128)(2,1)}) custom-call(bf16[256,2048]{1,0:T(8,128)(2,1)} %get-tuple-element.349.refs_0_, bf16[256,2048]{1,0:T(8,128)(2,1)} %copy-done.91, bf16[256,2048]{1,0:T(8,128)(2,1)} %collective-permute-done.21.refs_2_, bf16[1280,2048]{1,0:T(8,128)(2,1)} %refs_1_.15, ...), custom_call_target="tpu_custom_call" | custom-call | flops 5368709120 | bytes 20447232 | tf_op jit(solution)/shard_map/pallas_call | solution.py:525
  344.4 18.6 %shard_map.341 = (bf16[8,640,256]{2,1,0:T(8,128)(2,1)}, bf16[8,640,256]{2,1,0:T(8,128)(2,1)}) custom-call(s32[1]{0:T(128)} %bitcast.9.y_ref, bf16[1024,1280]{1,0:T(8,128)(2,1)} %get-tuple-element.482.refs_0_, bf16[1024,1280]{1,0:T(8,128)(2,1)} %get-tuple-element.485.refs_1_.refs_0_, bf16[1024,2048]{1,0:T(8,128)(2,1)} %get-tuple-element.368.refs_2_, ...), custom_call_target="tpu_custom_call" | custom-call | flops 10737418240 | bytes 18874368 | tf_op jit(solution)/shard_map/pallas_call | solution.py:1065
  369.0 18.7 %shard_map.342 = (f32[256,2048]{1,0:T(8,128)S(1)}, bf16[256,2048]{1,0:T(8,128)(2,1)}) custom-call(bf16[1024,1280]{1,0:T(8,128)(2,1)S(1)} %copy-done.37, bf16[1024,1280]{1,0:T(8,128)(2,1)} %get-tuple-element.387.refs_1_.refs_3_, bf16[2048,1280]{1,0:T(8,128)(2,1)} %refs_2_.3, bf16[2048,1280]{1,0:T(8,128)(2,1)} %refs_3_.11), custom_call_target="tpu_custom_call" | custom-call | flops 10737418240 | bytes 33554432 | tf_op jit(solution)/shard_map/pallas_call | solution.py:401
  394.0 17.1 %shard_map.343 = (bf16[5,1024,256]{2,1,0:T(8,128)(2,1)}, bf16[5,1024,256]{2,1,0:T(8,128)(2,1)}) custom-call(s32[1]{0:T(128)} %bitcast.9.y_ref, bf16[1024,2048]{1,0:T(8,128)(2,1)} %get-tuple-element.381.refs_0_, bf16[1024,2048]{1,0:T(8,128)(2,1)} %get-tuple-element.382.refs_1_, bf16[1024,1280]{1,0:T(8,128)(2,1)} %get-tuple-element.383.refs_0_.refs_2_, ...), custom_call_target="tpu_custom_call" | custom-call | flops 10737418240 | bytes 18874368 | tf_op jit(solution)/shard_map/pallas_call | solution.py:1065
  411.1 17.4 %shard_map.344 = (bf16[5,1024,256]{2,1,0:T(8,128)(2,1)}, bf16[5,1024,256]{2,1,0:T(8,128)(2,1)}) custom-call(s32[1]{0:T(128)} %bitcast.9.y_ref, bf16[1024,2048]{1,0:T(8,128)(2,1)} %get-tuple-element.381.refs_0_, bf16[1024,2048]{1,0:T(8,128)(2,1)} %get-tuple-element.382.refs_1_, bf16[1024,1280]{1,0:T(8,128)(2,1)} %get-tuple-element.386.refs_1_.refs_2_, ...), custom_call_target="tpu_custom_call" | custom-call | flops 10737418240 | bytes 18874368 | tf_op jit(solution)/shard_map/pallas_call | solution.py:1065
  440.4 14.9 %shard_map.346 = (bf16[1024,512]{1,0:T(8,128)(2,1)S(1)}, bf16[4096,512]{1,0:T(8,128)(2,1)}, bf16[4096,512]{1,0:T(8,128)(2,1)}) custom-call(s32[8]{0:T(128)S(1)} %add.273.which_ref, bf16[1024,512]{1,0:T(8,128)(2,1)S(1)} %get-tuple-element.309.query_ref, bf16[4096,512]{1,0:T(8,128)(2,1)S(1)} %copy-done.3, bf16[4096,512]{1,0:T(8,128)(2,1)S(1)} %copy-done.5, ...), custom_call_target="tpu_custom_call" | custom-call | flops 2147483648 | bytes 16777216 | tf_op jit(solution)/shard_map/pallas_call | solution.py:243
  467.9 14.9 %shard_map.349 = (bf16[1024,512]{1,0:T(8,128)(2,1)S(1)}, bf16[4096,512]{1,0:T(8,128)(2,1)}, bf16[4096,512]{1,0:T(8,128)(2,1)}) custom-call(s32[8]{0:T(128)S(1)} %add.278.which_ref, bf16[1024,512]{1,0:T(8,128)(2,1)S(1)} %get-tuple-element.317.query_ref, bf16[4096,512]{1,0:T(8,128)(2,1)S(1)} %copy-done.3, ...), custom_call_target="tpu_custom_call", output_to_operand_aliasing={{1}: (6, {}), {2}: (7, {})} | custom-call | flops 2147483648 | bytes 16777216 | tf_op jit(solution)/shard_map/pallas_call | solution.py:243
  524.0 14.3 %shard_map.353 = (bf16[2,1024,256]{2,1,0:T(8,128)(2,1)}, bf16[2,1024,256]{2,1,0:T(8,128)(2,1)}) custom-call(s32[1]{0:T(128)} %bitcast.9.y_ref, bf16[4096,2048]{1,0:T(8,128)(2,1)} %refs_0_.3, bf16[4096,512]{1,0:T(8,128)(2,1)} %get-tuple-element.435.refs_1_), custom_call_target="tpu_custom_call" | custom-call | flops 8589934592 | bytes 23068672 | tf_op jit(solution)/shard_map/pallas_call | solution.py:1065
  543.1 14.4 %shard_map.354 = (bf16[2,1024,256]{2,1,0:T(8,128)(2,1)}, bf16[2,1024,256]{2,1,0:T(8,128)(2,1)}) custom-call(s32[1]{0:T(128)} %bitcast.9.y_ref, bf16[4096,2048]{1,0:T(8,128)(2,1)} %refs_0_.3, bf16[4096,512]{1,0:T(8,128)(2,1)} %get-tuple-element.437.refs_1_), custom_call_target="tpu_custom_call" | custom-call | flops 8589934592 | bytes 23068672 | tf_op jit(solution)/shard_map/pallas_call | solution.py:1065
  563.1 11.3 shard_map.356.refs_0_.refs_2_
  583.6 16.1 %collective-permute-done.38 = bf16[8,256,256]{2,1,0:T(8,128)(2,1)} collective-permute-done((bf16[8,256,256]{2,1,0:T(8,128)(2,1)}, bf16[8,256,256]{2,1,0:T(8,128)(2,1)}, u32[]{:S(2)}, u32[]{:S(2)}) %collective-permute-start.38) | collective-permute-done | bytes 1048608 | tf_op jit(solution)/shard_map/ppermute | solution.py:573
  604.7 11.2 shard_map.359.refs_0_.refs_3_
  655.9 465.1 %shard_map.363 = (bf16[16384,256]{1,0:T(8,128)(2,1)}, bf16[2,23552,256]{2,1,0:T(8,128)(2,1)}, bf16[2048,256]{1,0:T(8,128)(2,1)}) custom-call(bf16[1024,2048]{1,0:T(8,128)(2,1)} %get-tuple-element.325.refs_0_, bf16[1024,2048]{1,0:T(8,128)(2,1)} %get-tuple-element.326.refs_1_, bf16[1024,1536]{1,0:T(8,128)(2,1)} %copy-done.14, bf16[1024,1536]{1,0:T(8,128)(2,1)} %copy-done.15, ...), custom_call_target="tpu_custom_call" | custom-call | flops 17179869184 | bytes 130023424 | tf_op jit(solution)/shard_map/pallas_call | solution.py:1001
  1140.2 12.3 %shard_map.365 = (f32[2048,1280]{1,0:T(8,128)}, f32[2048,1280]{1,0:T(8,128)}) custom-call(bf16[2,23552,256]{2,1,0:T(8,128)(2,1)} %get-tuple-element.506.refs_0_.refs_1_.refs_2_.refs_3_.refs_4_.refs_5_.refs_6_.refs_7_.refs_8_.refs_9_, bf16[2,23552,256]{2,1,0:T(8,128)(2,1)} %get-tuple-element.506.refs_0_.refs_1_.refs_2_.refs_3_.refs_4_.refs_5_.refs_6_.refs_7_.refs_8_.refs_9_, ...), custom_call_target="tpu_custom_call" | custom-call | flops 5242880 | bytes 31457280 | tf_op jit(solution)/shard_map/pallas_call | solution.py:1116
  1156.0 14.0 %shard_map.366 = (f32[2048,512]{1,0:T(8,128)}, f32[2048,512]{1,0:T(8,128)}, f32[2048,512]{1,0:T(8,128)}, f32[2048,512]{1,0:T(8,128)}, f32[2048,512]{1,0:T(8,128)}, /*index=5*/f32[2048,512]{1,0:T(8,128)}) custom-call(bf16[2,23552,256]{2,1,0:T(8,128)(2,1)} %get-tuple-element.506.refs_0_.refs_1_.refs_2_.refs_3_.refs_4_.refs_5_.refs_6_.refs_7_.refs_8_.refs_9_, ...), custom_call_target="tpu_custom_call" | custom-call | flops 6291456 | bytes 37748736 | tf_op jit(solution)/shard_map/pallas_call | solution.py:1116
  (396 shorter events, 347.9 us)
Async XLA Ops:
  4.1 34.2 %collective-permute-start.1 = (bf16[256,2048]{1,0:T(8,128)(2,1)S(1)}, bf16[256,2048]{1,0:T(8,128)(2,1)S(1)}, u32[]{:S(2)}, u32[]{:S(2)}) collective-permute-start(bf16[256,2048]{1,0:T(8,128)(2,1)S(1)} %get-tuple-element.566.own), channel_id=1, source_target_pairs={{0,1},{1,0},{2,3},{3,2},{4,5},{5,4},{6,7},{7,6},{8,9},{9,8},{10,11... | collective-permute-start | bytes 3145736 | tf_op jit(solution)/shard_map/ppermute | solution.py:573
  4.6 33.7 %collective-permute-start = (bf16[256,2048]{1,0:T(8,128)(2,1)S(1)}, bf16[256,2048]{1,0:T(8,128)(2,1)}, u32[]{:S(2)}, u32[]{:S(2)}) collective-permute-start(bf16[256,2048]{1,0:T(8,128)(2,1)S(1)} %get-tuple-element.566.own), channel_id=1, source_target_pairs={{0,2},{1,3},{2,0},{3,1},{4,6},{5,7},{6,4},{7,5},{8,10},{9,11},{10,... | collective-permute-start | bytes 3145736 | tf_op jit(solution)/shard_map/ppermute | solution.py:573
  38.4 25.6 %collective-permute-start.5 = (bf16[256,2048]{1,0:T(8,128)(2,1)S(1)}, bf16[256,2048]{1,0:T(8,128)(2,1)S(1)}, u32[]{:S(2)}, u32[]{:S(2)}) collective-permute-start(bf16[256,2048]{1,0:T(8,128)(2,1)S(1)} %get-tuple-element.284.own), channel_id=1, source_target_pairs={{0,2},{1,3},{2,0},{3,1},{4,6},{5,7},{6,4},{7,5},{8,10},{9,11},{10,... | collective-permute-start | bytes 3145736 | tf_op jit(solution)/shard_map/ppermute | solution.py:573
  112.5 25.6 %collective-permute-start.9 = (bf16[256,2048]{1,0:T(8,128)(2,1)S(1)}, bf16[256,2048]{1,0:T(8,128)(2,1)S(1)}, u32[]{:S(2)}, u32[]{:S(2)}) collective-permute-start(bf16[256,2048]{1,0:T(8,128)(2,1)S(1)} %multiply_convert_fusion.3.own), channel_id=1, source_target_pairs={{0,2},{1,3},{2,0},{3,1},{4,6},{5,7},{6,4},{7,5},{8,10},{9,11},{10,... | collective-permute-start | bytes 3145736 | tf_op jit(solution)/shard_map/ppermute | solution.py:573
  138.1 25.6 %collective-permute-start.11 = (bf16[256,2048]{1,0:T(8,128)(2,1)S(1)}, bf16[256,2048]{1,0:T(8,128)(2,1)S(1)}, u32[]{:S(2)}, u32[]{:S(2)}) collective-permute-start(bf16[256,2048]{1,0:T(8,128)(2,1)S(1)} %multiply_convert_fusion.2.own), channel_id=1, source_target_pairs={{0,2},{1,3},{2,0},{3,1},{4,6},{5,7},{6,4},{7,5},{8,10},{9,11},{10,... | collective-permute-start | bytes 3145736 | tf_op jit(solution)/shard_map/ppermute | solution.py:573
  212.4 25.6 %collective-permute-start.15 = (bf16[256,2048]{1,0:T(8,128)(2,1)S(1)}, bf16[256,2048]{1,0:T(8,128)(2,1)S(1)}, u32[]{:S(2)}, u32[]{:S(2)}) collective-permute-start(bf16[256,2048]{1,0:T(8,128)(2,1)S(1)} %multiply_convert_fusion.1.refs_0_), channel_id=1, source_target_pairs={{0,2},{1,3},{2,0},{3,1},{4,6},{5,7},{6,4},{7,5},{8,10},{9,11},{10,... | collective-permute-start | bytes 3145736 | tf_op jit(solution)/shard_map/ppermute | solution.py:573
  237.9 25.6 %collective-permute-start.17 = (bf16[256,2048]{1,0:T(8,128)(2,1)S(1)}, bf16[256,2048]{1,0:T(8,128)(2,1)S(1)}, u32[]{:S(2)}, u32[]{:S(2)}) collective-permute-start(bf16[256,2048]{1,0:T(8,128)(2,1)S(1)} %multiply_convert_fusion.refs_0_), channel_id=1, source_target_pairs={{0,2},{1,3},{2,0},{3,1},{4,6},{5,7},{6,4},{7,5},{8,10},{9,11},{10,... | collective-permute-start | bytes 3145736 | tf_op jit(solution)/shard_map/ppermute | solution.py:573
  264.5 25.9 %collective-permute-start.19 = (bf16[256,2048]{1,0:T(8,128)(2,1)}, bf16[256,2048]{1,0:T(8,128)(2,1)}, u32[]{:S(2)}, u32[]{:S(2)}) collective-permute-start(bf16[256,2048]{1,0:T(8,128)(2,1)} %get-tuple-element.344.refs_0_), channel_id=1, source_target_pairs={{0,2},{1,3},{2,0},{3,1},{4,6},{5,7},{6,4},{7,5},{8,10},{9,11},{10,... | collective-permute-start | bytes 3145736 | tf_op jit(solution)/shard_map/ppermute | solution.py:573
  290.4 35.9 %collective-permute-start.22 = (bf16[256,2048]{1,0:T(8,128)(2,1)S(1)}, bf16[256,2048]{1,0:T(8,128)(2,1)S(1)}, u32[]{:S(2)}, u32[]{:S(2)}) collective-permute-start(bf16[256,2048]{1,0:T(8,128)(2,1)S(1)} %copy-done.61), channel_id=1, source_target_pairs={{0,1},{1,0},{2,3},{3,2},{4,5},{5,4},{6,7},{7,6},{8,9},{9,8},{10,11... | collective-permute-start | bytes 3145736 | tf_op jit(solution)/shard_map/ppermute | solution.py:573
  290.4 35.9 %collective-permute-start.21 = (bf16[256,2048]{1,0:T(8,128)(2,1)S(1)}, bf16[256,2048]{1,0:T(8,128)(2,1)}, u32[]{:S(2)}, u32[]{:S(2)}) collective-permute-start(bf16[256,2048]{1,0:T(8,128)(2,1)S(1)} %copy-done.61), channel_id=1, source_target_pairs={{0,2},{1,3},{2,0},{3,1},{4,6},{5,7},{6,4},{7,5},{8,10},{9,11},{10,... | collective-permute-start | bytes 3145736 | tf_op jit(solution)/shard_map/ppermute | solution.py:573
  327.2 35.8 %collective-permute-start.23 = (bf16[256,2048]{1,0:T(8,128)(2,1)S(1)}, bf16[256,2048]{1,0:T(8,128)(2,1)S(1)}, u32[]{:S(2)}, u32[]{:S(2)}) collective-permute-start(bf16[256,2048]{1,0:T(8,128)(2,1)S(1)} %get-tuple-element.359), channel_id=1, source_target_pairs={{0,2},{1,3},{2,0},{3,1},{4,6},{5,7},{6,4},{7,5},{8,10},{9,11},{10,... | collective-permute-start | bytes 3145736 | tf_op jit(solution)/shard_map/ppermute | solution.py:573
  368.6 91.9 %collective-permute-start.29 = (bf16[8,640,256]{2,1,0:T(8,128)(2,1)}, bf16[8,640,256]{2,1,0:T(8,128)(2,1)}, u32[]{:S(2)}, u32[]{:S(2)}) collective-permute-start(bf16[8,640,256]{2,1,0:T(8,128)(2,1)} %get-tuple-element.401), channel_id=1, source_target_pairs={{0,4},{4,0},{8,12},{12,8},{16,20},{20,16},{24,28},{28,24},{1,5},{5... | collective-permute-start | bytes 7864328 | tf_op jit(solution)/shard_map/ppermute | solution.py:573
  393.5 35.0 %collective-permute-start.26 = (bf16[256,2048]{1,0:T(8,128)(2,1)}, bf16[256,2048]{1,0:T(8,128)(2,1)}, u32[]{:S(2)}, u32[]{:S(2)}) collective-permute-start(bf16[256,2048]{1,0:T(8,128)(2,1)} %get-tuple-element.380), channel_id=1, source_target_pairs={{0,2},{1,3},{2,0},{3,1},{4,6},{5,7},{6,4},{7,5},{8,10},{9,11},{10,... | collective-permute-start | bytes 3145736 | tf_op jit(solution)/shard_map/ppermute | solution.py:573
  435.2 25.6 %collective-permute-start.27 = (bf16[256,2048]{1,0:T(8,128)(2,1)S(1)}, bf16[256,2048]{1,0:T(8,128)(2,1)S(1)}, u32[]{:S(2)}, u32[]{:S(2)}) collective-permute-start(bf16[256,2048]{1,0:T(8,128)(2,1)S(1)} %get-tuple-element.403.own), channel_id=1, source_target_pairs={{0,2},{1,3},{2,0},{3,1},{4,6},{5,7},{6,4},{7,5},{8,10},{9,11},{10,... | collective-permute-start | bytes 3145736 | tf_op jit(solution)/shard_map/ppermute | solution.py:573
  460.7 36.4 %collective-permute-start.30 = (bf16[256,2048]{1,0:T(8,128)(2,1)S(1)}, bf16[256,2048]{1,0:T(8,128)(2,1)}, u32[]{:S(2)}, u32[]{:S(2)}) collective-permute-start(bf16[256,2048]{1,0:T(8,128)(2,1)S(1)} %get-tuple-element.413), channel_id=1, source_target_pairs={{0,2},{1,3},{2,0},{3,1},{4,6},{5,7},{6,4},{7,5},{8,10},{9,11},{10,... | collective-permute-start | bytes 3145736 | tf_op jit(solution)/shard_map/ppermute | solution.py:573
  462.2 60.1 %collective-permute-start.32 = (bf16[5,1024,256]{2,1,0:T(8,128)(2,1)}, bf16[5,1024,256]{2,1,0:T(8,128)(2,1)}, u32[]{:S(2)}, u32[]{:S(2)}) collective-permute-start(bf16[5,1024,256]{2,1,0:T(8,128)(2,1)} %get-tuple-element.430), channel_id=1, source_target_pairs={{0,4},{4,0},{8,12},{12,8},{16,20},{20,16},{24,28},{28,24},{1,5},{5... | collective-permute-start | bytes 7864328 | tf_op jit(solution)/shard_map/ppermute | solution.py:573
  462.7 120.9 %collective-permute-start.37 = (bf16[5,1024,256]{2,1,0:T(8,128)(2,1)}, bf16[5,1024,256]{2,1,0:T(8,128)(2,1)}, u32[]{:S(2)}, u32[]{:S(2)}) collective-permute-start(bf16[5,1024,256]{2,1,0:T(8,128)(2,1)} %get-tuple-element.449), channel_id=1, source_target_pairs={{0,4},{4,0},{8,12},{12,8},{16,20},{20,16},{24,28},{28,24},{1,5},{5... | collective-permute-start | bytes 7864328 | tf_op jit(solution)/shard_map/ppermute | solution.py:573
  523.4 34.2 %collective-permute-start.34 = (bf16[256,2048]{1,0:T(8,128)(2,1)S(1)}, bf16[256,2048]{1,0:T(8,128)(2,1)S(1)}, u32[]{:S(2)}, u32[]{:S(2)}) collective-permute-start(bf16[256,2048]{1,0:T(8,128)(2,1)S(1)} %get-tuple-element.432.own), channel_id=1, source_target_pairs={{0,1},{1,0},{2,3},{3,2},{4,5},{5,4},{6,7},{7,6},{8,9},{9,8},{10,11... | collective-permute-start | bytes 3145736 | tf_op jit(solution)/shard_map/ppermute | solution.py:573
  523.4 34.2 %collective-permute-start.33 = (bf16[256,2048]{1,0:T(8,128)(2,1)S(1)}, bf16[256,2048]{1,0:T(8,128)(2,1)S(1)}, u32[]{:S(2)}, u32[]{:S(2)}) collective-permute-start(bf16[256,2048]{1,0:T(8,128)(2,1)S(1)} %get-tuple-element.432.own), channel_id=1, source_target_pairs={{0,2},{1,3},{2,0},{3,1},{4,6},{5,7},{6,4},{7,5},{8,10},{9,11},{10,... | collective-permute-start | bytes 3145736 | tf_op jit(solution)/shard_map/ppermute | solution.py:573
  540.4 59.3 %collective-permute-start.38 = (bf16[8,256,256]{2,1,0:T(8,128)(2,1)}, bf16[8,256,256]{2,1,0:T(8,128)(2,1)}, u32[]{:S(2)}, u32[]{:S(2)}) collective-permute-start(bf16[8,256,256]{2,1,0:T(8,128)(2,1)} %get-tuple-element.450), channel_id=1, source_target_pairs={{0,4},{4,0},{8,12},{12,8},{16,20},{20,16},{24,28},{28,24},{1,5},{5... | collective-permute-start | bytes 3145736 | tf_op jit(solution)/shard_map/ppermute | solution.py:573
  557.6 42.1 %collective-permute-start.36 = (bf16[256,2048]{1,0:T(8,128)(2,1)S(1)}, bf16[256,2048]{1,0:T(8,128)(2,1)S(1)}, u32[]{:S(2)}, u32[]{:S(2)}) collective-permute-start(bf16[256,2048]{1,0:T(8,128)(2,1)S(1)} %get-tuple-element.446.own), channel_id=1, source_target_pairs={{0,1},{1,0},{2,3},{3,2},{4,5},{5,4},{6,7},{7,6},{8,9},{9,8},{10,11... | collective-permute-start | bytes 3145736 | tf_op jit(solution)/shard_map/ppermute | solution.py:573
  557.9 41.9 %collective-permute-start.35 = (bf16[256,2048]{1,0:T(8,128)(2,1)S(1)}, bf16[256,2048]{1,0:T(8,128)(2,1)S(1)}, u32[]{:S(2)}, u32[]{:S(2)}) collective-permute-start(bf16[256,2048]{1,0:T(8,128)(2,1)S(1)} %get-tuple-element.446.own), channel_id=1, source_target_pairs={{0,2},{1,3},{2,0},{3,1},{4,6},{5,7},{6,4},{7,5},{8,10},{9,11},{10,... | collective-permute-start | bytes 3145736 | tf_op jit(solution)/shard_map/ppermute | solution.py:573
  653.9 467.1 %collective-permute-start.43 = (bf16[256,2048]{1,0:T(8,128)(2,1)}, bf16[256,2048]{1,0:T(8,128)(2,1)}, u32[]{:S(2)}, u32[]{:S(2)}) collective-permute-start(bf16[256,2048]{1,0:T(8,128)(2,1)} %get-tuple-element.495), channel_id=1, source_target_pairs={{0,2},{1,3},{2,0},{3,1},{4,6},{5,7},{6,4},{7,5},{8,10},{9,11},{10,... | collective-permute-start | bytes 3145736 | tf_op jit(solution)/shard_map/ppermute | solution.py:573
  654.9 466.1 %collective-permute-start.44 = (bf16[256,2048]{1,0:T(8,128)(2,1)}, bf16[256,2048]{1,0:T(8,128)(2,1)}, u32[]{:S(2)}, u32[]{:S(2)}) collective-permute-start(bf16[256,2048]{1,0:T(8,128)(2,1)} %get-tuple-element.497), channel_id=1, source_target_pairs={{0,2},{1,3},{2,0},{3,1},{4,6},{5,7},{6,4},{7,5},{8,10},{9,11},{10,... | collective-permute-start | bytes 3145736 | tf_op jit(solution)/shard_map/ppermute | solution.py:573
  (123 other events, 2033.7 us)
